TPU v7x, 32 devices: a whole 2x2x4 slice. The times are simulated.
32 devices in a mesh: blk: 16 (over z, y, x), head: 2 (over core).
Axes of the slice: x: 2, y: 2, z: 4, core: 2. Of those that a mesh axis runs over, the one named last changes fastest.
Arguments:
- tokens: bfloat16 [512, 1024], P('blk'), may hold values from -6 to 6
- norm_gain: float32 [1024], replicated, may hold values from 0.25 to 1.75
- w_query: bfloat16 [1024, 1024], P(None, 'head')
- w_key: bfloat16 [1024, 1024], P(None, 'head'), may hold values from -0.1875 to 0.1875
- w_value: bfloat16 [1024, 1024], P(None, 'head'), may hold values from -0.1875 to 0.1875
- w_out: bfloat16 [1024, 1024], P('head'), may hold values from -0.1875 to 0.1875
- ffn_gain: float32 [1024], replicated, may hold values from 0.25 to 1.75
- w_gate: bfloat16 [1024, 4096], P(None, 'head'), may hold values from -0.1875 to 0.1875
- w_up: bfloat16 [1024, 4096], P(None, 'head'), may hold values from -0.1875 to 0.1875
- w_down: bfloat16 [4096, 1024], P('head'), may hold values from -0.09375 to 0.09375
- keys: bfloat16 [16384, 1024], P('blk', 'head'), may hold values from -6 to 6
- values: bfloat16 [16384, 1024], P('blk', 'head'), may hold values from -6 to 6
- key_variate: int32 [16384], P('blk'), may hold values from 0 to 3
- query_variate: int32 [512], replicated, may hold values from 0 to 3
- bias: float32 [2, 16], P(None, 'head'), may hold values from -2 to 2
- lengths: int32 [512], replicated, may hold values from 17 to 4096, as said below
- order: int32 [512], replicated, may hold values from 0 to 511, as said below
- live_blocks: int32 [256], P('blk'), may hold values from 0 to 1
Outputs:
- layer_out: bfloat16 [512, 1024], P('blk', 'head')
Inputs may be any that keep to these rules, and one draw needn't show every extreme that they name: lengths sum to 16384; the smallest is exactly 17 and the largest exactly 4096. Each request appears once; order[j] // 32 depends only on j % 16.
All inputs are finite; a program needn't handle non-finite values.
Results may differ from a plain program's by a relative error of at most 0.025.
Values may be sent and summed in bfloat16 or wider, within the bound.
No kernel may reach another device: no remote copies, remote signals or barrier semaphores. Data moves between devices by JAX's collectives and lax.ppermute only.
A program may use at most 64 MiB of HBM per device.

v0:
```python
import jax
import jax.numpy as jnp
from jax import lax
from jax.sharding import PartitionSpec as P


def normalize(inputs, gain):
    mean_square = jnp.mean(inputs * inputs, axis=-1, keepdims=True)
    return inputs * lax.rsqrt(mean_square + 1e-05) * gain


def pool_owner(first, count, ends, order):
    position = first + jnp.arange(count, dtype=jnp.int32)
    rank = jnp.searchsorted(ends, position, side="right")
    return order[rank]


def key_scores(query_rows, key_rows, same, bias, head_dim):
    count = key_rows.shape[0]
    product = query_rows.astype(jnp.float32) * key_rows.astype(jnp.float32)
    raw = jnp.sum(product.reshape(count, -1, head_dim), axis=2) / jnp.sqrt(jnp.float32(head_dim))
    return raw + jnp.where(same[:, None], bias[0][None, :], bias[1][None, :])


def weighted_rows(weight, value_rows, head_dim):
    count = value_rows.shape[0]
    value_heads = value_rows.astype(jnp.float32).reshape(count, -1, head_dim)
    return (weight[:, :, None] * value_heads).reshape(count, -1)


def body(
    tokens,
    norm_gain,
    w_query,
    w_key,
    w_value,
    w_out,
    ffn_gain,
    w_gate,
    w_up,
    w_down,
    keys,
    values,
    key_variate,
    query_variate,
    bias,
    lengths,
    order,
    live_blocks,
):
    req_dev = tokens.shape[0]
    d_model = tokens.shape[1]
    heads_local = bias.shape[1]
    head_dim = w_query.shape[1] // heads_local
    pool_dev = keys.shape[0]
    block_len = pool_dev // live_blocks.shape[0]
    total_req = lengths.shape[0]
    here = lax.axis_index("blk")
    head_index = lax.axis_index("head")
    width_local = d_model // lax.axis_size("head")
    inputs = tokens.astype(jnp.float32)
    normed = normalize(inputs, norm_gain).astype(jnp.bfloat16)
    query = jnp.dot(normed, w_query, preferred_element_type=jnp.float32).astype(jnp.bfloat16)
    key_new = jnp.dot(normed, w_key, preferred_element_type=jnp.float32).astype(jnp.bfloat16)
    value_new = jnp.dot(normed, w_value, preferred_element_type=jnp.float32).astype(jnp.bfloat16)
    ends = jnp.cumsum(lengths[order])
    floor_value = jnp.float32(-1e30)
    live = jnp.repeat(live_blocks, block_len) > 0
    all_query = lax.all_gather(query, "blk", axis=0, tiled=True)
    owner = pool_owner(here * pool_dev, pool_dev, ends, order)
    same = key_variate == query_variate[owner]
    score = key_scores(all_query[owner], keys, same, bias, head_dim)
    masked = jnp.where(live[:, None], score, floor_value)
    local_top = jnp.full((total_req, heads_local), -1e30, jnp.float32).at[owner].max(masked)
    global_top = lax.pmax(local_top, "blk")
    weight = jnp.where(live[:, None], jnp.exp(masked - global_top[owner]), jnp.float32(0.0))
    value_part = jax.ops.segment_sum(
        weighted_rows(weight, values, head_dim), owner, num_segments=total_req
    )
    total_part = jax.ops.segment_sum(weight, owner, num_segments=total_req)
    value_sum, total_sum = (
        lax.psum_scatter(value_part, "blk", scatter_dimension=0, tiled=True),
        lax.psum_scatter(total_part, "blk", scatter_dimension=0, tiled=True),
    )
    run_top = lax.dynamic_slice_in_dim(global_top, here * req_dev, req_dev)
    query_heads = query.astype(jnp.float32).reshape(req_dev, heads_local, head_dim)
    own = (
        jnp.sum(
            query_heads * key_new.astype(jnp.float32).reshape(req_dev, heads_local, head_dim),
            axis=2,
        )
        / jnp.sqrt(jnp.float32(head_dim))
        + bias[0][None, :]
    )
    top_final = jnp.maximum(run_top, own)
    rescale = jnp.exp(run_top - top_final)
    own_weight = jnp.exp(own - top_final)
    total_final = total_sum * rescale + own_weight
    value_final = value_sum * jnp.repeat(rescale, head_dim, axis=1) + jnp.repeat(
        own_weight, head_dim, axis=1
    ) * value_new.astype(jnp.float32)
    attended = (value_final / jnp.repeat(total_final, head_dim, axis=1)).astype(jnp.bfloat16)
    projected = jnp.dot(attended, w_out, preferred_element_type=jnp.float32)
    head_part = lax.psum_scatter(
        projected.astype(jnp.bfloat16), "head", scatter_dimension=1, tiled=True
    ).astype(jnp.float32)
    input_slice = lax.dynamic_slice_in_dim(inputs, head_index * width_local, width_local, 1)
    mixed = (input_slice + head_part).astype(jnp.bfloat16)
    mixed_float = mixed.astype(jnp.float32)
    square_total = lax.psum(jnp.sum(mixed_float * mixed_float, axis=1), "head")
    gain_slice = lax.dynamic_slice_in_dim(ffn_gain, head_index * width_local, width_local)
    scaled = mixed_float * lax.rsqrt(square_total[:, None] / d_model + 1e-05) * gain_slice
    hidden_in = lax.all_gather(scaled.astype(jnp.bfloat16), "head", axis=1, tiled=True)
    gate = jnp.dot(hidden_in, w_gate, preferred_element_type=jnp.float32)
    upper = jnp.dot(hidden_in, w_up, preferred_element_type=jnp.float32)
    hidden = (jax.nn.silu(gate) * upper).astype(jnp.bfloat16)
    down_part = lax.psum_scatter(
        jnp.dot(hidden, w_down, preferred_element_type=jnp.float32).astype(jnp.bfloat16),
        "head",
        scatter_dimension=1,
        tiled=True,
    ).astype(jnp.float32)
    return (mixed_float + down_part).astype(jnp.bfloat16)


def solution(mesh):
    placed = (
        P("blk", None),
        P(),
        P(None, "head"),
        P(None, "head"),
        P(None, "head"),
        P("head", None),
        P(),
        P(None, "head"),
        P(None, "head"),
        P("head", None),
        P("blk", "head"),
        P("blk", "head"),
        P("blk"),
        P(),
        P(None, "head"),
        P(),
        P(),
        P("blk"),
    )
    return jax.shard_map(
        body, mesh=mesh, in_specs=placed, out_specs=P("blk", "head"), check_vma=False
    )
```

profile of v0, /device:TPU:0, one launch (start us, length us, event | category | flops | bytes accessed | tf_op | source)
XLA Modules:
  0.0 433.0 jit_solution(14541460560648316760)
XLA Ops:
  7.3 3.6 gather_fusion.1
  11.6 69.5 %while.24 = (s32[]{:T(128)}, u32[1024]{0:T(1024)S(1)}, u32[1024]{0:T(1024)S(1)}, s32[512]{0:T(512)S(1)}, s32[]{:T(128)}, /*index=5*/s32[]{:T(128)}, s32[]{:T(128)}, s32[]{}) while((s32[]{:T(128)}, u32[1024]{0:T(1024)S(1)}, u32[1024]{0:T(1024)S(1)}, s32[512]{0:T(512)S(1)}, s32[]{:T(128)}, /*index=5*/s32[]{:T(128)}, s32[]{:T(128)}, ...), condition=%wide.region_3.4_spmd.clone, body=%wide.region_2.3_spmd.clone.sunk | while | flops 20484 | bytes 63609 | solution.py:14
  11.6 6.9 %gather_fusion = s32[1024]{0:T(1024)S(1)} fusion(s32[512]{0:T(512)S(1)} %get-tuple-element.165, u32[1024]{0:T(1024)S(1)} %broadcast_clamp_fusion.3), kind=kCustom, calls=%fused_computation.clone.clone.1 | custom fusion | bytes 12288 | tf_op jit(solution)/shard_map/jit(searchsorted)/jit(_searchsorted_scan_impl)/vmap(jit(_searchsorted_scan_impl))/while/body/eval_jaxpr/gather | solution.py:14
  18.5 6.9 %gather_fusion = s32[1024]{0:T(1024)S(1)} fusion(s32[512]{0:T(512)S(1)} %get-tuple-element.165, u32[1024]{0:T(1024)S(1)} %broadcast_clamp_fusion.3), kind=kCustom, calls=%fused_computation.clone.clone.1 | custom fusion | bytes 12288 | tf_op jit(solution)/shard_map/jit(searchsorted)/jit(_searchsorted_scan_impl)/vmap(jit(_searchsorted_scan_impl))/while/body/eval_jaxpr/gather | solution.py:14
  25.5 6.9 %gather_fusion = s32[1024]{0:T(1024)S(1)} fusion(s32[512]{0:T(512)S(1)} %get-tuple-element.165, u32[1024]{0:T(1024)S(1)} %broadcast_clamp_fusion.3), kind=kCustom, calls=%fused_computation.clone.clone.1 | custom fusion | bytes 12288 | tf_op jit(solution)/shard_map/jit(searchsorted)/jit(_searchsorted_scan_impl)/vmap(jit(_searchsorted_scan_impl))/while/body/eval_jaxpr/gather | solution.py:14
  32.4 6.9 %gather_fusion = s32[1024]{0:T(1024)S(1)} fusion(s32[512]{0:T(512)S(1)} %get-tuple-element.165, u32[1024]{0:T(1024)S(1)} %broadcast_clamp_fusion.3), kind=kCustom, calls=%fused_computation.clone.clone.1 | custom fusion | bytes 12288 | tf_op jit(solution)/shard_map/jit(searchsorted)/jit(_searchsorted_scan_impl)/vmap(jit(_searchsorted_scan_impl))/while/body/eval_jaxpr/gather | solution.py:14
  39.4 6.9 %gather_fusion = s32[1024]{0:T(1024)S(1)} fusion(s32[512]{0:T(512)S(1)} %get-tuple-element.165, u32[1024]{0:T(1024)S(1)} %broadcast_clamp_fusion.3), kind=kCustom, calls=%fused_computation.clone.clone.1 | custom fusion | bytes 12288 | tf_op jit(solution)/shard_map/jit(searchsorted)/jit(_searchsorted_scan_impl)/vmap(jit(_searchsorted_scan_impl))/while/body/eval_jaxpr/gather | solution.py:14
  46.3 6.9 %gather_fusion = s32[1024]{0:T(1024)S(1)} fusion(s32[512]{0:T(512)S(1)} %get-tuple-element.165, u32[1024]{0:T(1024)S(1)} %broadcast_clamp_fusion.3), kind=kCustom, calls=%fused_computation.clone.clone.1 | custom fusion | bytes 12288 | tf_op jit(solution)/shard_map/jit(searchsorted)/jit(_searchsorted_scan_impl)/vmap(jit(_searchsorted_scan_impl))/while/body/eval_jaxpr/gather | solution.py:14
  53.3 6.9 %gather_fusion = s32[1024]{0:T(1024)S(1)} fusion(s32[512]{0:T(512)S(1)} %get-tuple-element.165, u32[1024]{0:T(1024)S(1)} %broadcast_clamp_fusion.3), kind=kCustom, calls=%fused_computation.clone.clone.1 | custom fusion | bytes 12288 | tf_op jit(solution)/shard_map/jit(searchsorted)/jit(_searchsorted_scan_impl)/vmap(jit(_searchsorted_scan_impl))/while/body/eval_jaxpr/gather | solution.py:14
  60.2 6.9 %gather_fusion = s32[1024]{0:T(1024)S(1)} fusion(s32[512]{0:T(512)S(1)} %get-tuple-element.165, u32[1024]{0:T(1024)S(1)} %broadcast_clamp_fusion.3), kind=kCustom, calls=%fused_computation.clone.clone.1 | custom fusion | bytes 12288 | tf_op jit(solution)/shard_map/jit(searchsorted)/jit(_searchsorted_scan_impl)/vmap(jit(_searchsorted_scan_impl))/while/body/eval_jaxpr/gather | solution.py:14
  67.2 6.9 %gather_fusion = s32[1024]{0:T(1024)S(1)} fusion(s32[512]{0:T(512)S(1)} %get-tuple-element.165, u32[1024]{0:T(1024)S(1)} %broadcast_clamp_fusion.3), kind=kCustom, calls=%fused_computation.clone.clone.1 | custom fusion | bytes 12288 | tf_op jit(solution)/shard_map/jit(searchsorted)/jit(_searchsorted_scan_impl)/vmap(jit(_searchsorted_scan_impl))/while/body/eval_jaxpr/gather | solution.py:14
  74.1 6.9 %gather_fusion = s32[1024]{0:T(1024)S(1)} fusion(s32[512]{0:T(512)S(1)} %get-tuple-element.165, u32[1024]{0:T(1024)S(1)} %broadcast_clamp_fusion.3), kind=kCustom, calls=%fused_computation.clone.clone.1 | custom fusion | bytes 12288 | tf_op jit(solution)/shard_map/jit(searchsorted)/jit(_searchsorted_scan_impl)/vmap(jit(_searchsorted_scan_impl))/while/body/eval_jaxpr/gather | solution.py:14
  81.7 6.9 %gather_fusion.2 = s32[1024]{0:T(1024)S(1)} fusion(s32[512]{0:T(512)S(1)} %copy-done.1, s32[1024]{0:T(1024)S(1)} %fusion.31), kind=kCustom, calls=%fused_computation.2 | custom fusion | bytes 12288 | tf_op jit(solution)/shard_map/gather | solution.py:15
  89.1 45.3 %all_gather.6 = bf16[512,512]{1,0:T(8,128)(2,1)S(1)} all-gather(bf16[32,512]{1,0:T(8,128)(2,1)S(1)} %convolution_convert_fusion.3), channel_id=1, replica_groups=mesh['blk'=16,'head'=2] {'blk'}, dimensions={0}, use_global_device_ids=true | all-gather | bytes 557056 | tf_op jit(solution)/shard_map/all_gather | solution.py:69
  134.4 5.1 %gather_fusion.3 = bf16[1024,512]{1,0:T(8,128)(2,1)} fusion(bf16[512,512]{1,0:T(8,128)(2,1)S(1)} %all_gather.6, s32[1024]{0:T(1024)S(1)} %broadcast_clamp_fusion.1), kind=kCustom, calls=%fused_computation.3 | custom fusion | bytes 2101248 | tf_op jit(solution)/shard_map/gather | solution.py:72
  141.4 1.9 copy.40
  143.2 1.9 bitcast_reduce_fusion
  145.1 6.9 %gather_fusion.4 = s32[1024]{0:T(1024)S(1)} fusion(s32[512]{0:T(512)S(1)} %copy-done.2, s32[1024]{0:T(1024)S(1)} %broadcast_clamp_fusion.1), kind=kCustom, calls=%fused_computation.4 | custom fusion | bytes 12288 | tf_op jit(solution)/shard_map/gather | solution.py:71
  152.5 7.5 %scatter_custom_fusion = f32[512,8]{1,0:T(8,128)S(1)} fusion(s32[1024]{0:T(1024)S(1)} %bitcast.23, f32[1024,8]{1,0:T(8,128)S(1)} %copy.41, f32[]{:T(128)} %constant.71.clone.1), kind=kCustom, calls=%fused_computation.43 | custom fusion | flops 8192 | bytes 16388 | tf_op jit(solution)/shard_map/scatter-max | solution.py:74
  160.0 74.2 %pmax.7 = f32[512,8]{1,0:T(8,128)S(1)} all-reduce(f32[512,8]{1,0:T(8,128)S(1)} %scatter_custom_fusion), channel_id=1, replica_groups=mesh['blk'=16,'head'=2] {'blk'}, use_global_device_ids=true, to_apply=%region_7.8 | all-reduce | flops 4096 | bytes 32768 | tf_op jit(solution)/shard_map/pmax | solution.py:75
  234.2 2.8 gather_fusion.5
  237.5 8.1 %scatter_custom_fusion.2 = f32[512,8]{1,0:T(8,128)} fusion(s32[1024]{0:T(1024)S(1)} %gather_fusion.2, f32[1024,8]{1,0:T(8,128)S(1)} %copy.45, f32[]{:T(128)} %constant.64.clone.1), kind=kCustom, calls=%fused_computation.41 | custom fusion | flops 8192 | bytes 16388 | tf_op jit(solution)/shard_map/scatter-add | solution.py:80
  248.7 1.9 copy.44
  250.6 9.2 %scatter_custom_fusion.1 = f32[512,512]{1,0:T(8,128)} fusion(s32[1024]{0:T(1024)S(1)} %gather_fusion.2, f32[1024,512]{1,0:T(8,128)} %copy.44, f32[]{:T(128)} %constant.64.clone.1), kind=kCustom, calls=%fused_computation.33 | custom fusion | flops 524288 | bytes 1049088 | tf_op jit(solution)/shard_map/scatter-add | solution.py:77
  261.9 57.9 %reduce-scatter.7.cloned.1.call-done = f32[32,8]{1,0:T(8,128)} async-done(((f32[512,8]{1,0:T(8,128)}), f32[32,8]{1,0:T(8,128)}) %reduce-scatter.7.cloned.1.call-update) | async-done | bytes 1040 | tf_op jit(solution)/shard_map/reduce_scatter | solution.py:83
  321.1 74.9 %reduce-scatter.5.cloned.1.call-done = f32[32,512]{1,0:T(8,128)} async-done(((f32[512,512]{1,0:T(8,128)}), f32[32,512]{1,0:T(8,128)}) %reduce-scatter.5.cloned.1.call-update) | async-done | bytes 65552 | tf_op jit(solution)/shard_map/reduce_scatter | solution.py:82
  396.1 2.0 convolution_convert_fusion
  398.3 4.1 reduce-scatter.9.cloned.1.call-done
  403.3 2.5 psum.7
  407.7 3.0 fusion.35
  410.7 5.7 %fusion.4 = bf16[32,1024]{1,0:T(8,128)(2,1)} fusion(bf16[2048,1024]{1,0:T(8,128)(2,1)} %param.29, bf16[32,1024]{1,0:T(8,128)(2,1)S(1)} %all_gather.7, bf16[1024,2048]{1,0:T(8,128)(2,1)} %param.28, f32[32,2048]{1,0:T(8,128)S(1)} %fusion.35), kind=kOutput, calls=%fused_computation.21 | convolution fusion | flops 268861440 | bytes 8781824 | tf_op jit(solution)/shard_map/dot_general | solution.py:118
  416.4 8.8 %reduce-scatter.11.cloned.1.call-done = bf16[32,512]{1,0:T(8,128)(2,1)} async-done(((bf16[32,1024]{1,0:T(8,128)(2,1)}), bf16[32,512]{1,0:T(8,128)(2,1)}) %reduce-scatter.11.cloned.1.call-update) | async-done | bytes 32784 | tf_op jit(solution)/shard_map/reduce_scatter | solution.py:117
  (119 shorter events, 16.4 us)
Async XLA Ops:
  6.5 389.5 %copy-start = (bf16[512,1024]{1,0:T(8,128)(2,1)S(1)}, bf16[512,1024]{1,0:T(8,128)(2,1)}, u32[]{:S(2)}) copy-start(bf16[512,1024]{1,0:T(8,128)(2,1)} %param.25) | copy-start | bytes 3145732
  6.5 313.3 %reduce-scatter.7.cloned.1.call-start = ((), (), s32[]{:S(2)}) async-start(), calls=%async_computation.5 | async-start | bytes 278528 | tf_op jit(solution)/shard_map/reduce_scatter | solution.py:83
  81.0 0.7 copy-start.1
  81.7 6.9 %copy-start.3 = (bf16[32,1024]{1,0:T(8,128)(2,1)S(1)}, bf16[32,1024]{1,0:T(8,128)(2,1)}, u32[]{:S(2)}) copy-start(bf16[32,1024]{1,0:T(8,128)(2,1)} %param.20) | copy-start | bytes 196612
  81.7 7.0 %copy-start.4 = (bf16[1024,512]{1,0:T(8,128)(2,1)S(1)}, bf16[1024,512]{1,0:T(8,128)(2,1)}, u32[]{:S(2)}) copy-start(bf16[1024,512]{1,0:T(8,128)(2,1)} %param.22) | copy-start | bytes 3145732
  81.7 7.0 %copy-start.8 = (f32[1024]{0:T(1024)S(1)}, f32[1024]{0:T(1024)}, u32[]{:S(2)}) copy-start(f32[1024]{0:T(1024)} %param.21) | copy-start | bytes 12292
  143.2 1.9 copy-start.11
  143.2 1.9 copy-start.2
  145.1 6.9 %copy-start.12 = (s32[16]{0:T(128)S(1)}, s32[16]{0:T(128)}, u32[]{:S(2)}) copy-start(s32[16]{0:T(128)} %param.37) | copy-start | bytes 196
  145.1 7.1 %copy-start.9 = (s32[1024]{0:T(1024)S(1)}, s32[1024]{0:T(1024)}, u32[]{:S(2)}) copy-start(s32[1024]{0:T(1024)} %param.32) | copy-start | bytes 12292
  234.2 11.7 %copy-start.5 = (bf16[1024,512]{1,0:T(8,128)(2,1)S(1)}, bf16[1024,512]{1,0:T(8,128)(2,1)}, u32[]{:S(2)}) copy-start(bf16[1024,512]{1,0:T(8,128)(2,1)} %param.31) | copy-start | bytes 3145732
  245.6 150.4 %reduce-scatter.5.cloned.1.call-start = ((), (), s32[]{:S(2)}) async-start(), calls=%async_computation.4 | async-start | bytes 1114112 | tf_op jit(solution)/shard_map/reduce_scatter | solution.py:82
  250.6 9.3 %copy-start.6 = (bf16[1024,512]{1,0:T(8,128)(2,1)S(1)}, bf16[1024,512]{1,0:T(8,128)(2,1)}, u32[]{:S(2)}) copy-start(bf16[1024,512]{1,0:T(8,128)(2,1)} %param.23) | copy-start | bytes 3145732
  259.8 136.2 %copy-start.7 = (bf16[1024,512]{1,0:T(8,128)(2,1)S(1)}, bf16[1024,512]{1,0:T(8,128)(2,1)}, u32[]{:S(2)}) copy-start(bf16[1024,512]{1,0:T(8,128)(2,1)} %param.24) | copy-start | bytes 3145732
  259.8 142.6 %reduce-scatter.9.cloned.1.call-start = ((), (), s32[]{:S(2)}) async-start(), calls=%async_computation.6 | async-start | bytes 98304 | tf_op jit(solution)/shard_map/reduce_scatter | solution.py:104
  260.9 137.3 %copy-start.10 = (f32[1024]{0:T(1024)S(1)}, f32[1024]{0:T(1024)}, u32[]{:S(2)}) copy-start(f32[1024]{0:T(1024)} %param.26) | copy-start | bytes 12292
  398.1 27.0 %reduce-scatter.11.cloned.1.call-start = ((), (), s32[]{:S(2)}) async-start(), calls=%async_computation.7 | async-start | bytes 98304 | tf_op jit(solution)/shard_map/reduce_scatter | solution.py:117
Sparse Core Ops, SparseCore 0:
  245.7 73.9 reduce-scatter.6
  322.1 73.8 reduce-scatter.4
  398.2 4.1 reduce-scatter.8
  416.5 8.5 reduce-scatter.10
where the time goes:
time: 434 us; the launch traced here: 433 us
  waiting for transfers between devices  146 us (34%)
  blocking collectives  124 us (29%)
  local copies, waits for them, and re-layouts  102 us (24%)
  other arithmetic  35.1 us (8%)
  between operations  13.4 us (3%)
  matrix products  12 us (3%)
    reduce_scatter x1, waiting for transfers between devices, body(): lax.psum_scatter(value_part, 'blk', scatter_dimension=0, tiled=True)  74.9 us
    pmax x1, blocking collectives, body(): global_top = lax.pmax(local_top, 'blk')  74.2 us
    gather x10, local copies, waits for them, and re-layouts, pool_owner(): rank = jnp.searchsorted(ends, position, side='right')  68.7 us
    reduce_scatter x1, waiting for transfers between devices, body(): lax.psum_scatter(total_part, 'blk', scatter_dimension=0, tiled=True)  57.9 us
    all_gather x1, blocking collectives, body(): all_query = lax.all_gather(query, 'blk', axis=0, tiled=True)  45.3 us
    scatter-add x1, other arithmetic, body(): jax.ops.segment_sum(weighted_rows(weight, values, head_dim), owner, num_s...  9.23 us
    reduce_scatter x1, waiting for transfers between devices, body(): lax.psum_scatter(jnp.dot(hidden, w_down, preferred_element_type=jnp.float...  8.76 us
  transfers between devices with their start and end apart: 4, of which 4 were waited for; matrix products, arithmetic and copies ran while one was open for 4% of the time, Pallas kernels for 0%

commit v1 on v0

v1 whole, which is shorter than its diff:
```python
import functools

import jax
import jax.numpy as jnp
from jax import lax
from jax.experimental import pallas as pl
from jax.experimental.pallas import tpu as pltpu
from jax.sharding import PartitionSpec as P

LANES = 128
SHORTEST = 17
FLOOR = -1e30
F32 = jnp.float32
BF16 = jnp.bfloat16
I32 = jnp.int32


def cdiv(a, b):
    return -(-a // b)


def split_by(x, n):
    if n & (n - 1) == 0:
        return lax.shift_right_logical(x, n.bit_length() - 1), x & (n - 1)
    q = lax.div(x, n)
    return q, x - q * n


def iota(shape, dim):
    return lax.broadcasted_iota(I32, shape, dim)


def dot(a, b):
    return jnp.dot(a, b, preferred_element_type=F32)


def dot_exact(a, b):
    return jnp.dot(a, b, preferred_element_type=F32, precision=lax.Precision.HIGHEST)


def one_hot(mask):
    return jnp.where(mask, F32(1), F32(0)).astype(BF16)


def normalize(inputs, gain):
    mean_square = jnp.mean(inputs * inputs, axis=-1, keepdims=True)
    return inputs * lax.rsqrt(mean_square + 1e-05) * gain


class Sizes:
    def __init__(self, groups, req_dev, pool_dev, block, heads, head_dim):
        self.groups, self.req, self.pool = groups, req_dev, pool_dev
        self.block, self.heads, self.dim = block, heads, head_dim
        self.total = groups * req_dev
        most = (pool_dev - 2) // SHORTEST + 2
        self.slot = cdiv(most, groups)
        self.slots = groups * self.slot
        self.width = heads * head_dim
        self.chunks = self.width // LANES
        self.pair = LANES // head_dim
        self.ask_rows = cdiv(self.chunks * self.slot, 16) * 16
        self.back_rows = cdiv((self.chunks + 1) * self.slot, 16) * 16


def message_rows(z, rows, parts, transpose=False):
    shape = (z.groups * rows, parts * z.slots)
    m_dim, s_dim = (1, 0) if transpose else (0, 1)
    if transpose:
        shape = shape[::-1]
    group, inner = split_by(iota(shape, m_dim), rows)
    part, slot = split_by(inner, z.slot)
    source = part * z.slots + group * z.slot + slot
    return one_hot((source == iota(shape, s_dim)) & (part < parts))


def place_rows(lengths, order, variate, step=512):
    total = order.shape[1]
    step = min(step, total)
    sub = iota((16, total), 0)
    table = jnp.where(
        sub == 0,
        lax.shift_right_logical(lengths, 6),
        jnp.where(sub == 1, lengths & 63, jnp.where(sub == 2, variate, 0)),
    )
    table = table.astype(F32).astype(BF16)
    request = iota((total, step), 0)
    found, sums = [], []
    for at in range(0, total, step):
        found.append(dot(table, one_hot(request == order[:, at : at + step])))
    ordered = jnp.concatenate(found, axis=1) if len(found) > 1 else found[0]
    ordered_low = ordered.astype(BF16)
    for at in range(0, total, step):
        before = one_hot(iota((at + step, step), 0) <= iota((at + step, step), 1) + at)
        sums.append(dot(ordered_low[:, : at + step], before))
    summed = jnp.concatenate(sums, axis=1) if len(sums) > 1 else sums[0]
    ends = summed[0:1] * 64.0 + summed[1:2]
    starts = ends - (ordered[0:1] * 64.0 + ordered[1:2])
    return starts, ends, ordered[2:3]


def ask_kernel(z, tokens_ref, gain_ref, w_query_ref, lengths_ref, order_ref, variate_ref, live_ref,
               ask_ref, query_ref, home_ref, slot_ref, live_out_ref, w_query, sem):
    me = lax.axis_index("blk")
    copy = pltpu.make_async_copy(w_query_ref, w_query, sem)
    copy.start()
    order = order_ref[...]
    starts, ends, variates = place_rows(lengths_ref[...], order, variate_ref[...])
    shape = (z.slots, z.total)
    place = iota(shape, 1)
    other, turn = split_by(iota((z.slots, 1), 0), z.slot)
    home_of, local = split_by(order, z.req)

    def choose(home, pool):
        low = (pool * z.pool).astype(F32)
        first = jnp.sum(jnp.where(ends <= low, F32(1), F32(0)), axis=1, keepdims=True)
        first = first.astype(I32) + turn * z.groups
        return (
            (home_of == home)
            & (starts < low + F32(z.pool))
            & (place >= first)
            & (place < first + z.groups)
        )

    mine = choose(me, other)
    row = jnp.sum(jnp.where(mine, local.astype(F32) + 1.0, F32(0)), axis=1, keepdims=True) - 1.0
    row = row.astype(I32)
    home_ref[...] = jnp.broadcast_to(row, home_ref.shape)
    theirs = choose(other, jnp.full((1, 1), me, I32))
    low = (me * z.pool).astype(F32)
    begin = jnp.sum(jnp.where(theirs, starts - low, F32(0)), axis=1, keepdims=True)
    finish = jnp.sum(jnp.where(theirs, ends - low, F32(0)), axis=1, keepdims=True)
    kind = jnp.sum(jnp.where(theirs, variates, F32(0)), axis=1, keepdims=True)
    lane = iota((z.slots, LANES), 1)
    slot_ref[...] = jnp.where(
        lane == 0, begin, jnp.where(lane == 1, finish, kind)
    ).astype(I32)
    blocks = live_ref.shape[1]
    spread = one_hot(
        split_by(iota((blocks, z.pool), 1), z.block)[0] == iota((blocks, z.pool), 0)
    )
    live = jnp.broadcast_to(live_ref[...].astype(F32).astype(BF16), (16, blocks))
    live_out_ref[...] = dot(live, spread)[:8].astype(I32)

    normed = normalize(tokens_ref[...].astype(F32), gain_ref[...]).astype(BF16)
    copy.wait()
    query = dot(normed, w_query[...]).astype(BF16)
    query_ref[...] = query
    picked = dot(one_hot(row == iota((z.slots, z.req), 1)), query).astype(BF16)
    stacked = jnp.concatenate(
        [picked[:, c * LANES : (c + 1) * LANES] for c in range(z.chunks)], axis=0
    )
    ask_ref[...] = dot(message_rows(z, z.ask_rows, z.chunks), stacked).astype(BF16)


def pieces(z, columns):
    rows = columns[0].shape[0]
    lane = iota((rows, LANES), 1)
    full = jnp.zeros((rows, LANES), F32)
    for h, column in enumerate(columns):
        full = jnp.where((lane & (z.heads - 1)) == h, column, full)
    high = full.astype(BF16).astype(F32)
    rest = full - high
    middle = rest.astype(BF16).astype(F32)
    last = rest - middle
    n = z.heads
    return jnp.where(
        lane < n, high, jnp.where(lane < 2 * n, middle, jnp.where(lane < 3 * n, last, F32(0)))
    ).astype(BF16)


def own_kernel(z, tokens_ref, gain_ref, w_key_ref, w_value_ref, query_ref, bias_ref,
               value_ref, stat_ref):
    normed = normalize(tokens_ref[...].astype(F32), gain_ref[...]).astype(BF16)
    key_new = dot(normed, w_key_ref[...]).astype(BF16)
    value_ref[...] = dot(normed, w_value_ref[...]).astype(BF16)
    product = query_ref[...].astype(F32) * key_new.astype(F32)
    columns = []
    for h in range(z.heads):
        c, inner = divmod(h, z.pair)
        part = product[:, c * LANES : (c + 1) * LANES]
        lane_head = split_by(iota(part.shape, 1), z.dim)[0]
        raw = jnp.sum(jnp.where(lane_head == inner, part, F32(0)), axis=1, keepdims=True)
        columns.append(raw * F32(z.dim**-0.5) + bias_ref[0, h])
    stat_ref[...] = pieces(z, columns)


def attend_kernel(z, ask_ref, keys_ref, values_ref, slot_ref, variate_ref, live_ref, bias_ref, back_ref):
    stacked = dot(message_rows(z, z.ask_rows, z.chunks, transpose=True), ask_ref[...])
    begin, finish, kind = slot_ref[:, 0:1], slot_ref[:, 1:2], slot_ref[:, 2:3]
    shape = (z.slots, z.pool)
    token = iota(shape, 1)
    used = (token >= begin) & (token < finish) & (live_ref[0:1] > 0)
    same = variate_ref[...] == kind
    lane = split_by(iota((z.slots, LANES), 1), z.dim)[0]
    columns, parts = [], []
    for c in range(z.chunks):
        asked = stacked[c * z.slots : (c + 1) * z.slots] * F32(z.dim**-0.5)
        wide = jnp.concatenate(
            [jnp.where(lane == i, asked, F32(0)) for i in range(z.pair)], axis=0
        ).astype(BF16)
        chunk = slice(c * LANES, (c + 1) * LANES)
        score = lax.dot_general(
            wide, keys_ref[:, chunk], (((1,), (1,)), ((), ())), preferred_element_type=F32
        )
        weights, scale = [], []
        for i in range(z.pair):
            h = c * z.pair + i
            one = score[i * z.slots : (i + 1) * z.slots]
            one = one + jnp.where(same, bias_ref[0, h], bias_ref[1, h])
            one = jnp.where(used, one, F32(FLOOR))
            top = jnp.maximum(jnp.max(one, axis=1, keepdims=True), F32(FLOOR * 0.1))
            weight = jnp.exp(one - top).astype(BF16)
            total = jnp.sum(weight.astype(F32), axis=1, keepdims=True)
            some = total > 0
            safe = jnp.where(some, total, F32(1))
            columns.append(jnp.where(some, top + jnp.log(safe), F32(FLOOR)))
            scale.append(1.0 / safe)
            weights.append(weight)
        summed = dot(jnp.concatenate(weights, axis=0), values_ref[:, chunk])
        summed = summed * jnp.concatenate(scale, axis=0)
        part = summed[: z.slots]
        for i in range(1, z.pair):
            part = jnp.where(lane == i, summed[i * z.slots : (i + 1) * z.slots], part)
        parts.append(part.astype(BF16))
    parts.append(pieces(z, columns))
    back_ref[...] = dot(
        message_rows(z, z.back_rows, z.chunks + 1), jnp.concatenate(parts, axis=0)
    ).astype(BF16)


def merge_kernel(z, back_ref, home_ref, value_ref, stat_ref, w_out_ref, part_ref):
    stacked = dot(message_rows(z, z.back_rows, z.chunks + 1, transpose=True), back_ref[...]).astype(BF16)
    stat = jnp.concatenate([stacked[z.chunks * z.slots :], stat_ref[...]], axis=0)
    rows = z.slots + z.req
    wide = z.heads * z.req
    head_at, _ = split_by(iota((LANES, wide), 1), z.req)
    from_lane = iota((LANES, wide), 0)
    spread = one_hot(((from_lane & (z.heads - 1)) == head_at) & (from_lane < 3 * z.heads))
    level = dot(stat, spread)
    _, request = split_by(iota((rows, wide), 1), z.req)
    owner = jnp.concatenate([home_ref[:, 0:1], iota((z.req, 1), 0)], axis=0)
    match = owner == request
    level = jnp.where(match, level, F32(FLOOR))
    top = jnp.max(level, axis=0, keepdims=True)
    weight = jnp.where(match, jnp.exp(level - top), F32(0))
    weight = weight / jnp.sum(weight, axis=0, keepdims=True)
    high = weight.astype(BF16)
    low = (weight - high.astype(F32)).astype(BF16)
    lane = split_by(iota((z.req, LANES), 1), z.dim)[0]
    attended = []
    for c in range(z.chunks):
        held = jnp.concatenate(
            [stacked[c * z.slots : (c + 1) * z.slots], value_ref[:, c * LANES : (c + 1) * LANES]],
            axis=0,
        )
        dims = (((0,), (0,)), ((), ()))
        summed = lax.dot_general(high, held, dims, preferred_element_type=F32)
        summed = summed + lax.dot_general(low, held, dims, preferred_element_type=F32)
        base = c * z.pair * z.req
        part = summed[base : base + z.req]
        for i in range(1, z.pair):
            part = jnp.where(lane == i, summed[base + i * z.req : base + (i + 1) * z.req], part)
        attended.append(part.astype(BF16))
    part_ref[...] = dot(jnp.concatenate(attended, axis=1), w_out_ref[...]).astype(BF16)


def call(kernel, out, operands, specs, scratch=(), flops=0, nbytes=0, name=None):
    return pl.pallas_call(
        kernel,
        out_shape=[jax.ShapeDtypeStruct(s, d) for s, d in out],
        in_specs=specs,
        out_specs=[pl.BlockSpec(memory_space=pltpu.VMEM)] * len(out),
        scratch_shapes=list(scratch),
        compiler_params=pltpu.CompilerParams(vmem_limit_bytes=24 * 1024 * 1024),
        cost_estimate=pl.CostEstimate(flops=flops, bytes_accessed=nbytes, transcendentals=0),
        name=name,
    )(*operands)


def head_sum(x):
    if lax.axis_size("head") == 2:
        return x.astype(F32) + lax.ppermute(x, "head", [(0, 1), (1, 0)]).astype(F32)
    return lax.psum(x.astype(F32), "head")


def body(
    tokens,
    norm_gain,
    w_query,
    w_key,
    w_value,
    w_out,
    ffn_gain,
    w_gate,
    w_up,
    w_down,
    keys,
    values,
    key_variate,
    query_variate,
    bias,
    lengths,
    order,
    live_blocks,
):
    groups = lax.axis_size("blk")
    z = Sizes(
        groups,
        tokens.shape[0],
        keys.shape[0],
        keys.shape[0] // live_blocks.shape[0],
        bias.shape[1],
        w_query.shape[1] // bias.shape[1],
    )
    d_model = tokens.shape[1]
    head_count = lax.axis_size("head")
    width_local = d_model // head_count
    vmem = pl.BlockSpec(memory_space=pltpu.VMEM)
    smem = pl.BlockSpec(memory_space=pltpu.SMEM)
    anywhere = pl.BlockSpec(memory_space=pl.ANY)
    gain = norm_gain.reshape(1, -1)
    ask, query, home, slot, live = call(
        functools.partial(ask_kernel, z),
        [
            ((groups * z.ask_rows, LANES), BF16),
            ((z.req, z.width), BF16),
            ((z.slots, LANES), I32),
            ((z.slots, LANES), I32),
            ((8, z.pool), I32),
        ],
        (tokens, gain, w_query, lengths.reshape(1, -1), order.reshape(1, -1),
         query_variate.reshape(1, -1), live_blocks.reshape(1, -1)),
        [vmem, vmem, anywhere, vmem, vmem, vmem, vmem],
        scratch=[pltpu.VMEM(w_query.shape, BF16), pltpu.SemaphoreType.DMA],
        flops=10**9, nbytes=2 * 10**6, name="ask",
    )
    asked = lax.all_to_all(ask.reshape(groups, z.ask_rows, LANES), "blk", 0, 0).reshape(ask.shape)
    value_new, own = call(
        functools.partial(own_kernel, z),
        [((z.req, z.width), BF16), ((z.req, LANES), BF16)],
        (tokens, gain, w_key, w_value, query, bias),
        [vmem, vmem, vmem, vmem, vmem, smem],
        flops=10**9, nbytes=3 * 10**6, name="own",
    )
    (back,) = call(
        functools.partial(attend_kernel, z),
        [((groups * z.back_rows, LANES), BF16)],
        (asked, keys, values, slot, key_variate.reshape(1, -1), live, bias),
        [vmem, vmem, vmem, vmem, vmem, vmem, smem],
        flops=10**9, nbytes=3 * 10**6, name="attend",
    )
    returned = lax.all_to_all(back.reshape(groups, z.back_rows, LANES), "blk", 0, 0).reshape(back.shape)
    (part,) = call(
        functools.partial(merge_kernel, z),
        [((z.req, d_model), BF16)],
        (returned, home, value_new, own, w_out),
        [vmem] * 5,
        flops=10**9, nbytes=2 * 10**6, name="merge",
    )
    mixed = (tokens.astype(F32) + head_sum(part)).astype(BF16).astype(F32)
    hidden_in = normalize(mixed, ffn_gain).astype(BF16)
    gate = dot(hidden_in, w_gate)
    upper = dot(hidden_in, w_up)
    hidden = (jax.nn.silu(gate) * upper).astype(BF16)
    down = dot(hidden, w_down).astype(BF16)
    at = lax.axis_index("head")
    mixed_here = lax.dynamic_slice_in_dim(mixed, at * width_local, width_local, 1)
    if head_count == 2:
        here = lax.dynamic_slice_in_dim(down, at * width_local, width_local, 1)
        there = lax.dynamic_slice_in_dim(down, (1 - at) * width_local, width_local, 1)
        summed = here.astype(F32) + lax.ppermute(there, "head", [(0, 1), (1, 0)]).astype(F32)
    else:
        summed = lax.psum_scatter(down, "head", scatter_dimension=1, tiled=True).astype(F32)
    return (mixed_here + summed).astype(BF16)


def solution(mesh):
    placed = (
        P("blk", None),
        P(),
        P(None, "head"),
        P(None, "head"),
        P(None, "head"),
        P("head", None),
        P(),
        P(None, "head"),
        P(None, "head"),
        P("head", None),
        P("blk", "head"),
        P("blk", "head"),
        P("blk"),
        P(),
        P(None, "head"),
        P(),
        P(),
        P("blk"),
    )
    return jax.shard_map(
        body, mesh=mesh, in_specs=placed, out_specs=P("blk", "head"), check_vma=False
    )
```

time: 434 us -> 54.4 us (0.13)
  waiting for transfers between devices: 146 us -> 8.92 us
  blocking collectives: 124 us -> 15.6 us
  local copies, waits for them, and re-layouts: 102 us -> 9.33 us
  other arithmetic: 35.1 us -> 0.78 us
  between operations: 13.4 us -> 0.11 us
  Pallas kernels: 0 us -> 6.95 us
    reduce_scatter x4 -> x0, waiting for transfers between devices: 146 us -> none  [the longest x1 74.9 us: body(): lax.psum_scatter(value_part, 'blk', scatter_dimension=0, tiled=True)]
    gather x16 -> x0, local copies, waits for them, and re-layouts: 94 us -> none  [the longest x10 68.7 us: pool_owner(): rank = jnp.searchsorted(ends, position, side='right')]
    pmax x1 -> x0, blocking collectives: 74.2 us -> none  [body(): global_top = lax.pmax(local_top, 'blk')]
    all_gather x2 -> x0, blocking collectives: 47.2 us -> none  [the longest x1 45.3 us: body(): all_query = lax.all_gather(query, 'blk', axis=0, tiled=True)]
    scatter-add x2 -> x0, other arithmetic: 17.4 us -> none  [the longest x1 9.23 us: body(): jax.ops.segment_sum(weighted_rows(weight, values, head_dim), owner, num_s...]
    all_to_all x0 -> x1, blocking collectives: none -> 15.6 us  [body(): lax.all_to_all(ask.reshape(groups, z.ask_rows, LANES), 'blk', 0, 0)]
    another operation x4 -> x0, other arithmetic: 7.91 us -> none  [the longest x1 7.49 us: body(): jnp.full((total_req, heads_local), -1e+30, jnp.float32).at[owner]]
    unnamed x27 -> x36, local copies, waits for them, and re-layouts: 2.05 us -> 9.31 us
  transfers between devices with their start and end apart: 4 -> 3, of which waited for: 4 -> 3; matrix products, arithmetic and copies ran while one was open for 4% -> 0% of each run, Pallas kernels for 0% -> 2%
where the time goes in v1:
time: 54.4 us; the launch traced here: 53.8 us
  blocking collectives  15.6 us (29%)
  local copies, waits for them, and re-layouts  9.33 us (17%)
  waiting for transfers between devices  8.92 us (16%)
  matrix products  8.15 us (15%)
  Pallas kernels  6.95 us (13%)
  starting transfers between devices  3.9 us (7%)
  other arithmetic  0.78 us (1%)
    all_to_all x1, blocking collectives, body(): lax.all_to_all(ask.reshape(groups, z.ask_rows, LANES), 'blk', 0, 0)  15.6 us
    unnamed x36, local copies, waits for them, and re-layouts  9.31 us
    dot_general x2, matrix products, dot(): return jnp.dot(a, b, preferred_element_type=F32)  8.15 us
    pallas_call x4, Pallas kernels, call(): pl.pallas_call(kernel, out_shape=[jax.ShapeDtypeStruct(s, d) for s, d in...  6.95 us
    all_to_all x1, waiting for transfers between devices, body(): lax.all_to_all(back.reshape(groups, z.back_rows, LANES), 'blk', 0, 0)  6.63 us
    all_to_all x1, starting transfers between devices, body(): lax.all_to_all(back.reshape(groups, z.back_rows, LANES), 'blk', 0, 0)  3.64 us
    ppermute x1, waiting for transfers between devices, head_sum(): return x.astype(F32) + lax.ppermute(x, 'head', [(0, 1), (1, 0)]).astype(F32)  1.24 us
  transfers between devices with their start and end apart: 3, of which 3 were waited for; matrix products, arithmetic and copies ran while one was open for 0% of the time, Pallas kernels for 2%

profile of v1, /device:TPU:0, one launch (start us, length us, event | category | flops | bytes accessed | tf_op | source)
XLA Modules:
  0.0 53.8 jit_solution(13729120927356879678)
XLA Ops:
  0.0 0.9 %copy-done = bf16[32,1024]{1,0:T(8,128)(2,1)S(1)} copy-done((bf16[32,1024]{1,0:T(8,128)(2,1)S(1)}, bf16[32,1024]{1,0:T(8,128)(2,1)}, u32[]{:S(2)}) %copy-start) | copy-done | bytes 65560
  0.9 1.2 %copy-done.2 = bf16[1024,512]{1,0:T(8,128)(2,1)S(1)} copy-done((bf16[1024,512]{1,0:T(8,128)(2,1)S(1)}, bf16[1024,512]{1,0:T(8,128)(2,1)}, u32[]{:S(2)}) %copy-start.2) | copy-done | bytes 1048600
  2.1 0.7 %copy-done.9 = f32[1024]{0:T(1024)S(1)} copy-done((f32[1024]{0:T(1024)S(1)}, f32[1024]{0:T(1024)}, u32[]{:S(2)}) %copy-start.9) | copy-done | bytes 4120
  2.8 0.7 %copy-done.11 = s32[512]{0:T(512)S(1)} copy-done((s32[512]{0:T(512)S(1)}, s32[512]{0:T(512)}, u32[]{:S(2)}) %copy-start.11) | copy-done | bytes 2072
  3.5 0.7 %copy-done.12 = s32[512]{0:T(512)S(1)} copy-done((s32[512]{0:T(512)S(1)}, s32[512]{0:T(512)}, u32[]{:S(2)}) %copy-start.12) | copy-done | bytes 2072
  4.2 0.7 %copy-done.13 = s32[512]{0:T(512)S(1)} copy-done((s32[512]{0:T(512)S(1)}, s32[512]{0:T(512)}, u32[]{:S(2)}) %copy-start.13) | copy-done | bytes 2072
  4.8 0.7 %copy-done.16 = s32[16]{0:T(128)S(1)} copy-done((s32[16]{0:T(128)S(1)}, s32[16]{0:T(128)}, u32[]{:S(2)}) %copy-start.16) | copy-done | bytes 88
  5.5 1.3 %ask.1 = (bf16[256,128]{1,0:T(8,128)(2,1)S(1)}, bf16[32,512]{1,0:T(8,128)(2,1)S(1)}, s32[64,128]{1,0:T(8,128)S(1)}, s32[64,128]{1,0:T(8,128)S(1)}, s32[8,1024]{1,0:T(8,128)S(1)}) custom-call(bf16[32,1024]{1,0:T(8,128)(2,1)S(1)} %copy-done, f32[1,1024]{1,0:T(1,128)S(1)} %bitcast.17, bf16[1024,512]{1,0:T(8,128)(2,1)S(1)} %copy-done.2, s32[1,512]{1,0:T(1,128)S(1)} %bitcast.19, ...), custom_call_target="tpu_custom_call" | custom-call | flops 1000000000 | bytes 2000000 | tf_op jit(solution)/shard_map/ask/pallas_call | solution.py:268
  6.8 15.6 %all_to_all.10 = bf16[16,16,128]{2,1,0:T(8,128)(2,1)S(1)} all-to-all(bf16[16,16,128]{2,1,0:T(8,128)(2,1)S(1)} %bitcast.14), channel_id=1, replica_groups=mesh['blk'=16,'head'=2] {'blk'}, dimensions={0} | all-to-all | bytes 131072 | tf_op jit(solution)/shard_map/all_to_all | solution.py:337
  22.5 1.2 %copy-done.3 = bf16[1024,512]{1,0:T(8,128)(2,1)S(1)} copy-done((bf16[1024,512]{1,0:T(8,128)(2,1)S(1)}, bf16[1024,512]{1,0:T(8,128)(2,1)}, u32[]{:S(2)}) %copy-start.3) | copy-done | bytes 1048600
  23.7 1.2 %copy-done.4 = bf16[1024,512]{1,0:T(8,128)(2,1)S(1)} copy-done((bf16[1024,512]{1,0:T(8,128)(2,1)S(1)}, bf16[1024,512]{1,0:T(8,128)(2,1)}, u32[]{:S(2)}) %copy-start.4) | copy-done | bytes 1048600
  24.9 0.7 %copy-done.8 = s32[1024]{0:T(1024)S(1)} copy-done((s32[1024]{0:T(1024)S(1)}, s32[1024]{0:T(1024)}, u32[]{:S(2)}) %copy-start.8) | copy-done | bytes 4120
  25.6 0.7 %copy-done.14 = f32[2,8]{1,0:T(2,128)S(1)} copy-done((f32[2,8]{1,0:T(2,128)S(1)}, f32[2,8]{1,0:T(2,128)}, u32[]{:S(2)}) %copy-start.14) | copy-done | bytes 88
  26.3 3.5 %attend.1 = bf16[512,128]{1,0:T(8,128)(2,1)} custom-call(bf16[256,128]{1,0:T(8,128)(2,1)S(1)} %bitcast.15, bf16[1024,512]{1,0:T(8,128)(2,1)S(1)} %copy-done.3, bf16[1024,512]{1,0:T(8,128)(2,1)S(1)} %copy-done.4, s32[64,128]{1,0:T(8,128)S(1)} %get-tuple-element.13.slot_ref, s32[1,1024]{1,0:T(1,128)S(1)} %bitcast.16, ...), custom_call_target="tpu_custom_call" | custom-call | flops 1000000000 | bytes 3000000 | tf_op jit(solution)/shard_map/attend/pallas_call | solution.py:268
  29.8 3.6 %all-to-all-start.1 = ((bf16[16,32,128]{2,1,0:T(8,128)(2,1)}), bf16[16,32,128]{2,1,0:T(8,128)(2,1)S(1)}, u32[]{:S(2)}, u32[]{:S(2)}) async-start(bf16[16,32,128]{2,1,0:T(8,128)(2,1)} %bitcast.8), calls=%async_computation.1 | async-start | bytes 262144 | tf_op jit(solution)/shard_map/all_to_all | solution.py:352
  33.4 0.0 copy-done.10
  33.4 0.0 copy-done.15
  33.4 0.0 copy-done.1
  33.4 0.0 copy-done.5
  33.5 0.0 copy-done.6
  33.5 1.1 %own.1 = (bf16[32,512]{1,0:T(8,128)(2,1)S(1)}, bf16[32,128]{1,0:T(8,128)(2,1)S(1)}) custom-call(bf16[32,1024]{1,0:T(8,128)(2,1)S(1)} %copy-done.1, f32[1,1024]{1,0:T(1,128)S(1)} %bitcast.18, bf16[1024,512]{1,0:T(8,128)(2,1)S(1)} %copy-done.5, bf16[1024,512]{1,0:T(8,128)(2,1)S(1)} %copy-done.6, bf16[32,512]{1,0:T(8,128)(2,1)S(1)} %get-tuple-element.16.query_ref, ...), custom_call_target="tpu_custom_call" | custom-call | flops 1000000000 | bytes 3000000 | tf_op jit(solution)/shard_map/own/pallas_call | solution.py:268
  34.6 6.6 %all-to-all-done.1 = bf16[16,32,128]{2,1,0:T(8,128)(2,1)S(1)} async-done(((bf16[16,32,128]{2,1,0:T(8,128)(2,1)}), bf16[16,32,128]{2,1,0:T(8,128)(2,1)S(1)}, u32[]{:S(2)}, u32[]{:S(2)}) %all-to-all-start.1) | async-done | bytes 131104 | tf_op jit(solution)/shard_map/all_to_all | solution.py:352
  41.2 0.0 copy-done.7
  41.2 1.1 %merge.1 = bf16[32,1024]{1,0:T(8,128)(2,1)S(1)} custom-call(bf16[512,128]{1,0:T(8,128)(2,1)S(1)} %bitcast.13, s32[64,128]{1,0:T(8,128)S(1)} %get-tuple-element.15.home_ref, bf16[32,512]{1,0:T(8,128)(2,1)S(1)} %get-tuple-element.17.value_ref, bf16[32,128]{1,0:T(8,128)(2,1)S(1)} %get-tuple-element.18.stat_ref, bf16[512,1024]{1,0:T(8,128)(2,1)S(1)} %copy-done.7), custom_call_target="tpu_custom_call" | custom-call | flops 1000000000 | bytes 2000000 | tf_op jit(solution)/shard_map/merge/pallas_call | solution.py:268
  42.3 0.0 collective-permute-start
  42.3 1.2 %collective-permute-done = bf16[32,1024]{1,0:T(8,128)(2,1)S(1)} collective-permute-done((bf16[32,1024]{1,0:T(8,128)(2,1)S(1)}, bf16[32,1024]{1,0:T(8,128)(2,1)S(1)}, u32[]{:S(2)}, u32[]{:S(2)}) %collective-permute-start) | collective-permute-done | bytes 65568 | tf_op jit(solution)/shard_map/ppermute | solution.py:282
  43.5 0.1 multiply_reduce_fusion
  43.7 3.1 %fusion.11 = f32[32,2048]{1,0:T(8,128)S(1)} fusion(bf16[1024,2048]{1,0:T(8,128)(2,1)} %param.25, f32[32,1024]{1,0:T(8,128)S(1)} %get-tuple-element.20, f32[1024]{0:T(1024)S(1)} %copy-done.17, f32[32]{0:T(128)S(1)} %add_rsqrt_fusion), kind=kOutput, calls=%fused_computation.18 | convolution fusion | flops 134316032 | bytes 4591744 | tf_op jit(solution)/shard_map/dot_general | solution.py:34
  46.8 5.1 %fusion.2 = bf16[32,1024]{1,0:T(8,128)(2,1)S(1)} fusion(bf16[2048,1024]{1,0:T(8,128)(2,1)} %param.27, bf16[1024,2048]{1,0:T(8,128)(2,1)} %param.26, f32[32,2048]{1,0:T(8,128)S(1)} %fusion.11, f32[32,1024]{1,0:T(8,128)S(1)} %get-tuple-element.20, f32[1024]{0:T(1024)S(1)} %copy-done.17, f32[32]{0:T(128)S(1)} %add_rsqrt_fusion), kind=kOutput, calls=%fused_computation.3 | convolution fusion | flops 268959744 | bytes 8851584 | tf_op jit(solution)/shard_map/dot_general | solution.py:34
  51.9 0.2 collective-permute-start.1
  52.1 1.1 %collective-permute-done.1 = bf16[32,512]{1,0:T(8,128)(2,1)S(1)} collective-permute-done((bf16[32,512]{1,0:T(8,128)(2,1)S(1)}, bf16[32,512]{1,0:T(8,128)(2,1)S(1)}, u32[]{:S(2)}, u32[]{:S(2)}) %collective-permute-start.1) | collective-permute-done | bytes 32800 | tf_op jit(solution)/shard_map/ppermute | solution.py:371
  53.1 0.6 %add_convert_fusion.1 = bf16[32,512]{1,0:T(8,128)(2,1)} fusion(bf16[32,512]{1,0:T(8,128)(2,1)S(1)} %collective-permute-done.1, f32[32,1024]{1,0:T(8,128)S(1)} %get-tuple-element.20, s32[]{:T(128)S(6)} %select_n.7, bf16[32,1024]{1,0:T(8,128)(2,1)S(1)} %fusion.2), kind=kLoop, calls=%fused_computation.14 | loop fusion | flops 81920 | bytes 163844 | tf_op jit(solution)/shard_map/convert_element_type | solution.py:374
  (21 shorter events, 0.1 us)
Async XLA Ops:
  0.0 33.4 %copy-start.10 = (f32[1024]{0:T(1024)S(1)}, f32[1024]{0:T(1024)}, u32[]{:S(2)}) copy-start(f32[1024]{0:T(1024)} %param.19) | copy-start | bytes 12292
  0.0 33.4 %copy-start.15 = (f32[2,8]{1,0:T(2,128)S(1)}, f32[2,8]{1,0:T(2,128)}, u32[]{:S(2)}) copy-start(f32[2,8]{1,0:T(2,128)} %bias_ref.3) | copy-start | bytes 196
  0.0 0.9 %copy-start = (bf16[32,1024]{1,0:T(8,128)(2,1)S(1)}, bf16[32,1024]{1,0:T(8,128)(2,1)}, u32[]{:S(2)}) copy-start(bf16[32,1024]{1,0:T(8,128)(2,1)} %tokens_ref.3) | copy-start | bytes 196612
  0.9 1.2 %copy-start.2 = (bf16[1024,512]{1,0:T(8,128)(2,1)S(1)}, bf16[1024,512]{1,0:T(8,128)(2,1)}, u32[]{:S(2)}) copy-start(bf16[1024,512]{1,0:T(8,128)(2,1)} %w_query_ref.1) | copy-start | bytes 3145732
  2.1 0.7 %copy-start.9 = (f32[1024]{0:T(1024)S(1)}, f32[1024]{0:T(1024)}, u32[]{:S(2)}) copy-start(f32[1024]{0:T(1024)} %param.19) | copy-start | bytes 12292
  2.8 0.7 %copy-start.11 = (s32[512]{0:T(512)S(1)}, s32[512]{0:T(512)}, u32[]{:S(2)}) copy-start(s32[512]{0:T(512)} %param.33) | copy-start | bytes 6148
  3.5 0.7 %copy-start.12 = (s32[512]{0:T(512)S(1)}, s32[512]{0:T(512)}, u32[]{:S(2)}) copy-start(s32[512]{0:T(512)} %param.34) | copy-start | bytes 6148
  4.1 0.7 %copy-start.13 = (s32[512]{0:T(512)S(1)}, s32[512]{0:T(512)}, u32[]{:S(2)}) copy-start(s32[512]{0:T(512)} %param.31) | copy-start | bytes 6148
  4.8 0.7 %copy-start.16 = (s32[16]{0:T(128)S(1)}, s32[16]{0:T(128)}, u32[]{:S(2)}) copy-start(s32[16]{0:T(128)} %param.35) | copy-start | bytes 196
  5.5 28.0 %copy-start.1 = (bf16[32,1024]{1,0:T(8,128)(2,1)S(1)}, bf16[32,1024]{1,0:T(8,128)(2,1)}, u32[]{:S(2)}) copy-start(bf16[32,1024]{1,0:T(8,128)(2,1)} %tokens_ref.3) | copy-start | bytes 196612
  5.5 28.0 %copy-start.5 = (bf16[1024,512]{1,0:T(8,128)(2,1)S(1)}, bf16[1024,512]{1,0:T(8,128)(2,1)}, u32[]{:S(2)}) copy-start(bf16[1024,512]{1,0:T(8,128)(2,1)} %w_key_ref.1) | copy-start | bytes 3145732
  5.5 28.0 %copy-start.6 = (bf16[1024,512]{1,0:T(8,128)(2,1)S(1)}, bf16[1024,512]{1,0:T(8,128)(2,1)}, u32[]{:S(2)}) copy-start(bf16[1024,512]{1,0:T(8,128)(2,1)} %w_value_ref.1) | copy-start | bytes 3145732
  5.5 35.7 %copy-start.7 = (bf16[512,1024]{1,0:T(8,128)(2,1)S(1)}, bf16[512,1024]{1,0:T(8,128)(2,1)}, u32[]{:S(2)}) copy-start(bf16[512,1024]{1,0:T(8,128)(2,1)} %w_out_ref.1) | copy-start | bytes 3145732
  22.5 1.2 %copy-start.3 = (bf16[1024,512]{1,0:T(8,128)(2,1)S(1)}, bf16[1024,512]{1,0:T(8,128)(2,1)}, u32[]{:S(2)}) copy-start(bf16[1024,512]{1,0:T(8,128)(2,1)} %keys_ref.1) | copy-start | bytes 3145732
  23.7 1.2 %copy-start.4 = (bf16[1024,512]{1,0:T(8,128)(2,1)S(1)}, bf16[1024,512]{1,0:T(8,128)(2,1)}, u32[]{:S(2)}) copy-start(bf16[1024,512]{1,0:T(8,128)(2,1)} %values_ref.1) | copy-start | bytes 3145732
  24.9 0.7 %copy-start.8 = (s32[1024]{0:T(1024)S(1)}, s32[1024]{0:T(1024)}, u32[]{:S(2)}) copy-start(s32[1024]{0:T(1024)} %param.30) | copy-start | bytes 12292
  25.6 0.7 %copy-start.14 = (f32[2,8]{1,0:T(2,128)S(1)}, f32[2,8]{1,0:T(2,128)}, u32[]{:S(2)}) copy-start(f32[2,8]{1,0:T(2,128)} %bias_ref.3) | copy-start | bytes 196
  29.8 13.9 %copy-start.17 = (f32[1024]{0:T(1024)S(1)}, f32[1024]{0:T(1024)}, u32[]{:S(2)}) copy-start(f32[1024]{0:T(1024)} %param.24) | copy-start | bytes 12292
  29.8 11.4 %all-to-all-start.1 = ((bf16[16,32,128]{2,1,0:T(8,128)(2,1)}), bf16[16,32,128]{2,1,0:T(8,128)(2,1)S(1)}, u32[]{:S(2)}, u32[]{:S(2)}) async-start(bf16[16,32,128]{2,1,0:T(8,128)(2,1)} %bitcast.8), calls=%async_computation.1 | async-start | bytes 262144 | tf_op jit(solution)/shard_map/all_to_all | solution.py:352
  42.3 1.3 %collective-permute-start = (bf16[32,1024]{1,0:T(8,128)(2,1)S(1)}, bf16[32,1024]{1,0:T(8,128)(2,1)S(1)}, u32[]{:S(2)}, u32[]{:S(2)}) collective-permute-start(bf16[32,1024]{1,0:T(8,128)(2,1)S(1)} %merge.1), channel_id=1, source_target_pairs={{0,1},{1,0},{2,3},{3,2},{4,5},{5,4},{6,7},{7,6},{8,9},{9,8},{10,11... | collective-permute-start | bytes 196616 | tf_op jit(solution)/shard_map/ppermute | solution.py:282
  51.9 1.3 %collective-permute-start.1 = (bf16[32,512]{1,0:T(8,128)(2,1)S(1)}, bf16[32,512]{1,0:T(8,128)(2,1)S(1)}, u32[]{:S(2)}, u32[]{:S(2)}) collective-permute-start(bf16[32,512]{1,0:T(8,128)(2,1)S(1)} %constant_dynamic-slice_fusion), channel_id=1, source_target_pairs={{0,1},{1,0},{2,3},{3,2},{4,5},{5,4},{6,7},{7,6},{8,9},{9,8},{10,11... | collective-permute-start | bytes 98312 | tf_op jit(solution)/shard_map/ppermute | solution.py:371

commit v2 on v1

v2 whole, which is shorter than its diff:
```python
import functools

import jax
import jax.numpy as jnp
from jax import lax
from jax.experimental import pallas as pl
from jax.experimental.pallas import tpu as pltpu
from jax.sharding import PartitionSpec as P

LANES = 128
SHORTEST = 17
WHOLE = 63
FLOOR = -1e30
AHEAD = 12
F32 = jnp.float32
BF16 = jnp.bfloat16
I32 = jnp.int32


def cdiv(a, b):
    return -(-a // b)


def split_by(x, n):
    if n & (n - 1) == 0:
        return lax.shift_right_logical(x, n.bit_length() - 1), x & (n - 1)
    q = lax.div(x, n)
    return q, x - q * n


def iota(shape, dim):
    return lax.broadcasted_iota(I32, shape, dim)


def dot(a, b):
    return jnp.dot(a, b, preferred_element_type=F32)


def dot_exact(a, b):
    return jnp.dot(a, b, preferred_element_type=F32, precision=lax.Precision.HIGHEST)


def one_hot(mask):
    return jnp.where(mask, F32(1), F32(0)).astype(BF16)


def normalize(inputs, gain):
    mean_square = jnp.mean(inputs * inputs, axis=-1, keepdims=True)
    return inputs * lax.rsqrt(mean_square + 1e-05) * gain


class Sizes:
    def __init__(self, groups, cores, req_dev, pool_dev, block, heads, head_dim):
        self.groups, self.cores, self.req, self.pool = groups, cores, req_dev, pool_dev
        self.block, self.heads, self.dim = block, heads, head_dim
        self.total = groups * req_dev
        most = (pool_dev - 2) // SHORTEST + 2
        self.slot = cdiv(most, groups)
        self.slots = groups * self.slot
        self.width = heads * head_dim
        self.chunks = self.width // LANES
        self.wide = min(self.width, 2 * LANES)
        self.pair = LANES // head_dim
        self.ask_rows = cdiv(self.chunks * self.slot, 16) * 16
        self.back_rows = cdiv((self.chunks + 1) * self.slot, 8) * 8


def message_rows(z, rows, parts, cores=1, core=None, transpose=False):
    many, few = z.groups * cores * rows, parts * z.slots
    at = iota((1, many) if transpose else (many, 1), 1 if transpose else 0)
    device, inner = split_by(at, rows)
    group, its_core = split_by(device, cores)
    part, slot = split_by(inner, z.slot)
    source = part * z.slots + group * z.slot + slot
    used = part < parts
    if core is not None:
        used = used & (its_core == core)
    source = jnp.where(used, source, -1)
    shape = (few, many) if transpose else (many, few)
    return one_hot(source == iota(shape, 0 if transpose else 1))


def place_rows(lengths, order, variate, step=512):
    total = order.shape[1]
    step = min(step, total)
    sub = iota((16, total), 0)
    table = jnp.where(
        sub == 0,
        lax.shift_right_logical(lengths, 6),
        jnp.where(sub == 1, lengths & 63, jnp.where(sub == 2, variate, 0)),
    )
    table = table.astype(F32).astype(BF16)
    request = iota((total, step), 0)
    found, sums = [], []
    for at in range(0, total, step):
        found.append(dot(table, one_hot(request == order[:, at : at + step])))
    ordered = jnp.concatenate(found, axis=1) if len(found) > 1 else found[0]
    ordered_low = ordered.astype(BF16)
    for at in range(0, total, step):
        before = one_hot(iota((at + step, step), 0) <= iota((at + step, step), 1) + at)
        sums.append(dot(ordered_low[:, : at + step], before))
    summed = jnp.concatenate(sums, axis=1) if len(sums) > 1 else sums[0]
    ends = summed[0:1] * 64.0 + summed[1:2]
    starts = ends - (ordered[0:1] * 64.0 + ordered[1:2])
    return starts, ends, ordered[2:3]


def fetch(pairs, sems):
    copies = [pltpu.make_async_copy(src, dst, sems.at[i]) for i, (src, dst) in enumerate(pairs)]
    for copy in copies:
        copy.start()
    return copies


def ask_kernel(z, lengths_hbm, order_hbm, variate_hbm, live_hbm, key_variate_hbm, bias_hbm, tokens_hbm,
               gain_hbm, w_query_hbm, ask_ref, rows_ref, facts_ref, home_ref,
               bias_ref, lengths_ref, order_ref, variate_ref, live_ref, key_variate_ref, tokens_ref,
               gain_ref, w_query_ref, sems):
    me = lax.axis_index("blk")
    copies = fetch(
        [
            (lengths_hbm, lengths_ref),
            (order_hbm, order_ref),
            (variate_hbm, variate_ref),
            (live_hbm, live_ref),
            (key_variate_hbm, key_variate_ref),
            (bias_hbm, bias_ref),
            (tokens_hbm, tokens_ref),
            (gain_hbm, gain_ref),
            (w_query_hbm, w_query_ref),
        ],
        sems,
    )
    for copy in copies[:6]:
        copy.wait()
    order = order_ref[...]
    starts, ends, variates = place_rows(lengths_ref[...], order, variate_ref[...])
    shape = (z.slots, z.total)
    place = iota(shape, 1)
    other, turn = split_by(iota((z.slots, 1), 0), z.slot)
    home_of, local = split_by(order, z.req)

    def choose(home, pool):
        low = (pool * z.pool).astype(F32)
        first = jnp.sum(jnp.where(ends <= low, F32(1), F32(0)), axis=1, keepdims=True)
        first = first.astype(I32) + turn * z.groups
        return (
            (home_of == home)
            & (starts < low + F32(z.pool))
            & (place >= first)
            & (place < first + z.groups)
        )

    mine = choose(me, other)
    row = jnp.sum(jnp.where(mine, local.astype(F32) + 1.0, F32(0)), axis=1, keepdims=True) - 1.0
    row = row.astype(I32)
    theirs = choose(other, jnp.full((1, 1), me, I32))
    low = (me * z.pool).astype(F32)
    begin = jnp.sum(jnp.where(theirs, starts - low, F32(0)), axis=1, keepdims=True)
    finish = jnp.sum(jnp.where(theirs, ends - low, F32(0)), axis=1, keepdims=True)
    kind = jnp.sum(jnp.where(theirs, variates, F32(0)), axis=1, keepdims=True)
    lane = iota((z.slots, LANES), 1)
    facts = jnp.where(lane == 0, begin, jnp.where(lane == 1, finish, kind))
    facts_ref[8:, 0:LANES] = facts
    home_ref[...] = jnp.broadcast_to(row, home_ref.shape)
    blocks = live_ref.shape[1]
    spread = one_hot(
        split_by(iota((blocks, z.pool), 1), z.block)[0] == iota((blocks, z.pool), 0)
    )
    live = jnp.broadcast_to(live_ref[...].astype(F32).astype(BF16), (16, blocks))
    kinds = jnp.where(dot(live, spread)[:1] > 0, key_variate_ref[...], -1)
    facts_ref[0:1, :] = kinds.astype(F32)
    facts_ref[1:3, 0 : z.heads] = bias_ref[...]

    for copy in copies[6:]:
        copy.wait()
    normed = normalize(tokens_ref[...].astype(F32), gain_ref[...]).astype(BF16)
    rows_ref[:, z.width :] = normed
    query = dot(normed, w_query_ref[...]).astype(BF16)
    rows_ref[:, : z.width] = query
    picked = dot(one_hot(row == iota((z.slots, z.req), 1)), query).astype(BF16)
    stacked = jnp.concatenate(
        [picked[:, c * LANES : (c + 1) * LANES] for c in range(z.chunks)], axis=0
    )
    ask_ref[...] = dot(message_rows(z, z.ask_rows, z.chunks), stacked).astype(BF16)


def pieces(z, columns):
    rows = columns[0].shape[0]
    lane = iota((rows, LANES), 1)
    full = jnp.zeros((rows, LANES), F32)
    for h, column in enumerate(columns):
        full = jnp.where((lane & (z.heads - 1)) == h, column, full)
    high = full.astype(BF16).astype(F32)
    rest = full - high
    middle = rest.astype(BF16).astype(F32)
    last = rest - middle
    n = z.heads
    return jnp.where(
        lane < n, high, jnp.where(lane < 2 * n, middle, jnp.where(lane < 3 * n, last, F32(0)))
    ).astype(BF16)


def hold_kernel(*refs):
    refs[-1][...] = jnp.zeros(refs[-1].shape, F32)


def own_kernel(z, after_ref, rows_ref, facts_ref, w_key_ref, w_value_ref, value_ref, stat_ref):
    del after_ref
    normed = rows_ref[:, z.width :]
    key_new = dot(normed, w_key_ref[...]).astype(BF16)
    product = rows_ref[:, : z.width].astype(F32) * key_new.astype(F32)
    columns = []
    for h in range(z.heads):
        c, inner = divmod(h, z.pair)
        part = product[:, c * LANES : (c + 1) * LANES]
        lane_head = split_by(iota(part.shape, 1), z.dim)[0]
        raw = jnp.sum(jnp.where(lane_head == inner, part, F32(0)), axis=1, keepdims=True)
        columns.append(raw * F32(z.dim**-0.5) + facts_ref[1:2, h : h + 1])
    stat_ref[...] = pieces(z, columns)
    value_ref[...] = dot(normed, w_value_ref[...]).astype(BF16)


def feed_kernel(steps, tokens_ref, part_ref, other_ref, gain_ref, w_gate_ref, w_up_ref, w_down_ref,
                mixed_ref, down_ref):
    mixed = tokens_ref[...].astype(F32) + (part_ref[...].astype(F32) + other_ref[...].astype(F32))
    mixed = mixed.astype(BF16).astype(F32)
    hidden_in = normalize(mixed, gain_ref[...]).astype(BF16)
    units = w_gate_ref.shape[1] // steps
    total = jnp.zeros(mixed.shape, F32)
    for step in range(steps):
        at = slice(step * units, (step + 1) * units)
        gate = dot(hidden_in, w_gate_ref[:, at])
        upper = dot(hidden_in, w_up_ref[:, at])
        hidden = (jax.nn.silu(gate) * upper).astype(BF16)
        total = total + dot(hidden, w_down_ref[at, :])
    mixed_ref[...] = mixed.astype(BF16)
    down_ref[...] = total.astype(BF16)


def attend_kernel(z, ask_ref, keys_ref, values_ref, facts_ref, after_ref, back_ref, done_ref):
    del after_ref
    done_ref[...] = jnp.zeros(done_ref.shape, F32)
    stacked = dot(message_rows(z, z.ask_rows, z.chunks, transpose=True), ask_ref[...])
    begin, finish, kind = facts_ref[8:, 0:1], facts_ref[8:, 1:2], facts_ref[8:, 2:3]
    token = iota((z.slots, z.pool), 1).astype(F32)
    kinds = facts_ref[0:1, :]
    used = (token >= begin) & (token < finish) & (kinds >= 0)
    same = kinds == kind
    lane = split_by(iota((z.slots, z.wide), 1), z.dim)[0]
    many = z.wide // z.dim
    each = z.wide // LANES
    columns, parts = [], []
    for c in range(z.width // z.wide):
        asked = jnp.concatenate(
            [stacked[(c * each + i) * z.slots : (c * each + i + 1) * z.slots] for i in range(each)], axis=1
        )
        asked = (asked * F32(z.dim**-0.5)).astype(BF16)
        blocks = jnp.concatenate(
            [jnp.where(lane == i, asked, jnp.zeros_like(asked)) for i in range(many)], axis=0
        )
        chunk = slice(c * z.wide, (c + 1) * z.wide)
        score = lax.dot_general(
            blocks, keys_ref[:, chunk], (((1,), (1,)), ((), ())), preferred_element_type=F32
        )
        weights, scale = [], []
        for i in range(many):
            h = c * many + i
            one = score[i * z.slots : (i + 1) * z.slots]
            one = one + jnp.where(same, facts_ref[1:2, h : h + 1], facts_ref[2:3, h : h + 1])
            one = jnp.where(used, one, F32(FLOOR))
            top = jnp.maximum(jnp.max(one, axis=1, keepdims=True), F32(FLOOR * 0.1))
            weight = jnp.exp(one - top)
            total = jnp.sum(weight, axis=1, keepdims=True)
            some = total > 0
            safe = jnp.where(some, total, F32(1))
            columns.append(jnp.where(some, top + jnp.log(safe), F32(FLOOR)))
            scale.append(1.0 / safe)
            weights.append(weight.astype(BF16))
        summed = dot(jnp.concatenate(weights, axis=0), values_ref[:, chunk])
        part = summed[: z.slots] * scale[0]
        for i in range(1, many):
            part = jnp.where(lane == i, summed[i * z.slots : (i + 1) * z.slots] * scale[i], part)
        part = part.astype(BF16)
        parts += [part[:, i * LANES : (i + 1) * LANES] for i in range(each)]
    parts.append(pieces(z, columns))
    back_ref[...] = dot(
        message_rows(z, z.back_rows, z.chunks + 1, z.cores), jnp.concatenate(parts, axis=0)
    ).astype(BF16)


def merged(z, stacked, owner, value, stat):
    stat = jnp.concatenate([stacked[z.chunks * z.slots :], stat], axis=0)
    rows = z.slots + z.req
    wide = z.heads * z.req
    head_at, _ = split_by(iota((LANES, wide), 1), z.req)
    from_lane = iota((LANES, wide), 0)
    spread = one_hot(((from_lane & (z.heads - 1)) == head_at) & (from_lane < 3 * z.heads))
    level = dot(stat, spread)
    _, request = split_by(iota((rows, wide), 1), z.req)
    match = owner == request
    level = jnp.where(match, level, F32(FLOOR))
    top = jnp.max(level, axis=0, keepdims=True)
    weight = jnp.where(match, jnp.exp(level - top), F32(0))
    weight = weight / jnp.sum(weight, axis=0, keepdims=True)
    high = weight.astype(BF16)
    low = (weight - high.astype(F32)).astype(BF16)
    held = jnp.concatenate(
        [
            jnp.concatenate([stacked[c * z.slots : (c + 1) * z.slots] for c in range(z.chunks)], axis=1),
            value,
        ],
        axis=0,
    )
    dims = (((0,), (0,)), ((), ()))
    summed = lax.dot_general(high, held, dims, preferred_element_type=F32)
    summed = summed + lax.dot_general(low, held, dims, preferred_element_type=F32)
    lane = split_by(iota((z.req, z.width), 1), z.dim)[0]
    attended = summed[: z.req]
    for h in range(1, z.heads):
        attended = jnp.where(lane == h, summed[h * z.req : (h + 1) * z.req], attended)
    return attended.astype(BF16)


def tail_kernel(z, steps, *refs):
    n = z.cores
    count = 4 + 3 * n
    given, gate_hbm, up_hbm, down_hbm = refs[:count], *refs[count : count + 3]
    refs = refs[count + 3 :]
    here_ref, away_refs = refs[0], refs[1:n]
    held, gate_ref, up_ref, down_ref, total_ref, sems = refs[n : n + count], *refs[n + count :]
    units = gate_ref.shape[1] // steps
    pairs = list(zip(given, held))
    for step in range(steps):
        at = slice(step * units, (step + 1) * units)
        pairs += [
            (gate_hbm.at[:, at], gate_ref.at[:, at]),
            (up_hbm.at[:, at], up_ref.at[:, at]),
            (down_hbm.at[at, :], down_ref.at[at, :]),
        ]
    copies = [pltpu.make_async_copy(src, dst, sems.at[i]) for i, (src, dst) in enumerate(pairs)]
    ahead = count + AHEAD
    for copy in copies[:ahead]:
        copy.start()
    for copy in copies[:count]:
        copy.wait()
    back_ref, home_ref, tokens_ref, gain_ref = held[:4]
    stats, values, outs = held[4 : 4 + n], held[4 + n : 4 + 2 * n], held[4 + 2 * n : 4 + 3 * n]
    me = lax.axis_index("head")
    owner = jnp.concatenate([home_ref[:, 0:1], iota((z.req, 1), 0)], axis=0)
    mixed = None
    for i in range(n):
        core = lax.rem(me + i, n)
        choose = message_rows(z, z.back_rows, z.chunks + 1, n, core, transpose=True)
        stacked = dot(choose, back_ref[...]).astype(BF16)
        attended = merged(z, stacked, owner, values[i][...], stats[i][...])
        term = dot(attended, outs[i][...])
        mixed = term if mixed is None else mixed + term
    mixed = (tokens_ref[...].astype(F32) + mixed).astype(BF16).astype(F32)
    hidden_in = normalize(mixed, gain_ref[...]).astype(BF16)
    total = jnp.zeros(mixed.shape, F32)
    for step in range(steps):
        at = slice(step * units, (step + 1) * units)
        for at_copy in range(count + 3 * step, count + 3 * step + 3):
            copies[at_copy].wait()
            if at_copy + AHEAD < len(copies):
                copies[at_copy + AHEAD].start()
        gate = dot(hidden_in, gate_ref[:, at])
        upper = dot(hidden_in, up_ref[:, at])
        hidden = (jax.nn.silu(gate) * upper).astype(BF16)
        total = total + dot(hidden, down_ref[at, :])
    width = mixed.shape[1] // n

    def block(i):
        return pl.ds(pl.multiple_of(lax.rem(me + i, n) * width, width), width)

    total_ref[0] = total
    total_ref[1] = mixed
    here_ref[...] = total_ref[0, :, block(0)] + total_ref[1, :, block(0)]
    for i in range(1, n):
        away_refs[i - 1][...] = total_ref[0, :, block(i)].astype(BF16)


VMEM = pl.BlockSpec(memory_space=pltpu.VMEM)
HBM = pl.BlockSpec(memory_space=pltpu.HBM)


def call(kernel, out, operands, specs, scratch=(), name=None, limit=16):
    return pl.pallas_call(
        kernel,
        out_shape=[jax.ShapeDtypeStruct(s, d) for s, d in out],
        in_specs=specs,
        out_specs=[VMEM] * len(out),
        scratch_shapes=list(scratch),
        compiler_params=pltpu.CompilerParams(vmem_limit_bytes=int(limit * 1024 * 1024)),
        cost_estimate=pl.CostEstimate(flops=10**10, bytes_accessed=10**7, transcendentals=0),
        name=name,
    )(*operands)


def from_core(x, shift):
    n = lax.axis_size("head")
    return lax.ppermute(x, "head", [((i + shift) % n, i) for i in range(n)])


def all_cores(x):
    return [x] + [from_core(x, i) for i in range(1, lax.axis_size("head"))]


def body(
    tokens,
    norm_gain,
    w_query,
    w_key,
    w_value,
    w_out,
    ffn_gain,
    w_gate,
    w_up,
    w_down,
    keys,
    values,
    key_variate,
    query_variate,
    bias,
    lengths,
    order,
    live_blocks,
):
    groups = lax.axis_size("blk")
    head_count = lax.axis_size("head")
    z = Sizes(
        groups,
        head_count,
        tokens.shape[0],
        keys.shape[0],
        keys.shape[0] // live_blocks.shape[0],
        bias.shape[1],
        w_query.shape[1] // bias.shape[1],
    )
    d_model = tokens.shape[1]
    width_local = d_model // head_count
    row = lambda x: x.reshape(1, -1)
    small = (row(lengths), row(order), row(query_variate), row(live_blocks), row(key_variate))
    operands = small + (bias, tokens, row(norm_gain), w_query)
    token = ((8, LANES), F32)
    ask, rows, facts, home = call(
        functools.partial(ask_kernel, z),
        [
            ((groups * z.ask_rows, LANES), BF16),
            ((z.req, z.width + d_model), BF16),
            ((8 + z.slots, z.pool), F32),
            ((z.slots, LANES), I32),
        ],
        operands,
        [HBM] * len(operands),
        scratch=[pltpu.VMEM((2, z.heads), F32)]
        + [pltpu.VMEM(x.shape, x.dtype) for x in small + operands[6:]]
        + [pltpu.SemaphoreType.DMA((len(operands),))],
        name="ask",
        limit=WHOLE,
    )
    asked = lax.all_to_all(ask.reshape(groups, z.ask_rows, LANES), "blk", 0, 0).reshape(ask.shape)
    (held,) = call(hold_kernel, [token], (facts, keys, values), [VMEM] * 3, name="hold")
    back, done = call(
        functools.partial(attend_kernel, z),
        [((groups * head_count * z.back_rows, LANES), BF16), token],
        (asked, keys, values, facts, held),
        [VMEM] * 5,
        name="attend",
    )
    returned = lax.all_to_all(
        back.reshape(groups * head_count, z.back_rows, LANES), ("blk", "head"), 0, 0
    ).reshape(back.shape)
    value_new, own = call(
        functools.partial(own_kernel, z),
        [((z.req, z.width), BF16), ((z.req, LANES), BF16)],
        (done, rows, facts, w_key, w_value),
        [VMEM] * 5,
        name="own",
    )
    w_out_after, _ = lax.optimization_barrier((w_out, held))
    outs = [w_out] + [from_core(w_out_after, i) for i in range(1, head_count)]
    given = (returned, home, tokens, row(ffn_gain), *all_cores(own), *all_cores(value_new), *outs)
    feed = (w_gate, w_up, w_down)
    steps = cdiv(w_gate.shape[1], 512)
    here, *away = call(
        functools.partial(tail_kernel, z, steps),
        [((z.req, width_local), F32)] + [((z.req, width_local), BF16)] * (head_count - 1),
        given + feed,
        [HBM] * (len(given) + 3),
        scratch=[pltpu.VMEM(x.shape, x.dtype) for x in given + feed]
        + [pltpu.VMEM((2, z.req, d_model), F32), pltpu.SemaphoreType.DMA((len(given) + 3 * steps,))],
        name="tail",
        limit=48,
    )
    for i, x in enumerate(away, 1):
        here = here + from_core(x, head_count - i).astype(F32)
    return here.astype(BF16)


def solution(mesh):
    placed = (
        P("blk", None),
        P(),
        P(None, "head"),
        P(None, "head"),
        P(None, "head"),
        P("head", None),
        P(),
        P(None, "head"),
        P(None, "head"),
        P("head", None),
        P("blk", "head"),
        P("blk", "head"),
        P("blk"),
        P(),
        P(None, "head"),
        P(),
        P(),
        P("blk"),
    )
    return jax.shard_map(
        body, mesh=mesh, in_specs=placed, out_specs=P("blk", "head"), check_vma=False
    )
```

time: 54.4 us -> 42.9 us (0.79)
  blocking collectives: 15.6 us -> 0 us
  starting transfers between devices: 3.9 us -> 13 us
  matrix products: 8.15 us -> 0 us
  Pallas kernels: 6.95 us -> 12.7 us
  local copies, waits for them, and re-layouts: 9.33 us -> 5.55 us
  waiting for transfers between devices: 8.92 us -> 10.5 us
    all_to_all x1 -> x0, blocking collectives: 15.6 us -> none  [body(): lax.all_to_all(ask.reshape(groups, z.ask_rows, LANES), 'blk', 0, 0)]
    dot_general x2 -> x0, matrix products: 8.15 us -> none  [dot(): return jnp.dot(a, b, preferred_element_type=F32)]
    all_to_all x1 -> x2, starting transfers between devices: 3.64 us -> 11.7 us  [the longest x1 8.32 us: body(): lax.all_to_all(ask.reshape(groups, z.ask_rows, LANES), 'blk', 0, 0)]
    pallas_call x4 -> x5, Pallas kernels: 6.95 us -> 12.7 us  [call(): pl.pallas_call(kernel, out_shape=[jax.ShapeDtypeStruct(s, d) for s, d in...]
    unnamed x36 -> x24, local copies, waits for them, and re-layouts: 9.31 us -> 5.55 us
    all_to_all x1 -> x2, waiting for transfers between devices: 6.63 us -> 8.71 us  [the longest x1 4.68 us: body(): lax.all_to_all(back.reshape(groups * head_count, z.back_rows, LANES), ('b...]
    ppermute x2 -> x4, starting transfers between devices: 0.26 us -> 1.31 us  [from_core(): return lax.ppermute(x, 'head', [((i + shift) % n, i) for i in range(n)])]
    ppermute x2 -> x4, waiting for transfers between devices: 2.29 us -> 1.78 us  [from_core(): return lax.ppermute(x, 'head', [((i + shift) % n, i) for i in range(n)])]
  transfers between devices with their start and end apart: 3 -> 6, of which waited for: 3 -> 4; matrix products, arithmetic and copies ran while one was open for 0% -> 0% of each run, Pallas kernels for 2% -> 8%
where the time goes in v2:
time: 42.9 us; the launch traced here: 42.4 us
  starting transfers between devices  13 us (30%)
  Pallas kernels  12.7 us (30%)
  waiting for transfers between devices  10.5 us (24%)
  local copies, waits for them, and re-layouts  5.55 us (13%)
  other arithmetic  0.63 us (1%)
    pallas_call x5, Pallas kernels, call(): pl.pallas_call(kernel, out_shape=[jax.ShapeDtypeStruct(s, d) for s, d in...  12.7 us
    all_to_all x1, starting transfers between devices, body(): lax.all_to_all(ask.reshape(groups, z.ask_rows, LANES), 'blk', 0, 0)  8.32 us
    unnamed x24, local copies, waits for them, and re-layouts  5.55 us
    all_to_all x1, waiting for transfers between devices, body(): lax.all_to_all(back.reshape(groups * head_count, z.back_rows, LANES), ('b...  4.68 us
    all_to_all x1, waiting for transfers between devices, body(): lax.all_to_all(ask.reshape(groups, z.ask_rows, LANES), 'blk', 0, 0)  4.02 us
    all_to_all x1, starting transfers between devices, body(): lax.all_to_all(back.reshape(groups * head_count, z.back_rows, LANES), ('b...  3.34 us
    ppermute x4, waiting for transfers between devices, from_core(): return lax.ppermute(x, 'head', [((i + shift) % n, i) for i in range(n)])  1.78 us
    ppermute x4, starting transfers between devices, from_core(): return lax.ppermute(x, 'head', [((i + shift) % n, i) for i in range(n)])  1.31 us
  transfers between devices with their start and end apart: 6, of which 4 were waited for; matrix products, arithmetic and copies ran while one was open for 0% of the time, Pallas kernels for 8%

profile of v2, /device:TPU:0, one launch (start us, length us, event | category | flops | bytes accessed | tf_op | source)
XLA Modules:
  0.0 42.4 jit_solution(12052059043869182825)
XLA Ops:
  0.0 2.8 %ask.1 = (bf16[256,128]{1,0:T(8,128)(2,1)}, bf16[32,1536]{1,0:T(8,128)(2,1)}, f32[72,1024]{1,0:T(8,128)}, s32[64,128]{1,0:T(8,128)}) custom-call(s32[1,512]{1,0:T(1,128)} %bitcast.17, s32[1,512]{1,0:T(1,128)} %bitcast.18, s32[1,512]{1,0:T(1,128)} %bitcast.19, s32[1,16]{1,0:T(1,128)} %bitcast.20, s32[1,1024]{1,0:T(1,128)} %bitcast.15, f32[2,8]{1,0:T(2,128)} %bias_hbm.1, ...), custom_call_target="tpu_custom_call" | custom-call | flops 10000000000 | bytes 10000000 | tf_op jit(solution)/shard_map/ask/pallas_call | solution.py:389
  2.8 8.3 %all-to-all-start = ((bf16[16,16,128]{2,1,0:T(8,128)(2,1)}), bf16[16,16,128]{2,1,0:T(8,128)(2,1)S(1)}, u32[]{:S(2)}, u32[]{:S(2)}) async-start(bf16[16,16,128]{2,1,0:T(8,128)(2,1)} %bitcast.14), calls=%async_computation | async-start | bytes 131072 | tf_op jit(solution)/shard_map/all_to_all | solution.py:463
  11.1 0.0 copy-start
  11.1 1.2 %copy-done = bf16[1024,512]{1,0:T(8,128)(2,1)S(1)} copy-done((bf16[1024,512]{1,0:T(8,128)(2,1)S(1)}, bf16[1024,512]{1,0:T(8,128)(2,1)}, u32[]{:S(2)}) %copy-start) | copy-done | bytes 1048600
  12.3 1.2 %copy-done.2 = bf16[1024,512]{1,0:T(8,128)(2,1)S(1)} copy-done((bf16[1024,512]{1,0:T(8,128)(2,1)S(1)}, bf16[1024,512]{1,0:T(8,128)(2,1)}, u32[]{:S(2)}) %copy-start.2) | copy-done | bytes 1048600
  13.6 1.0 %copy-done.8 = f32[72,1024]{1,0:T(8,128)S(1)} copy-done((f32[72,1024]{1,0:T(8,128)S(1)}, f32[72,1024]{1,0:T(8,128)}, u32[]{:S(2)}) %copy-start.8) | copy-done | bytes 294936
  14.5 0.1 collective-permute-start.2
  14.6 4.0 %all-to-all-done = bf16[16,16,128]{2,1,0:T(8,128)(2,1)S(1)} async-done(((bf16[16,16,128]{2,1,0:T(8,128)(2,1)}), bf16[16,16,128]{2,1,0:T(8,128)(2,1)S(1)}, u32[]{:S(2)}, u32[]{:S(2)}) %all-to-all-start) | async-done | bytes 65568 | tf_op jit(solution)/shard_map/all_to_all | solution.py:463
  18.6 0.0 copy-done.1
  18.6 0.0 copy-done.3
  18.6 0.0 copy-done.9
  18.7 0.0 copy-start.4
  18.7 2.6 %attend.1 = (bf16[768,128]{1,0:T(8,128)(2,1)}, f32[8,128]{1,0:T(8,128)S(1)}) custom-call(bf16[256,128]{1,0:T(8,128)(2,1)S(1)} %bitcast.12, bf16[1024,512]{1,0:T(8,128)(2,1)S(1)} %copy-done.1, bf16[1024,512]{1,0:T(8,128)(2,1)S(1)} %copy-done.3, f32[72,1024]{1,0:T(8,128)S(1)} %copy-done.9, f32[8,128]{1,0:T(8,128)S(1)} %hold.1.after_ref), custom_call_target="tpu_custom_call" | custom-call | flops 10000000000 | bytes 10000000 | tf_op jit(solution)/shard_map/attend/pallas_call | solution.py:389
  21.3 3.3 %all-to-all-start.1 = ((bf16[32,24,128]{2,1,0:T(8,128)(2,1)}), bf16[32,24,128]{2,1,0:T(8,128)(2,1)S(1)}, u32[]{:S(2)}, u32[]{:S(2)}) async-start(bf16[32,24,128]{2,1,0:T(8,128)(2,1)} %bitcast.8), calls=%async_computation.1 | async-start | bytes 393216 | tf_op jit(solution)/shard_map/all_to_all | solution.py:472
  24.7 0.0 copy-done.4
  24.7 0.0 copy-start.5
  24.7 1.2 %copy-done.5 = bf16[1024,512]{1,0:T(8,128)(2,1)S(1)} copy-done((bf16[1024,512]{1,0:T(8,128)(2,1)S(1)}, bf16[1024,512]{1,0:T(8,128)(2,1)}, u32[]{:S(2)}) %copy-start.5) | copy-done | bytes 1048600
  25.9 0.9 %copy-done.10 = bf16[32,1536]{1,0:T(8,128)(2,1)S(1)} copy-done((bf16[32,1536]{1,0:T(8,128)(2,1)S(1)}, bf16[32,1536]{1,0:T(8,128)(2,1)}, u32[]{:S(2)}) %copy-start.10) | copy-done | bytes 98328
  26.8 0.6 %own.1 = (bf16[32,512]{1,0:T(8,128)(2,1)S(1)}, bf16[32,128]{1,0:T(8,128)(2,1)S(1)}) custom-call(f32[8,128]{1,0:T(8,128)S(1)} %get-tuple-element.20.after_ref, bf16[32,1536]{1,0:T(8,128)(2,1)S(1)} %copy-done.10, f32[72,1024]{1,0:T(8,128)S(1)} %copy-done.9, bf16[1024,512]{1,0:T(8,128)(2,1)S(1)} %copy-done.4, bf16[1024,512]{1,0:T(8,128)(2,1)S(1)} %copy-done.5), custom_call_target="tpu_custom_call" | custom-call | flops 10000000000 | bytes 10000000 | tf_op jit(solution)/shard_map/own/pallas_call | solution.py:389
  27.4 0.3 collective-permute-start.1
  27.7 0.3 collective-permute-start
  27.9 0.9 %collective-permute-done.refs_5_ = bf16[32,128]{1,0:T(8,128)(2,1)S(1)} collective-permute-done((bf16[32,128]{1,0:T(8,128)(2,1)S(1)}, bf16[32,128]{1,0:T(8,128)(2,1)S(1)}, u32[]{:S(2)}, u32[]{:S(2)}) %collective-permute-start) | collective-permute-done | bytes 8224 | tf_op jit(solution)/shard_map/ppermute | solution.py:403
  28.9 0.0 collective-permute-done.1.refs_7_
  28.9 4.7 %all-to-all-done.1 = bf16[32,24,128]{2,1,0:T(8,128)(2,1)S(1)} async-done(((bf16[32,24,128]{2,1,0:T(8,128)(2,1)}), bf16[32,24,128]{2,1,0:T(8,128)(2,1)S(1)}, u32[]{:S(2)}, u32[]{:S(2)}) %all-to-all-start.1) | async-done | bytes 196640 | tf_op jit(solution)/shard_map/all_to_all | solution.py:472
  33.5 0.0 collective-permute-done.2.refs_9_
  33.5 0.0 copy-done.6
  33.5 0.0 copy-done.7
  33.6 0.0 copy-done.11
  33.6 6.7 %tail.1 = (f32[32,512]{1,0:T(8,128)S(1)}, bf16[32,512]{1,0:T(8,128)(2,1)S(1)}) custom-call(bf16[768,128]{1,0:T(8,128)(2,1)S(1)} %bitcast.11, s32[64,128]{1,0:T(8,128)S(1)} %copy-done.11, bf16[32,1024]{1,0:T(8,128)(2,1)S(1)} %copy-done.6, f32[1,1024]{1,0:T(1,128)S(1)} %bitcast.13, bf16[32,128]{1,0:T(8,128)(2,1)S(1)} %get-tuple-element.22.refs_4_, ...), custom_call_target="tpu_custom_call" | custom-call | flops 10000000000 | bytes 10000000 | tf_op jit(solution)/shard_map/tail/pallas_call | solution.py:389
  40.3 0.7 %collective-permute-start.3 = (bf16[32,512]{1,0:T(8,128)(2,1)S(1)}, bf16[32,512]{1,0:T(8,128)(2,1)S(1)}, u32[]{:S(2)}, u32[]{:S(2)}) collective-permute-start(bf16[32,512]{1,0:T(8,128)(2,1)S(1)} %get-tuple-element.26), channel_id=1, source_target_pairs={{1,0},{0,1},{3,2},{2,3},{5,4},{4,5},{7,6},{6,7},{9,8},{8,9},{11,10... | collective-permute-start | bytes 98312 | tf_op jit(solution)/shard_map/ppermute | solution.py:403
  41.0 0.9 %collective-permute-done.3 = bf16[32,512]{1,0:T(8,128)(2,1)S(1)} collective-permute-done((bf16[32,512]{1,0:T(8,128)(2,1)S(1)}, bf16[32,512]{1,0:T(8,128)(2,1)S(1)}, u32[]{:S(2)}, u32[]{:S(2)}) %collective-permute-start.3) | collective-permute-done | bytes 32800 | tf_op jit(solution)/shard_map/ppermute | solution.py:403
  41.8 0.6 %add_convert_fusion = bf16[32,512]{1,0:T(8,128)(2,1)} fusion(f32[32,512]{1,0:T(8,128)S(1)} %get-tuple-element.25, bf16[32,512]{1,0:T(8,128)(2,1)S(1)} %collective-permute-done.3), kind=kLoop, calls=%fused_computation | loop fusion | flops 49152 | bytes 131072 | tf_op jit(solution)/shard_map/convert_element_type | solution.py:499
  (10 shorter events, 0.0 us)
Async XLA Ops:
  2.8 15.9 %all-to-all-start = ((bf16[16,16,128]{2,1,0:T(8,128)(2,1)}), bf16[16,16,128]{2,1,0:T(8,128)(2,1)S(1)}, u32[]{:S(2)}, u32[]{:S(2)}) async-start(bf16[16,16,128]{2,1,0:T(8,128)(2,1)} %bitcast.14), calls=%async_computation | async-start | bytes 131072 | tf_op jit(solution)/shard_map/all_to_all | solution.py:463
  11.1 1.2 %copy-start = (bf16[1024,512]{1,0:T(8,128)(2,1)S(1)}, bf16[1024,512]{1,0:T(8,128)(2,1)}, u32[]{:S(2)}) copy-start(bf16[1024,512]{1,0:T(8,128)(2,1)} %keys_ref.1) | copy-start | bytes 3145732
  12.3 1.2 %copy-start.2 = (bf16[1024,512]{1,0:T(8,128)(2,1)S(1)}, bf16[1024,512]{1,0:T(8,128)(2,1)}, u32[]{:S(2)}) copy-start(bf16[1024,512]{1,0:T(8,128)(2,1)} %values_ref.1) | copy-start | bytes 3145732
  13.6 1.0 %copy-start.8 = (f32[72,1024]{1,0:T(8,128)S(1)}, f32[72,1024]{1,0:T(8,128)}, u32[]{:S(2)}) copy-start(f32[72,1024]{1,0:T(8,128)} %get-tuple-element.17.refs_0_.facts_ref) | copy-start | bytes 884740
  14.5 4.1 %copy-start.1 = (bf16[1024,512]{1,0:T(8,128)(2,1)S(1)}, bf16[1024,512]{1,0:T(8,128)(2,1)}, u32[]{:S(2)}) copy-start(bf16[1024,512]{1,0:T(8,128)(2,1)} %keys_ref.1) | copy-start | bytes 3145732
  14.5 4.1 %copy-start.3 = (bf16[1024,512]{1,0:T(8,128)(2,1)S(1)}, bf16[1024,512]{1,0:T(8,128)(2,1)}, u32[]{:S(2)}) copy-start(bf16[1024,512]{1,0:T(8,128)(2,1)} %values_ref.1) | copy-start | bytes 3145732
  14.5 4.1 %copy-start.9 = (f32[72,1024]{1,0:T(8,128)S(1)}, f32[72,1024]{1,0:T(8,128)}, u32[]{:S(2)}) copy-start(f32[72,1024]{1,0:T(8,128)} %get-tuple-element.17.refs_0_.facts_ref) | copy-start | bytes 884740
  14.5 19.0 %collective-permute-start.2 = (bf16[512,1024]{1,0:T(8,128)(2,1)}, bf16[512,1024]{1,0:T(8,128)(2,1)}, u32[]{:S(2)}, u32[]{:S(2)}) collective-permute-start(bf16[512,1024]{1,0:T(8,128)(2,1)} %refs_8_.1), channel_id=1, source_target_pairs={{1,0},{0,1},{3,2},{2,3},{5,4},{4,5},{7,6},{6,7},{9,8},{8,9},{11,10... | collective-permute-start | bytes 3145736 | tf_op jit(solution)/shard_map/ppermute | solution.py:403
  18.7 6.0 %copy-start.4 = (bf16[1024,512]{1,0:T(8,128)(2,1)S(1)}, bf16[1024,512]{1,0:T(8,128)(2,1)}, u32[]{:S(2)}) copy-start(bf16[1024,512]{1,0:T(8,128)(2,1)} %w_key_ref.1) | copy-start | bytes 3145732
  21.3 12.2 %all-to-all-start.1 = ((bf16[32,24,128]{2,1,0:T(8,128)(2,1)}), bf16[32,24,128]{2,1,0:T(8,128)(2,1)S(1)}, u32[]{:S(2)}, u32[]{:S(2)}) async-start(bf16[32,24,128]{2,1,0:T(8,128)(2,1)} %bitcast.8), calls=%async_computation.1 | async-start | bytes 393216 | tf_op jit(solution)/shard_map/all_to_all | solution.py:472
  24.7 1.2 %copy-start.5 = (bf16[1024,512]{1,0:T(8,128)(2,1)S(1)}, bf16[1024,512]{1,0:T(8,128)(2,1)}, u32[]{:S(2)}) copy-start(bf16[1024,512]{1,0:T(8,128)(2,1)} %w_value_ref.1) | copy-start | bytes 3145732
  25.9 0.9 %copy-start.10 = (bf16[32,1536]{1,0:T(8,128)(2,1)S(1)}, bf16[32,1536]{1,0:T(8,128)(2,1)}, u32[]{:S(2)}) copy-start(bf16[32,1536]{1,0:T(8,128)(2,1)} %get-tuple-element.21.rows_ref) | copy-start | bytes 294916
  26.8 6.8 %copy-start.6 = (bf16[32,1024]{1,0:T(8,128)(2,1)S(1)}, bf16[32,1024]{1,0:T(8,128)(2,1)}, u32[]{:S(2)}) copy-start(bf16[32,1024]{1,0:T(8,128)(2,1)} %refs_2_.3) | copy-start | bytes 196612
  26.8 6.8 %copy-start.7 = (f32[1024]{0:T(1024)S(1)}, f32[1024]{0:T(1024)}, u32[]{:S(2)}) copy-start(f32[1024]{0:T(1024)} %param.24) | copy-start | bytes 12292
  26.8 6.8 %copy-start.11 = (s32[64,128]{1,0:T(8,128)S(1)}, s32[64,128]{1,0:T(8,128)}, u32[]{:S(2)}) copy-start(s32[64,128]{1,0:T(8,128)} %get-tuple-element.19.refs_1_) | copy-start | bytes 98308
  27.4 1.5 %collective-permute-start.1 = (bf16[32,512]{1,0:T(8,128)(2,1)S(1)}, bf16[32,512]{1,0:T(8,128)(2,1)S(1)}, u32[]{:S(2)}, u32[]{:S(2)}) collective-permute-start(bf16[32,512]{1,0:T(8,128)(2,1)S(1)} %get-tuple-element.23.refs_6_), channel_id=1, source_target_pairs={{1,0},{0,1},{3,2},{2,3},{5,4},{4,5},{7,6},{6,7},{9,8},{8,9},{11,10... | collective-permute-start | bytes 98312 | tf_op jit(solution)/shard_map/ppermute | solution.py:403
  27.7 1.2 %collective-permute-start = (bf16[32,128]{1,0:T(8,128)(2,1)S(1)}, bf16[32,128]{1,0:T(8,128)(2,1)S(1)}, u32[]{:S(2)}, u32[]{:S(2)}) collective-permute-start(bf16[32,128]{1,0:T(8,128)(2,1)S(1)} %get-tuple-element.22.refs_4_), channel_id=1, source_target_pairs={{1,0},{0,1},{3,2},{2,3},{5,4},{4,5},{7,6},{6,7},{9,8},{8,9},{11,10... | collective-permute-start | bytes 24584 | tf_op jit(solution)/shard_map/ppermute | solution.py:403
  40.3 1.5 %collective-permute-start.3 = (bf16[32,512]{1,0:T(8,128)(2,1)S(1)}, bf16[32,512]{1,0:T(8,128)(2,1)S(1)}, u32[]{:S(2)}, u32[]{:S(2)}) collective-permute-start(bf16[32,512]{1,0:T(8,128)(2,1)S(1)} %get-tuple-element.26), channel_id=1, source_target_pairs={{1,0},{0,1},{3,2},{2,3},{5,4},{4,5},{7,6},{6,7},{9,8},{8,9},{11,10... | collective-permute-start | bytes 98312 | tf_op jit(solution)/shard_map/ppermute | solution.py:403

commit v3 on v2

--- a/solution.py
+++ b/solution.py
@@ -11,7 +11,6 @@
 SHORTEST = 17
 WHOLE = 63
 FLOOR = -1e30
-AHEAD = 12
 F32 = jnp.float32
 BF16 = jnp.bfloat16
 I32 = jnp.int32
@@ -61,23 +60,17 @@
         self.chunks = self.width // LANES
         self.wide = min(self.width, 2 * LANES)
         self.pair = LANES // head_dim
-        self.ask_rows = cdiv(self.chunks * self.slot, 16) * 16
-        self.back_rows = cdiv((self.chunks + 1) * self.slot, 8) * 8
-
-
-def message_rows(z, rows, parts, cores=1, core=None, transpose=False):
-    many, few = z.groups * cores * rows, parts * z.slots
-    at = iota((1, many) if transpose else (many, 1), 1 if transpose else 0)
-    device, inner = split_by(at, rows)
-    group, its_core = split_by(device, cores)
-    part, slot = split_by(inner, z.slot)
-    source = part * z.slots + group * z.slot + slot
-    used = part < parts
-    if core is not None:
-        used = used & (its_core == core)
-    source = jnp.where(used, source, -1)
-    shape = (few, many) if transpose else (many, few)
-    return one_hot(source == iota(shape, 0 if transpose else 1))
+
+
+def deal(z, rows, out_ref, cores=1):
+    for g in range(z.groups):
+        part = rows[g * z.slot : (g + 1) * z.slot].astype(BF16)
+        for core in range(cores):
+            out_ref[g * cores + core] = part
+
+
+def collect(z, ref, cores=1, core=0):
+    return jnp.concatenate([ref[g * cores + core].astype(F32) for g in range(z.groups)], axis=0)
 
 
 def place_rows(lengths, order, variate, step=512):
@@ -178,11 +171,7 @@
     rows_ref[:, z.width :] = normed
     query = dot(normed, w_query_ref[...]).astype(BF16)
     rows_ref[:, : z.width] = query
-    picked = dot(one_hot(row == iota((z.slots, z.req), 1)), query).astype(BF16)
-    stacked = jnp.concatenate(
-        [picked[:, c * LANES : (c + 1) * LANES] for c in range(z.chunks)], axis=0
-    )
-    ask_ref[...] = dot(message_rows(z, z.ask_rows, z.chunks), stacked).astype(BF16)
+    deal(z, dot(one_hot(row == iota((z.slots, z.req), 1)), query), ask_ref)
 
 
 def pieces(z, columns):
@@ -198,7 +187,7 @@
     n = z.heads
     return jnp.where(
         lane < n, high, jnp.where(lane < 2 * n, middle, jnp.where(lane < 3 * n, last, F32(0)))
-    ).astype(BF16)
+    )
 
 
 def hold_kernel(*refs):
@@ -217,31 +206,14 @@
         lane_head = split_by(iota(part.shape, 1), z.dim)[0]
         raw = jnp.sum(jnp.where(lane_head == inner, part, F32(0)), axis=1, keepdims=True)
         columns.append(raw * F32(z.dim**-0.5) + facts_ref[1:2, h : h + 1])
-    stat_ref[...] = pieces(z, columns)
+    stat_ref[...] = pieces(z, columns).astype(BF16)
     value_ref[...] = dot(normed, w_value_ref[...]).astype(BF16)
-
-
-def feed_kernel(steps, tokens_ref, part_ref, other_ref, gain_ref, w_gate_ref, w_up_ref, w_down_ref,
-                mixed_ref, down_ref):
-    mixed = tokens_ref[...].astype(F32) + (part_ref[...].astype(F32) + other_ref[...].astype(F32))
-    mixed = mixed.astype(BF16).astype(F32)
-    hidden_in = normalize(mixed, gain_ref[...]).astype(BF16)
-    units = w_gate_ref.shape[1] // steps
-    total = jnp.zeros(mixed.shape, F32)
-    for step in range(steps):
-        at = slice(step * units, (step + 1) * units)
-        gate = dot(hidden_in, w_gate_ref[:, at])
-        upper = dot(hidden_in, w_up_ref[:, at])
-        hidden = (jax.nn.silu(gate) * upper).astype(BF16)
-        total = total + dot(hidden, w_down_ref[at, :])
-    mixed_ref[...] = mixed.astype(BF16)
-    down_ref[...] = total.astype(BF16)
 
 
 def attend_kernel(z, ask_ref, keys_ref, values_ref, facts_ref, after_ref, back_ref, done_ref):
     del after_ref
     done_ref[...] = jnp.zeros(done_ref.shape, F32)
-    stacked = dot(message_rows(z, z.ask_rows, z.chunks, transpose=True), ask_ref[...])
+    stacked = collect(z, ask_ref)
     begin, finish, kind = facts_ref[8:, 0:1], facts_ref[8:, 1:2], facts_ref[8:, 2:3]
     token = iota((z.slots, z.pool), 1).astype(F32)
     kinds = facts_ref[0:1, :]
@@ -249,17 +221,14 @@
     same = kinds == kind
     lane = split_by(iota((z.slots, z.wide), 1), z.dim)[0]
     many = z.wide // z.dim
-    each = z.wide // LANES
     columns, parts = [], []
     for c in range(z.width // z.wide):
-        asked = jnp.concatenate(
-            [stacked[(c * each + i) * z.slots : (c * each + i + 1) * z.slots] for i in range(each)], axis=1
-        )
+        chunk = slice(c * z.wide, (c + 1) * z.wide)
+        asked = stacked[:, chunk]
         asked = (asked * F32(z.dim**-0.5)).astype(BF16)
         blocks = jnp.concatenate(
             [jnp.where(lane == i, asked, jnp.zeros_like(asked)) for i in range(many)], axis=0
         )
-        chunk = slice(c * z.wide, (c + 1) * z.wide)
         score = lax.dot_general(
             blocks, keys_ref[:, chunk], (((1,), (1,)), ((), ())), preferred_element_type=F32
         )
@@ -281,16 +250,13 @@
         part = summed[: z.slots] * scale[0]
         for i in range(1, many):
             part = jnp.where(lane == i, summed[i * z.slots : (i + 1) * z.slots] * scale[i], part)
-        part = part.astype(BF16)
-        parts += [part[:, i * LANES : (i + 1) * LANES] for i in range(each)]
+        parts.append(part)
     parts.append(pieces(z, columns))
-    back_ref[...] = dot(
-        message_rows(z, z.back_rows, z.chunks + 1, z.cores), jnp.concatenate(parts, axis=0)
-    ).astype(BF16)
+    deal(z, jnp.concatenate(parts, axis=1), back_ref, z.cores)
 
 
 def merged(z, stacked, owner, value, stat):
-    stat = jnp.concatenate([stacked[z.chunks * z.slots :], stat], axis=0)
+    stat = jnp.concatenate([stacked[:, z.width :], stat], axis=0)
     rows = z.slots + z.req
     wide = z.heads * z.req
     head_at, _ = split_by(iota((LANES, wide), 1), z.req)
@@ -305,13 +271,7 @@
     weight = weight / jnp.sum(weight, axis=0, keepdims=True)
     high = weight.astype(BF16)
     low = (weight - high.astype(F32)).astype(BF16)
-    held = jnp.concatenate(
-        [
-            jnp.concatenate([stacked[c * z.slots : (c + 1) * z.slots] for c in range(z.chunks)], axis=1),
-            value,
-        ],
-        axis=0,
-    )
+    held = jnp.concatenate([stacked[:, : z.width], value], axis=0)
     dims = (((0,), (0,)), ((), ()))
     summed = lax.dot_general(high, held, dims, preferred_element_type=F32)
     summed = summed + lax.dot_general(low, held, dims, preferred_element_type=F32)
@@ -329,46 +289,43 @@
     refs = refs[count + 3 :]
     here_ref, away_refs = refs[0], refs[1:n]
     held, gate_ref, up_ref, down_ref, total_ref, sems = refs[n : n + count], *refs[n + count :]
-    units = gate_ref.shape[1] // steps
+    depth, units = gate_ref.shape[0] // steps, down_ref.shape[0] // steps
+    deep = [slice(i * depth, (i + 1) * depth) for i in range(steps)]
+    unit = [slice(i * units, (i + 1) * units) for i in range(steps)]
     pairs = list(zip(given, held))
-    for step in range(steps):
-        at = slice(step * units, (step + 1) * units)
-        pairs += [
-            (gate_hbm.at[:, at], gate_ref.at[:, at]),
-            (up_hbm.at[:, at], up_ref.at[:, at]),
-            (down_hbm.at[at, :], down_ref.at[at, :]),
-        ]
+    for at in deep:
+        pairs += [(gate_hbm.at[at, :], gate_ref.at[at, :]), (up_hbm.at[at, :], up_ref.at[at, :])]
+    pairs += [(down_hbm.at[at, :], down_ref.at[at, :]) for at in unit]
     copies = [pltpu.make_async_copy(src, dst, sems.at[i]) for i, (src, dst) in enumerate(pairs)]
-    ahead = count + AHEAD
-    for copy in copies[:ahead]:
+    for copy in copies:
         copy.start()
-    for copy in copies[:count]:
+    ready = 4 + 2 * n
+    for copy in copies[:ready]:
         copy.wait()
     back_ref, home_ref, tokens_ref, gain_ref = held[:4]
     stats, values, outs = held[4 : 4 + n], held[4 + n : 4 + 2 * n], held[4 + 2 * n : 4 + 3 * n]
     me = lax.axis_index("head")
     owner = jnp.concatenate([home_ref[:, 0:1], iota((z.req, 1), 0)], axis=0)
-    mixed = None
+    attended = []
     for i in range(n):
         core = lax.rem(me + i, n)
-        choose = message_rows(z, z.back_rows, z.chunks + 1, n, core, transpose=True)
-        stacked = dot(choose, back_ref[...]).astype(BF16)
-        attended = merged(z, stacked, owner, values[i][...], stats[i][...])
-        term = dot(attended, outs[i][...])
-        mixed = term if mixed is None else mixed + term
+        stacked = collect(z, back_ref, n, core).astype(BF16)
+        attended.append(merged(z, stacked, owner, values[i][...], stats[i][...]))
+    for copy in copies[ready:count]:
+        copy.wait()
+    mixed = sum(dot(attended[i], outs[i][...]) for i in range(n))
     mixed = (tokens_ref[...].astype(F32) + mixed).astype(BF16).astype(F32)
     hidden_in = normalize(mixed, gain_ref[...]).astype(BF16)
-    total = jnp.zeros(mixed.shape, F32)
-    for step in range(steps):
-        at = slice(step * units, (step + 1) * units)
-        for at_copy in range(count + 3 * step, count + 3 * step + 3):
-            copies[at_copy].wait()
-            if at_copy + AHEAD < len(copies):
-                copies[at_copy + AHEAD].start()
-        gate = dot(hidden_in, gate_ref[:, at])
-        upper = dot(hidden_in, up_ref[:, at])
-        hidden = (jax.nn.silu(gate) * upper).astype(BF16)
-        total = total + dot(hidden, down_ref[at, :])
+    gate = upper = total = 0
+    for i, at in enumerate(deep):
+        for copy in copies[count + 2 * i : count + 2 * i + 2]:
+            copy.wait()
+        gate = gate + dot(hidden_in[:, at], gate_ref[at, :])
+        upper = upper + dot(hidden_in[:, at], up_ref[at, :])
+    hidden = (jax.nn.silu(gate) * upper).astype(BF16)
+    for i, at in enumerate(unit):
+        copies[count + 2 * steps + i].wait()
+        total = total + dot(hidden[:, at], down_ref[at, :])
     width = mixed.shape[1] // n
 
     def block(i):
@@ -447,7 +404,7 @@
     ask, rows, facts, home = call(
         functools.partial(ask_kernel, z),
         [
-            ((groups * z.ask_rows, LANES), BF16),
+            ((groups, z.slot, z.width), BF16),
             ((z.req, z.width + d_model), BF16),
             ((8 + z.slots, z.pool), F32),
             ((z.slots, LANES), I32),
@@ -460,18 +417,16 @@
         name="ask",
         limit=WHOLE,
     )
-    asked = lax.all_to_all(ask.reshape(groups, z.ask_rows, LANES), "blk", 0, 0).reshape(ask.shape)
+    asked = lax.all_to_all(ask, "blk", 0, 0)
     (held,) = call(hold_kernel, [token], (facts, keys, values), [VMEM] * 3, name="hold")
     back, done = call(
         functools.partial(attend_kernel, z),
-        [((groups * head_count * z.back_rows, LANES), BF16), token],
+        [((groups * head_count, z.slot, z.width + LANES), BF16), token],
         (asked, keys, values, facts, held),
         [VMEM] * 5,
         name="attend",
     )
-    returned = lax.all_to_all(
-        back.reshape(groups * head_count, z.back_rows, LANES), ("blk", "head"), 0, 0
-    ).reshape(back.shape)
+    returned = lax.all_to_all(back, ("blk", "head"), 0, 0)
     value_new, own = call(
         functools.partial(own_kernel, z),
         [((z.req, z.width), BF16), ((z.req, LANES), BF16)],
@@ -483,7 +438,7 @@
     outs = [w_out] + [from_core(w_out_after, i) for i in range(1, head_count)]
     given = (returned, home, tokens, row(ffn_gain), *all_cores(own), *all_cores(value_new), *outs)
     feed = (w_gate, w_up, w_down)
-    steps = cdiv(w_gate.shape[1], 512)
+    steps = 8
     here, *away = call(
         functools.partial(tail_kernel, z, steps),
         [((z.req, width_local), F32)] + [((z.req, width_local), BF16)] * (head_count - 1),

time: 42.9 us -> 41.1 us (0.958)
  Pallas kernels: 12.7 us -> 11.5 us
    pallas_call x5, Pallas kernels: 12.7 us -> 11.5 us  [call(): pl.pallas_call(kernel, out_shape=[jax.ShapeDtypeStruct(s, d) for s, d in...]
  transfers between devices with their start and end apart: 6 -> 6, of which waited for: 4 -> 4; matrix products, arithmetic and copies ran while one was open for 0% -> 0% of each run, Pallas kernels for 8% -> 7%
where the time goes in v3:
time: 41.1 us; the launch traced here: 40.7 us
  starting transfers between devices  12.8 us (31%)
  Pallas kernels  11.5 us (28%)
  waiting for transfers between devices  10.2 us (25%)
  local copies, waits for them, and re-layouts  5.55 us (14%)
  other arithmetic  0.63 us (2%)
    pallas_call x5, Pallas kernels, call(): pl.pallas_call(kernel, out_shape=[jax.ShapeDtypeStruct(s, d) for s, d in...  11.5 us
    all_to_all x1, starting transfers between devices, body(): asked = lax.all_to_all(ask, 'blk', 0, 0)  8.32 us
    unnamed x24, local copies, waits for them, and re-layouts  5.55 us
    all_to_all x1, waiting for transfers between devices, body(): returned = lax.all_to_all(back, ('blk', 'head'), 0, 0)  4.37 us
    all_to_all x1, waiting for transfers between devices, body(): asked = lax.all_to_all(ask, 'blk', 0, 0)  4.01 us
    all_to_all x1, starting transfers between devices, body(): returned = lax.all_to_all(back, ('blk', 'head'), 0, 0)  3.35 us
    ppermute x4, waiting for transfers between devices, from_core(): return lax.ppermute(x, 'head', [((i + shift) % n, i) for i in range(n)])  1.78 us
    ppermute x4, starting transfers between devices, from_core(): return lax.ppermute(x, 'head', [((i + shift) % n, i) for i in range(n)])  1.1 us
  transfers between devices with their start and end apart: 6, of which 4 were waited for; matrix products, arithmetic and copies ran while one was open for 0% of the time, Pallas kernels for 7%

profile of v3, /device:TPU:0, one launch (start us, length us, event | category | flops | bytes accessed | tf_op | source)
XLA Modules:
  0.0 40.7 jit_solution(13227990082733801922)
XLA Ops:
  0.0 2.6 %ask.1 = (bf16[16,4,512]{2,1,0:T(4,128)(2,1)}, bf16[32,1536]{1,0:T(8,128)(2,1)}, f32[72,1024]{1,0:T(8,128)}, s32[64,128]{1,0:T(8,128)}) custom-call(s32[1,512]{1,0:T(1,128)} %bitcast.10, s32[1,512]{1,0:T(1,128)} %bitcast.11, s32[1,512]{1,0:T(1,128)} %bitcast.12, s32[1,16]{1,0:T(1,128)} %bitcast.13, s32[1,1024]{1,0:T(1,128)} %bitcast.8, f32[2,8]{1,0:T(2,128)} %bias_hbm.1, ...), custom_call_target="tpu_custom_call" | custom-call | flops 10000000000 | bytes 10000000 | tf_op jit(solution)/shard_map/ask/pallas_call | solution.py:346
  2.6 8.3 %all-to-all-start = ((bf16[16,4,512]{2,1,0:T(4,128)(2,1)}), bf16[16,4,512]{2,1,0:T(4,128)(2,1)S(1)}, u32[]{:S(2)}, u32[]{:S(2)}) async-start(bf16[16,4,512]{2,1,0:T(4,128)(2,1)} %get-tuple-element.16), calls=%async_computation | async-start | bytes 131072 | tf_op jit(solution)/shard_map/all_to_all | solution.py:420
  10.9 0.0 copy-start
  10.9 1.2 %copy-done = bf16[1024,512]{1,0:T(8,128)(2,1)S(1)} copy-done((bf16[1024,512]{1,0:T(8,128)(2,1)S(1)}, bf16[1024,512]{1,0:T(8,128)(2,1)}, u32[]{:S(2)}) %copy-start) | copy-done | bytes 1048600
  12.2 1.2 %copy-done.2 = bf16[1024,512]{1,0:T(8,128)(2,1)S(1)} copy-done((bf16[1024,512]{1,0:T(8,128)(2,1)S(1)}, bf16[1024,512]{1,0:T(8,128)(2,1)}, u32[]{:S(2)}) %copy-start.2) | copy-done | bytes 1048600
  13.4 1.0 %copy-done.8 = f32[72,1024]{1,0:T(8,128)S(1)} copy-done((f32[72,1024]{1,0:T(8,128)S(1)}, f32[72,1024]{1,0:T(8,128)}, u32[]{:S(2)}) %copy-start.8) | copy-done | bytes 294936
  14.4 0.0 copy-start.4
  14.4 0.1 collective-permute-start.2
  14.5 4.0 %all-to-all-done.ask_ref = bf16[16,4,512]{2,1,0:T(4,128)(2,1)S(1)} async-done(((bf16[16,4,512]{2,1,0:T(4,128)(2,1)}), bf16[16,4,512]{2,1,0:T(4,128)(2,1)S(1)}, u32[]{:S(2)}, u32[]{:S(2)}) %all-to-all-start) | async-done | bytes 65568 | tf_op jit(solution)/shard_map/all_to_all | solution.py:420
  18.5 0.0 copy-done.1
  18.5 0.0 copy-done.3
  18.5 0.0 copy-done.9
  18.5 2.2 %attend.1 = (bf16[32,4,640]{2,1,0:T(4,128)(2,1)}, f32[8,128]{1,0:T(8,128)S(1)}) custom-call(bf16[16,4,512]{2,1,0:T(4,128)(2,1)S(1)} %all-to-all-done.ask_ref, bf16[1024,512]{1,0:T(8,128)(2,1)S(1)} %copy-done.1, bf16[1024,512]{1,0:T(8,128)(2,1)S(1)} %copy-done.3, f32[72,1024]{1,0:T(8,128)S(1)} %copy-done.9, f32[8,128]{1,0:T(8,128)S(1)} %hold.1.after_ref), custom_call_target="tpu_custom_call" | custom-call | flops 10000000000 | bytes 10000000 | tf_op jit(solution)/shard_map/attend/pallas_call | solution.py:346
  20.7 3.4 %all-to-all-start.1 = ((bf16[32,4,640]{2,1,0:T(4,128)(2,1)}), bf16[32,4,640]{2,1,0:T(4,128)(2,1)S(1)}, u32[]{:S(2)}, u32[]{:S(2)}) async-start(bf16[32,4,640]{2,1,0:T(4,128)(2,1)} %get-tuple-element.18), calls=%async_computation.1 | async-start | bytes 327680 | tf_op jit(solution)/shard_map/all_to_all | solution.py:429
  24.0 0.0 copy-done.4
  24.0 0.0 copy-start.5
  24.1 1.2 %copy-done.5 = bf16[1024,512]{1,0:T(8,128)(2,1)S(1)} copy-done((bf16[1024,512]{1,0:T(8,128)(2,1)S(1)}, bf16[1024,512]{1,0:T(8,128)(2,1)}, u32[]{:S(2)}) %copy-start.5) | copy-done | bytes 1048600
  25.3 0.9 %copy-done.10 = bf16[32,1536]{1,0:T(8,128)(2,1)S(1)} copy-done((bf16[32,1536]{1,0:T(8,128)(2,1)S(1)}, bf16[32,1536]{1,0:T(8,128)(2,1)}, u32[]{:S(2)}) %copy-start.10) | copy-done | bytes 98328
  26.2 0.6 %own.1 = (bf16[32,512]{1,0:T(8,128)(2,1)S(1)}, bf16[32,128]{1,0:T(8,128)(2,1)S(1)}) custom-call(f32[8,128]{1,0:T(8,128)S(1)} %get-tuple-element.20.after_ref, bf16[32,1536]{1,0:T(8,128)(2,1)S(1)} %copy-done.10, f32[72,1024]{1,0:T(8,128)S(1)} %copy-done.9, bf16[1024,512]{1,0:T(8,128)(2,1)S(1)} %copy-done.4, bf16[1024,512]{1,0:T(8,128)(2,1)S(1)} %copy-done.5), custom_call_target="tpu_custom_call" | custom-call | flops 10000000000 | bytes 10000000 | tf_op jit(solution)/shard_map/own/pallas_call | solution.py:346
  26.7 0.3 collective-permute-start.1
  27.1 0.3 collective-permute-start
  27.3 0.9 %collective-permute-done.refs_5_ = bf16[32,128]{1,0:T(8,128)(2,1)S(1)} collective-permute-done((bf16[32,128]{1,0:T(8,128)(2,1)S(1)}, bf16[32,128]{1,0:T(8,128)(2,1)S(1)}, u32[]{:S(2)}, u32[]{:S(2)}) %collective-permute-start) | collective-permute-done | bytes 8224 | tf_op jit(solution)/shard_map/ppermute | solution.py:360
  28.2 0.0 collective-permute-done.1.refs_7_
  28.2 4.4 %all-to-all-done.1.refs_0_ = bf16[32,4,640]{2,1,0:T(4,128)(2,1)S(1)} async-done(((bf16[32,4,640]{2,1,0:T(4,128)(2,1)}), bf16[32,4,640]{2,1,0:T(4,128)(2,1)S(1)}, u32[]{:S(2)}, u32[]{:S(2)}) %all-to-all-start.1) | async-done | bytes 163872 | tf_op jit(solution)/shard_map/all_to_all | solution.py:429
  32.6 0.0 collective-permute-done.2.refs_9_
  32.6 0.0 copy-done.6
  32.6 0.0 copy-done.7
  32.6 0.0 copy-done.11
  32.6 6.1 %tail.1 = (f32[32,512]{1,0:T(8,128)S(1)}, bf16[32,512]{1,0:T(8,128)(2,1)S(1)}) custom-call(bf16[32,4,640]{2,1,0:T(4,128)(2,1)S(1)} %all-to-all-done.1.refs_0_, s32[64,128]{1,0:T(8,128)S(1)} %copy-done.11, bf16[32,1024]{1,0:T(8,128)(2,1)S(1)} %copy-done.6, f32[1,1024]{1,0:T(1,128)S(1)} %bitcast.7, bf16[32,128]{1,0:T(8,128)(2,1)S(1)} %get-tuple-element.22.refs_4_, ...), custom_call_target="tpu_custom_call" | custom-call | flops 10000000000 | bytes 10000000 | tf_op jit(solution)/shard_map/tail/pallas_call | solution.py:346
  38.8 0.5 %collective-permute-start.3 = (bf16[32,512]{1,0:T(8,128)(2,1)S(1)}, bf16[32,512]{1,0:T(8,128)(2,1)S(1)}, u32[]{:S(2)}, u32[]{:S(2)}) collective-permute-start(bf16[32,512]{1,0:T(8,128)(2,1)S(1)} %get-tuple-element.26), channel_id=1, source_target_pairs={{1,0},{0,1},{3,2},{2,3},{5,4},{4,5},{7,6},{6,7},{9,8},{8,9},{11,10... | collective-permute-start | bytes 98312 | tf_op jit(solution)/shard_map/ppermute | solution.py:360
  39.2 0.9 %collective-permute-done.3 = bf16[32,512]{1,0:T(8,128)(2,1)S(1)} collective-permute-done((bf16[32,512]{1,0:T(8,128)(2,1)S(1)}, bf16[32,512]{1,0:T(8,128)(2,1)S(1)}, u32[]{:S(2)}, u32[]{:S(2)}) %collective-permute-start.3) | collective-permute-done | bytes 32800 | tf_op jit(solution)/shard_map/ppermute | solution.py:360
  40.1 0.6 %add_convert_fusion = bf16[32,512]{1,0:T(8,128)(2,1)} fusion(f32[32,512]{1,0:T(8,128)S(1)} %get-tuple-element.25, bf16[32,512]{1,0:T(8,128)(2,1)S(1)} %collective-permute-done.3), kind=kLoop, calls=%fused_computation | loop fusion | flops 49152 | bytes 131072 | tf_op jit(solution)/shard_map/convert_element_type | solution.py:454
  (10 shorter events, 0.0 us)
Async XLA Ops:
  2.6 15.9 %all-to-all-start = ((bf16[16,4,512]{2,1,0:T(4,128)(2,1)}), bf16[16,4,512]{2,1,0:T(4,128)(2,1)S(1)}, u32[]{:S(2)}, u32[]{:S(2)}) async-start(bf16[16,4,512]{2,1,0:T(4,128)(2,1)} %get-tuple-element.16), calls=%async_computation | async-start | bytes 131072 | tf_op jit(solution)/shard_map/all_to_all | solution.py:420
  10.9 1.2 %copy-start = (bf16[1024,512]{1,0:T(8,128)(2,1)S(1)}, bf16[1024,512]{1,0:T(8,128)(2,1)}, u32[]{:S(2)}) copy-start(bf16[1024,512]{1,0:T(8,128)(2,1)} %keys_ref.1) | copy-start | bytes 3145732
  12.2 1.2 %copy-start.2 = (bf16[1024,512]{1,0:T(8,128)(2,1)S(1)}, bf16[1024,512]{1,0:T(8,128)(2,1)}, u32[]{:S(2)}) copy-start(bf16[1024,512]{1,0:T(8,128)(2,1)} %values_ref.1) | copy-start | bytes 3145732
  13.4 1.0 %copy-start.8 = (f32[72,1024]{1,0:T(8,128)S(1)}, f32[72,1024]{1,0:T(8,128)}, u32[]{:S(2)}) copy-start(f32[72,1024]{1,0:T(8,128)} %get-tuple-element.17.refs_0_.facts_ref) | copy-start | bytes 884740
  14.3 4.1 %copy-start.1 = (bf16[1024,512]{1,0:T(8,128)(2,1)S(1)}, bf16[1024,512]{1,0:T(8,128)(2,1)}, u32[]{:S(2)}) copy-start(bf16[1024,512]{1,0:T(8,128)(2,1)} %keys_ref.1) | copy-start | bytes 3145732
  14.4 4.1 %copy-start.3 = (bf16[1024,512]{1,0:T(8,128)(2,1)S(1)}, bf16[1024,512]{1,0:T(8,128)(2,1)}, u32[]{:S(2)}) copy-start(bf16[1024,512]{1,0:T(8,128)(2,1)} %values_ref.1) | copy-start | bytes 3145732
  14.4 4.1 %copy-start.9 = (f32[72,1024]{1,0:T(8,128)S(1)}, f32[72,1024]{1,0:T(8,128)}, u32[]{:S(2)}) copy-start(f32[72,1024]{1,0:T(8,128)} %get-tuple-element.17.refs_0_.facts_ref) | copy-start | bytes 884740
  14.4 9.7 %copy-start.4 = (bf16[1024,512]{1,0:T(8,128)(2,1)S(1)}, bf16[1024,512]{1,0:T(8,128)(2,1)}, u32[]{:S(2)}) copy-start(bf16[1024,512]{1,0:T(8,128)(2,1)} %w_key_ref.1) | copy-start | bytes 3145732
  14.4 18.2 %collective-permute-start.2 = (bf16[512,1024]{1,0:T(8,128)(2,1)}, bf16[512,1024]{1,0:T(8,128)(2,1)}, u32[]{:S(2)}, u32[]{:S(2)}) collective-permute-start(bf16[512,1024]{1,0:T(8,128)(2,1)} %refs_8_.1), channel_id=1, source_target_pairs={{1,0},{0,1},{3,2},{2,3},{5,4},{4,5},{7,6},{6,7},{9,8},{8,9},{11,10... | collective-permute-start | bytes 3145736 | tf_op jit(solution)/shard_map/ppermute | solution.py:360
  20.7 11.9 %all-to-all-start.1 = ((bf16[32,4,640]{2,1,0:T(4,128)(2,1)}), bf16[32,4,640]{2,1,0:T(4,128)(2,1)S(1)}, u32[]{:S(2)}, u32[]{:S(2)}) async-start(bf16[32,4,640]{2,1,0:T(4,128)(2,1)} %get-tuple-element.18), calls=%async_computation.1 | async-start | bytes 327680 | tf_op jit(solution)/shard_map/all_to_all | solution.py:429
  24.0 1.2 %copy-start.5 = (bf16[1024,512]{1,0:T(8,128)(2,1)S(1)}, bf16[1024,512]{1,0:T(8,128)(2,1)}, u32[]{:S(2)}) copy-start(bf16[1024,512]{1,0:T(8,128)(2,1)} %w_value_ref.1) | copy-start | bytes 3145732
  25.3 0.9 %copy-start.10 = (bf16[32,1536]{1,0:T(8,128)(2,1)S(1)}, bf16[32,1536]{1,0:T(8,128)(2,1)}, u32[]{:S(2)}) copy-start(bf16[32,1536]{1,0:T(8,128)(2,1)} %get-tuple-element.21.rows_ref) | copy-start | bytes 294916
  26.2 6.4 %copy-start.6 = (bf16[32,1024]{1,0:T(8,128)(2,1)S(1)}, bf16[32,1024]{1,0:T(8,128)(2,1)}, u32[]{:S(2)}) copy-start(bf16[32,1024]{1,0:T(8,128)(2,1)} %refs_2_.3) | copy-start | bytes 196612
  26.2 6.4 %copy-start.7 = (f32[1024]{0:T(1024)S(1)}, f32[1024]{0:T(1024)}, u32[]{:S(2)}) copy-start(f32[1024]{0:T(1024)} %param.24) | copy-start | bytes 12292
  26.2 6.5 %copy-start.11 = (s32[64,128]{1,0:T(8,128)S(1)}, s32[64,128]{1,0:T(8,128)}, u32[]{:S(2)}) copy-start(s32[64,128]{1,0:T(8,128)} %get-tuple-element.19.refs_1_) | copy-start | bytes 98308
  26.7 1.5 %collective-permute-start.1 = (bf16[32,512]{1,0:T(8,128)(2,1)S(1)}, bf16[32,512]{1,0:T(8,128)(2,1)S(1)}, u32[]{:S(2)}, u32[]{:S(2)}) collective-permute-start(bf16[32,512]{1,0:T(8,128)(2,1)S(1)} %get-tuple-element.23.refs_6_), channel_id=1, source_target_pairs={{1,0},{0,1},{3,2},{2,3},{5,4},{4,5},{7,6},{6,7},{9,8},{8,9},{11,10... | collective-permute-start | bytes 98312 | tf_op jit(solution)/shard_map/ppermute | solution.py:360
  27.1 1.2 %collective-permute-start = (bf16[32,128]{1,0:T(8,128)(2,1)S(1)}, bf16[32,128]{1,0:T(8,128)(2,1)S(1)}, u32[]{:S(2)}, u32[]{:S(2)}) collective-permute-start(bf16[32,128]{1,0:T(8,128)(2,1)S(1)} %get-tuple-element.22.refs_4_), channel_id=1, source_target_pairs={{1,0},{0,1},{3,2},{2,3},{5,4},{4,5},{7,6},{6,7},{9,8},{8,9},{11,10... | collective-permute-start | bytes 24584 | tf_op jit(solution)/shard_map/ppermute | solution.py:360
  38.8 1.3 %collective-permute-start.3 = (bf16[32,512]{1,0:T(8,128)(2,1)S(1)}, bf16[32,512]{1,0:T(8,128)(2,1)S(1)}, u32[]{:S(2)}, u32[]{:S(2)}) collective-permute-start(bf16[32,512]{1,0:T(8,128)(2,1)S(1)} %get-tuple-element.26), channel_id=1, source_target_pairs={{1,0},{0,1},{3,2},{2,3},{5,4},{4,5},{7,6},{6,7},{9,8},{8,9},{11,10... | collective-permute-start | bytes 98312 | tf_op jit(solution)/shard_map/ppermute | solution.py:360

commit v4 on v3

--- a/solution.py
+++ b/solution.py
@@ -9,8 +9,9 @@
 
 LANES = 128
 SHORTEST = 17
-WHOLE = 63
 FLOOR = -1e30
+STEPS = 4
+DOWN_STEPS = 3
 F32 = jnp.float32
 BF16 = jnp.bfloat16
 I32 = jnp.int32
@@ -190,13 +191,12 @@
     )
 
 
-def hold_kernel(*refs):
-    refs[-1][...] = jnp.zeros(refs[-1].shape, F32)
-
-
-def own_kernel(z, after_ref, rows_ref, facts_ref, w_key_ref, w_value_ref, value_ref, stat_ref):
-    del after_ref
+def first_load_kernel(z, count, facts_ref, rows_ref, *refs):
+    far, w_key_hbm, w_value_hbm = refs[:count], refs[count], refs[count + 1]
+    near, own_ref, w_key_ref, w_value_ref, sems = refs[count + 2 : 2 * count + 2], *refs[2 * count + 2 :]
+    copies = fetch([(w_key_hbm, w_key_ref), (w_value_hbm, w_value_ref), *zip(far, near)], sems)
     normed = rows_ref[:, z.width :]
+    copies[0].wait()
     key_new = dot(normed, w_key_ref[...]).astype(BF16)
     product = rows_ref[:, : z.width].astype(F32) * key_new.astype(F32)
     columns = []
@@ -206,12 +206,24 @@
         lane_head = split_by(iota(part.shape, 1), z.dim)[0]
         raw = jnp.sum(jnp.where(lane_head == inner, part, F32(0)), axis=1, keepdims=True)
         columns.append(raw * F32(z.dim**-0.5) + facts_ref[1:2, h : h + 1])
-    stat_ref[...] = pieces(z, columns).astype(BF16)
-    value_ref[...] = dot(normed, w_value_ref[...]).astype(BF16)
-
-
-def attend_kernel(z, ask_ref, keys_ref, values_ref, facts_ref, after_ref, back_ref, done_ref):
+    own_ref[:, z.width :] = pieces(z, columns).astype(BF16)
+    copies[1].wait()
+    own_ref[:, : z.width] = dot(normed, w_value_ref[...]).astype(BF16)
+    for copy in copies[2:]:
+        copy.wait()
+
+
+def second_load_kernel(count, after_ref, *refs):
     del after_ref
+    down_hbm, down_ref, sems = refs[count], refs[-2], refs[-1]
+    rows = down_ref.shape[0]
+    pairs = list(zip(refs[:count], refs[count + 1 : 2 * count + 1]))
+    pairs.append((down_hbm.at[down_hbm.shape[0] - rows :, :], down_ref))
+    for copy in fetch(pairs, sems):
+        copy.wait()
+
+
+def attend_kernel(z, ask_ref, keys_ref, values_ref, facts_ref, back_ref, done_ref):
     done_ref[...] = jnp.zeros(done_ref.shape, F32)
     stacked = collect(z, ask_ref)
     begin, finish, kind = facts_ref[8:, 0:1], facts_ref[8:, 1:2], facts_ref[8:, 2:3]
@@ -270,11 +282,9 @@
     weight = jnp.where(match, jnp.exp(level - top), F32(0))
     weight = weight / jnp.sum(weight, axis=0, keepdims=True)
     high = weight.astype(BF16)
-    low = (weight - high.astype(F32)).astype(BF16)
     held = jnp.concatenate([stacked[:, : z.width], value], axis=0)
     dims = (((0,), (0,)), ((), ()))
     summed = lax.dot_general(high, held, dims, preferred_element_type=F32)
-    summed = summed + lax.dot_general(low, held, dims, preferred_element_type=F32)
     lane = split_by(iota((z.req, z.width), 1), z.dim)[0]
     attended = summed[: z.req]
     for h in range(1, z.heads):
@@ -284,47 +294,42 @@
 
 def tail_kernel(z, steps, *refs):
     n = z.cores
-    count = 4 + 3 * n
-    given, gate_hbm, up_hbm, down_hbm = refs[:count], *refs[count : count + 3]
-    refs = refs[count + 3 :]
-    here_ref, away_refs = refs[0], refs[1:n]
-    held, gate_ref, up_ref, down_ref, total_ref, sems = refs[n : n + count], *refs[n + count :]
-    depth, units = gate_ref.shape[0] // steps, down_ref.shape[0] // steps
-    deep = [slice(i * depth, (i + 1) * depth) for i in range(steps)]
-    unit = [slice(i * units, (i + 1) * units) for i in range(steps)]
-    pairs = list(zip(given, held))
-    for at in deep:
-        pairs += [(gate_hbm.at[at, :], gate_ref.at[at, :]), (up_hbm.at[at, :], up_ref.at[at, :])]
+    back_ref, home_ref, tokens_ref, gain_ref = refs[:4]
+    owns, outs = refs[4 : 4 + n], refs[4 + n : 4 + 2 * n]
+    kept_ref, gate_hbm, up_hbm, down_hbm, here_ref, *away_refs = refs[4 + 2 * n : 8 + 3 * n]
+    gate_ref, up_ref, down_ref, total_ref, sems = refs[8 + 3 * n :]
+    kept, streamed = kept_ref.shape[0], down_ref.shape[0]
+
+    def cut(rows, count):
+        return [slice(i * (rows // count), (i + 1) * (rows // count)) for i in range(count)]
+
+    deep, unit = cut(gate_ref.shape[0], steps), cut(streamed, DOWN_STEPS)
+    pairs = [(gate_hbm.at[at, :], gate_ref.at[at, :]) for at in deep]
+    pairs += [(up_hbm.at[at, :], up_ref.at[at, :]) for at in deep]
     pairs += [(down_hbm.at[at, :], down_ref.at[at, :]) for at in unit]
-    copies = [pltpu.make_async_copy(src, dst, sems.at[i]) for i, (src, dst) in enumerate(pairs)]
-    for copy in copies:
-        copy.start()
-    ready = 4 + 2 * n
-    for copy in copies[:ready]:
-        copy.wait()
-    back_ref, home_ref, tokens_ref, gain_ref = held[:4]
-    stats, values, outs = held[4 : 4 + n], held[4 + n : 4 + 2 * n], held[4 + 2 * n : 4 + 3 * n]
+    copies = fetch(pairs, sems)
     me = lax.axis_index("head")
     owner = jnp.concatenate([home_ref[:, 0:1], iota((z.req, 1), 0)], axis=0)
     attended = []
     for i in range(n):
         core = lax.rem(me + i, n)
         stacked = collect(z, back_ref, n, core).astype(BF16)
-        attended.append(merged(z, stacked, owner, values[i][...], stats[i][...]))
-    for copy in copies[ready:count]:
-        copy.wait()
+        attended.append(merged(z, stacked, owner, owns[i][:, : z.width], owns[i][:, z.width :]))
     mixed = sum(dot(attended[i], outs[i][...]) for i in range(n))
     mixed = (tokens_ref[...].astype(F32) + mixed).astype(BF16).astype(F32)
     hidden_in = normalize(mixed, gain_ref[...]).astype(BF16)
-    gate = upper = total = 0
+    gate = upper = 0
     for i, at in enumerate(deep):
-        for copy in copies[count + 2 * i : count + 2 * i + 2]:
-            copy.wait()
+        copies[i].wait()
         gate = gate + dot(hidden_in[:, at], gate_ref[at, :])
+    gate = jax.nn.silu(gate)
+    for i, at in enumerate(deep):
+        copies[steps + i].wait()
         upper = upper + dot(hidden_in[:, at], up_ref[at, :])
-    hidden = (jax.nn.silu(gate) * upper).astype(BF16)
+    hidden = (gate * upper).astype(BF16)
+    total = dot(hidden[:, streamed:], kept_ref[...])
     for i, at in enumerate(unit):
-        copies[count + 2 * steps + i].wait()
+        copies[2 * steps + i].wait()
         total = total + dot(hidden[:, at], down_ref[at, :])
     width = mixed.shape[1] // n
 
@@ -342,10 +347,14 @@
 HBM = pl.BlockSpec(memory_space=pltpu.HBM)
 
 
+def in_hbm(*arrays):
+    return tuple(pltpu.with_memory_space_constraint(x, pltpu.HBM) for x in arrays)
+
+
 def call(kernel, out, operands, specs, scratch=(), name=None, limit=16):
     return pl.pallas_call(
         kernel,
-        out_shape=[jax.ShapeDtypeStruct(s, d) for s, d in out],
+        out_shape=out,
         in_specs=specs,
         out_specs=[VMEM] * len(out),
         scratch_shapes=list(scratch),
@@ -400,54 +409,66 @@
     row = lambda x: x.reshape(1, -1)
     small = (row(lengths), row(order), row(query_variate), row(live_blocks), row(key_variate))
     operands = small + (bias, tokens, row(norm_gain), w_query)
-    token = ((8, LANES), F32)
     ask, rows, facts, home = call(
         functools.partial(ask_kernel, z),
         [
-            ((groups, z.slot, z.width), BF16),
-            ((z.req, z.width + d_model), BF16),
-            ((8 + z.slots, z.pool), F32),
-            ((z.slots, LANES), I32),
+            jax.ShapeDtypeStruct((groups, z.slot, z.width), BF16),
+            pltpu.VMEM((z.req, z.width + d_model), BF16),
+            pltpu.VMEM((8 + z.slots, z.pool), F32),
+            pltpu.VMEM((z.slots, LANES), I32),
         ],
-        operands,
+        in_hbm(*operands),
         [HBM] * len(operands),
         scratch=[pltpu.VMEM((2, z.heads), F32)]
         + [pltpu.VMEM(x.shape, x.dtype) for x in small + operands[6:]]
         + [pltpu.SemaphoreType.DMA((len(operands),))],
         name="ask",
-        limit=WHOLE,
     )
     asked = lax.all_to_all(ask, "blk", 0, 0)
-    (held,) = call(hold_kernel, [token], (facts, keys, values), [VMEM] * 3, name="hold")
+    early = (keys, values)
+    keys_near, values_near, own = call(
+        functools.partial(first_load_kernel, z, len(early)),
+        [pltpu.VMEM(x.shape, x.dtype) for x in early] + [pltpu.VMEM((z.req, z.width + LANES), BF16)],
+        (facts, rows) + in_hbm(*early, w_key, w_value),
+        [VMEM] * 2 + [HBM] * (len(early) + 2),
+        scratch=[pltpu.VMEM(x.shape, x.dtype) for x in (w_key, w_value)]
+        + [pltpu.SemaphoreType.DMA((len(early) + 2,))],
+        name="first_load",
+    )
+    w_out_after, _ = lax.optimization_barrier((w_out, own))
+    outs = [w_out] + [from_core(w_out_after, i) for i in range(1, head_count)]
+    owns = all_cores(own)
     back, done = call(
         functools.partial(attend_kernel, z),
-        [((groups * head_count, z.slot, z.width + LANES), BF16), token],
-        (asked, keys, values, facts, held),
-        [VMEM] * 5,
+        [jax.ShapeDtypeStruct((groups * head_count, z.slot, z.width + LANES), BF16), pltpu.VMEM((8, LANES), F32)],
+        (asked, keys_near, values_near, facts),
+        [VMEM] * 4,
         name="attend",
     )
     returned = lax.all_to_all(back, ("blk", "head"), 0, 0)
-    value_new, own = call(
-        functools.partial(own_kernel, z),
-        [((z.req, z.width), BF16), ((z.req, LANES), BF16)],
-        (done, rows, facts, w_key, w_value),
-        [VMEM] * 5,
-        name="own",
-    )
-    w_out_after, _ = lax.optimization_barrier((w_out, held))
-    outs = [w_out] + [from_core(w_out_after, i) for i in range(1, head_count)]
-    given = (returned, home, tokens, row(ffn_gain), *all_cores(own), *all_cores(value_new), *outs)
+    kept = w_down.shape[0] // 4
+    late = (tokens, row(ffn_gain), *outs)
+    tokens_near, gain_near, *outs_near, down_near = call(
+        functools.partial(second_load_kernel, len(late)),
+        [pltpu.VMEM(x.shape, x.dtype) for x in late] + [pltpu.VMEM((kept, d_model), BF16)],
+        (done,) + in_hbm(*late, w_down),
+        [VMEM] + [HBM] * (len(late) + 1),
+        scratch=[pltpu.SemaphoreType.DMA((len(late) + 1,))],
+        name="second_load",
+    )
+    given = (returned, home, tokens_near, gain_near, *owns, *outs_near, down_near)
     feed = (w_gate, w_up, w_down)
-    steps = 8
     here, *away = call(
-        functools.partial(tail_kernel, z, steps),
-        [((z.req, width_local), F32)] + [((z.req, width_local), BF16)] * (head_count - 1),
-        given + feed,
-        [HBM] * (len(given) + 3),
-        scratch=[pltpu.VMEM(x.shape, x.dtype) for x in given + feed]
-        + [pltpu.VMEM((2, z.req, d_model), F32), pltpu.SemaphoreType.DMA((len(given) + 3 * steps,))],
+        functools.partial(tail_kernel, z, STEPS),
+        [pltpu.VMEM((z.req, width_local), F32)]
+        + [pltpu.VMEM((z.req, width_local), BF16)] * (head_count - 1),
+        given + in_hbm(*feed),
+        [VMEM] * len(given) + [HBM] * 3,
+        scratch=[pltpu.VMEM(x.shape, x.dtype) for x in feed[:2]]
+        + [pltpu.VMEM((w_down.shape[0] - kept, d_model), BF16)]
+        + [pltpu.VMEM((2, z.req, d_model), F32), pltpu.SemaphoreType.DMA((2 * STEPS + DOWN_STEPS,))],
         name="tail",
-        limit=48,
+        limit=24,
     )
     for i, x in enumerate(away, 1):
         here = here + from_core(x, head_count - i).astype(F32)

time: 41.1 us -> 39.8 us (0.968)
  local copies, waits for them, and re-layouts: 5.55 us -> 0 us
  Pallas kernels: 11.5 us -> 14.7 us
  waiting for transfers between devices: 10.2 us -> 12.2 us
  starting transfers between devices: 12.8 us -> 11.9 us
    unnamed x24 -> x0, local copies, waits for them, and re-layouts: 5.55 us -> none
    pallas_call x5, Pallas kernels: 11.5 us -> 14.7 us  [call(): pl.pallas_call(kernel, out_shape=out, in_specs=specs, out_specs=[VMEM] *...]
    all_to_all x1, waiting for transfers between devices: 4.37 us -> 6.58 us  [body(): returned = lax.all_to_all(back, ('blk', 'head'), 0, 0)]
    ppermute x4 -> x3, waiting for transfers between devices: 1.78 us -> 0.87 us  [from_core(): return lax.ppermute(x, 'head', [((i + shift) % n, i) for i in range(n)])]
    all_to_all x1, starting transfers between devices: 3.35 us -> 2.58 us  [body(): returned = lax.all_to_all(back, ('blk', 'head'), 0, 0)]
    all_to_all x1, waiting for transfers between devices: 4.01 us -> 4.74 us  [body(): asked = lax.all_to_all(ask, 'blk', 0, 0)]
    ppermute x4 -> x3, starting transfers between devices: 1.1 us -> 1.01 us  [from_core(): return lax.ppermute(x, 'head', [((i + shift) % n, i) for i in range(n)])]
  transfers between devices with their start and end apart: 6 -> 5, of which waited for: 4 -> 3; matrix products, arithmetic and copies ran while one was open for 0% -> 0% of each run, Pallas kernels for 7% -> 16%
where the time goes in v4:
time: 39.8 us; the launch traced here: 39.5 us
  Pallas kernels  14.7 us (37%)
  waiting for transfers between devices  12.2 us (31%)
  starting transfers between devices  11.9 us (30%)
  other arithmetic  0.63 us (2%)
    pallas_call x5, Pallas kernels, call(): pl.pallas_call(kernel, out_shape=out, in_specs=specs, out_specs=[VMEM] *...  14.7 us
    all_to_all x1, starting transfers between devices, body(): asked = lax.all_to_all(ask, 'blk', 0, 0)  8.32 us
    all_to_all x1, waiting for transfers between devices, body(): returned = lax.all_to_all(back, ('blk', 'head'), 0, 0)  6.58 us
    all_to_all x1, waiting for transfers between devices, body(): asked = lax.all_to_all(ask, 'blk', 0, 0)  4.74 us
    all_to_all x1, starting transfers between devices, body(): returned = lax.all_to_all(back, ('blk', 'head'), 0, 0)  2.58 us
    ppermute x3, starting transfers between devices, from_core(): return lax.ppermute(x, 'head', [((i + shift) % n, i) for i in range(n)])  1.01 us
    ppermute x3, waiting for transfers between devices, from_core(): return lax.ppermute(x, 'head', [((i + shift) % n, i) for i in range(n)])  0.87 us
  transfers between devices with their start and end apart: 5, of which 3 were waited for; matrix products, arithmetic and copies ran while one was open for 0% of the time, Pallas kernels for 16%

profile of v4, /device:TPU:0, one launch (start us, length us, event | category | flops | bytes accessed | tf_op | source)
XLA Modules:
  0.0 39.5 jit_solution(17061384204112615279)
XLA Ops:
  0.0 2.6 %ask.1 = (bf16[16,4,512]{2,1,0:T(4,128)(2,1)}, bf16[32,1536]{1,0:T(8,128)(2,1)S(1)}, f32[72,1024]{1,0:T(8,128)S(1)}, s32[64,128]{1,0:T(8,128)S(1)}) custom-call(s32[1,512]{1,0:T(1,128)} %bitcast.10, s32[1,512]{1,0:T(1,128)} %bitcast.11, s32[1,512]{1,0:T(1,128)} %bitcast.12, s32[1,16]{1,0:T(1,128)} %bitcast.13, s32[1,1024]{1,0:T(1,128)} %bitcast.7, ...), custom_call_target="tpu_custom_call" | custom-call | flops 10000000000 | bytes 10000000 | tf_op jit(solution)/shard_map/ask/pallas_call | solution.py:355
  2.6 8.3 %all-to-all-start = ((bf16[16,4,512]{2,1,0:T(4,128)(2,1)}), bf16[16,4,512]{2,1,0:T(4,128)(2,1)S(1)}, u32[]{:S(2)}, u32[]{:S(2)}) async-start(bf16[16,4,512]{2,1,0:T(4,128)(2,1)} %get-tuple-element.22), calls=%async_computation | async-start | bytes 131072 | tf_op jit(solution)/shard_map/all_to_all | solution.py:427
  10.9 2.2 %first_load.1 = (bf16[1024,512]{1,0:T(8,128)(2,1)S(1)}, bf16[1024,512]{1,0:T(8,128)(2,1)S(1)}, bf16[32,640]{1,0:T(8,128)(2,1)S(1)}) custom-call(f32[72,1024]{1,0:T(8,128)S(1)} %get-tuple-element.23.facts_ref, bf16[32,1536]{1,0:T(8,128)(2,1)S(1)} %get-tuple-element.24.rows_ref, bf16[1024,512]{1,0:T(8,128)(2,1)} %refs_0_.2, bf16[1024,512]{1,0:T(8,128)(2,1)} %refs_1_.1, ...), custom_call_target="tpu_custom_call" | custom-call | flops 10000000000 | bytes 10000000 | tf_op jit(solution)/shard_map/first_load/pallas_call | solution.py:355
  13.1 0.1 collective-permute-start
  13.2 0.5 %collective-permute-start.1 = (bf16[32,640]{1,0:T(8,128)(2,1)S(1)}, bf16[32,640]{1,0:T(8,128)(2,1)S(1)}, u32[]{:S(2)}, u32[]{:S(2)}) collective-permute-start(bf16[32,640]{1,0:T(8,128)(2,1)S(1)} %get-tuple-element.30.refs_4_), channel_id=1, source_target_pairs={{1,0},{0,1},{3,2},{2,3},{5,4},{4,5},{7,6},{6,7},{9,8},{8,9},{11,10... | collective-permute-start | bytes 122888 | tf_op jit(solution)/shard_map/ppermute | solution.py:369
  13.7 4.7 %all-to-all-done.ask_ref = bf16[16,4,512]{2,1,0:T(4,128)(2,1)S(1)} async-done(((bf16[16,4,512]{2,1,0:T(4,128)(2,1)}), bf16[16,4,512]{2,1,0:T(4,128)(2,1)S(1)}, u32[]{:S(2)}, u32[]{:S(2)}) %all-to-all-start) | async-done | bytes 65568 | tf_op jit(solution)/shard_map/all_to_all | solution.py:427
  18.5 2.2 %attend.1 = (bf16[32,4,640]{2,1,0:T(4,128)(2,1)}, f32[8,128]{1,0:T(8,128)S(1)}) custom-call(bf16[16,4,512]{2,1,0:T(4,128)(2,1)S(1)} %all-to-all-done.ask_ref, bf16[1024,512]{1,0:T(8,128)(2,1)S(1)} %get-tuple-element.25.keys_ref, bf16[1024,512]{1,0:T(8,128)(2,1)S(1)} %get-tuple-element.26.values_ref, f32[72,1024]{1,0:T(8,128)S(1)} %get-tuple-element.23.facts_ref), custom_call_target="tpu_custom_call" | custom-call | flops 10000000000 | bytes 10000000 | tf_op jit(solution)/shard_map/attend/pallas_call | solution.py:355
  20.6 2.6 %all-to-all-start.1 = ((bf16[32,4,640]{2,1,0:T(4,128)(2,1)}), bf16[32,4,640]{2,1,0:T(4,128)(2,1)S(1)}, u32[]{:S(2)}, u32[]{:S(2)}) async-start(bf16[32,4,640]{2,1,0:T(4,128)(2,1)} %get-tuple-element.27), calls=%async_computation.1 | async-start | bytes 327680 | tf_op jit(solution)/shard_map/all_to_all | solution.py:448
  23.2 0.0 collective-permute-done.refs_3_
  23.2 2.0 %second_load.1 = (bf16[32,1024]{1,0:T(8,128)(2,1)S(1)}, f32[1,1024]{1,0:T(1,128)S(1)}, bf16[512,1024]{1,0:T(8,128)(2,1)S(1)}, bf16[512,1024]{1,0:T(8,128)(2,1)S(1)}, bf16[512,1024]{1,0:T(8,128)(2,1)S(1)}) custom-call(f32[8,128]{1,0:T(8,128)S(1)} %get-tuple-element.29.after_ref, bf16[32,1024]{1,0:T(8,128)(2,1)} %refs_0_.3, f32[1,1024]{1,0:T(1,128)} %bitcast.9, ...), custom_call_target="tpu_custom_call" | custom-call | flops 10000000000 | bytes 10000000 | tf_op jit(solution)/shard_map/second_load/pallas_call | solution.py:355
  25.2 0.0 collective-permute-done.1.refs_5_
  25.2 6.6 %all-to-all-done.1.refs_0_ = bf16[32,4,640]{2,1,0:T(4,128)(2,1)S(1)} async-done(((bf16[32,4,640]{2,1,0:T(4,128)(2,1)}), bf16[32,4,640]{2,1,0:T(4,128)(2,1)S(1)}, u32[]{:S(2)}, u32[]{:S(2)}) %all-to-all-start.1) | async-done | bytes 163872 | tf_op jit(solution)/shard_map/all_to_all | solution.py:448
  31.8 5.8 %tail.1 = (f32[32,512]{1,0:T(8,128)S(1)}, bf16[32,512]{1,0:T(8,128)(2,1)S(1)}) custom-call(bf16[32,4,640]{2,1,0:T(4,128)(2,1)S(1)} %all-to-all-done.1.refs_0_, s32[64,128]{1,0:T(8,128)S(1)} %get-tuple-element.28.refs_1_, bf16[32,1024]{1,0:T(8,128)(2,1)S(1)} %get-tuple-element.32.refs_2_, f32[1,1024]{1,0:T(1,128)S(1)} %get-tuple-element.33.refs_3_, ...), custom_call_target="tpu_custom_call" | custom-call | flops 10000000000 | bytes 10000000 | tf_op jit(solution)/shard_map/tail/pallas_call | solution.py:355
  37.6 0.4 %collective-permute-start.2 = (bf16[32,512]{1,0:T(8,128)(2,1)S(1)}, bf16[32,512]{1,0:T(8,128)(2,1)S(1)}, u32[]{:S(2)}, u32[]{:S(2)}) collective-permute-start(bf16[32,512]{1,0:T(8,128)(2,1)S(1)} %get-tuple-element.38), channel_id=1, source_target_pairs={{1,0},{0,1},{3,2},{2,3},{5,4},{4,5},{7,6},{6,7},{9,8},{8,9},{11,10... | collective-permute-start | bytes 98312 | tf_op jit(solution)/shard_map/ppermute | solution.py:369
  38.1 0.9 %collective-permute-done.2 = bf16[32,512]{1,0:T(8,128)(2,1)S(1)} collective-permute-done((bf16[32,512]{1,0:T(8,128)(2,1)S(1)}, bf16[32,512]{1,0:T(8,128)(2,1)S(1)}, u32[]{:S(2)}, u32[]{:S(2)}) %collective-permute-start.2) | collective-permute-done | bytes 32800 | tf_op jit(solution)/shard_map/ppermute | solution.py:369
  38.9 0.6 %add_convert_fusion = bf16[32,512]{1,0:T(8,128)(2,1)} fusion(f32[32,512]{1,0:T(8,128)S(1)} %get-tuple-element.37, bf16[32,512]{1,0:T(8,128)(2,1)S(1)} %collective-permute-done.2), kind=kLoop, calls=%fused_computation | loop fusion | flops 49152 | bytes 131072 | tf_op jit(solution)/shard_map/convert_element_type | solution.py:475
Async XLA Ops:
  2.6 15.9 %all-to-all-start = ((bf16[16,4,512]{2,1,0:T(4,128)(2,1)}), bf16[16,4,512]{2,1,0:T(4,128)(2,1)S(1)}, u32[]{:S(2)}, u32[]{:S(2)}) async-start(bf16[16,4,512]{2,1,0:T(4,128)(2,1)} %get-tuple-element.22), calls=%async_computation | async-start | bytes 131072 | tf_op jit(solution)/shard_map/all_to_all | solution.py:427
  13.1 10.1 %collective-permute-start = (bf16[512,1024]{1,0:T(8,128)(2,1)}, bf16[512,1024]{1,0:T(8,128)(2,1)}, u32[]{:S(2)}, u32[]{:S(2)}) collective-permute-start(bf16[512,1024]{1,0:T(8,128)(2,1)} %refs_2_.3), channel_id=1, source_target_pairs={{1,0},{0,1},{3,2},{2,3},{5,4},{4,5},{7,6},{6,7},{9,8},{8,9},{11,10... | collective-permute-start | bytes 3145736 | tf_op jit(solution)/shard_map/ppermute | solution.py:369
  13.2 12.0 %collective-permute-start.1 = (bf16[32,640]{1,0:T(8,128)(2,1)S(1)}, bf16[32,640]{1,0:T(8,128)(2,1)S(1)}, u32[]{:S(2)}, u32[]{:S(2)}) collective-permute-start(bf16[32,640]{1,0:T(8,128)(2,1)S(1)} %get-tuple-element.30.refs_4_), channel_id=1, source_target_pairs={{1,0},{0,1},{3,2},{2,3},{5,4},{4,5},{7,6},{6,7},{9,8},{8,9},{11,10... | collective-permute-start | bytes 122888 | tf_op jit(solution)/shard_map/ppermute | solution.py:369
  20.6 11.2 %all-to-all-start.1 = ((bf16[32,4,640]{2,1,0:T(4,128)(2,1)}), bf16[32,4,640]{2,1,0:T(4,128)(2,1)S(1)}, u32[]{:S(2)}, u32[]{:S(2)}) async-start(bf16[32,4,640]{2,1,0:T(4,128)(2,1)} %get-tuple-element.27), calls=%async_computation.1 | async-start | bytes 327680 | tf_op jit(solution)/shard_map/all_to_all | solution.py:448
  37.6 1.3 %collective-permute-start.2 = (bf16[32,512]{1,0:T(8,128)(2,1)S(1)}, bf16[32,512]{1,0:T(8,128)(2,1)S(1)}, u32[]{:S(2)}, u32[]{:S(2)}) collective-permute-start(bf16[32,512]{1,0:T(8,128)(2,1)S(1)} %get-tuple-element.38), channel_id=1, source_target_pairs={{1,0},{0,1},{3,2},{2,3},{5,4},{4,5},{7,6},{6,7},{9,8},{8,9},{11,10... | collective-permute-start | bytes 98312 | tf_op jit(solution)/shard_map/ppermute | solution.py:369

commit v5 on v4

--- a/solution.py
+++ b/solution.py
@@ -11,7 +11,7 @@
 SHORTEST = 17
 FLOOR = -1e30
 STEPS = 4
-DOWN_STEPS = 3
+DOWN_STEPS = 4
 F32 = jnp.float32
 BF16 = jnp.bfloat16
 I32 = jnp.int32
@@ -106,73 +106,78 @@
     return copies
 
 
-def ask_kernel(z, lengths_hbm, order_hbm, variate_hbm, live_hbm, key_variate_hbm, bias_hbm, tokens_hbm,
-               gain_hbm, w_query_hbm, ask_ref, rows_ref, facts_ref, home_ref,
-               bias_ref, lengths_ref, order_ref, variate_ref, live_ref, key_variate_ref, tokens_ref,
-               gain_ref, w_query_ref, sems):
+def choose(z, starts, ends, home_of, turn, home, pool):
+    low = (pool * z.pool).astype(F32)
+    first = jnp.sum(jnp.where(ends <= low, F32(1), F32(0)), axis=1, keepdims=True)
+    first = first + (turn * z.groups).astype(F32)
+    place = iota((z.slots, z.total), 1).astype(F32)
+    return (
+        (home_of == home)
+        & (starts < low + F32(z.pool))
+        & (place >= first)
+        & (place < first + F32(z.groups))
+    )
+
+
+def ask_kernel(z, lengths_hbm, order_hbm, variate_hbm, tokens_hbm, gain_hbm, w_query_hbm, ask_ref, rows_ref,
+               places_ref, home_ref, lengths_ref, order_ref, variate_ref, tokens_ref, gain_ref, w_query_ref,
+               sems):
     me = lax.axis_index("blk")
     copies = fetch(
         [
             (lengths_hbm, lengths_ref),
             (order_hbm, order_ref),
             (variate_hbm, variate_ref),
-            (live_hbm, live_ref),
-            (key_variate_hbm, key_variate_ref),
-            (bias_hbm, bias_ref),
             (tokens_hbm, tokens_ref),
             (gain_hbm, gain_ref),
             (w_query_hbm, w_query_ref),
         ],
         sems,
     )
-    for copy in copies[:6]:
+    for copy in copies[:3]:
         copy.wait()
     order = order_ref[...]
     starts, ends, variates = place_rows(lengths_ref[...], order, variate_ref[...])
-    shape = (z.slots, z.total)
-    place = iota(shape, 1)
+    home_of, local = split_by(order, z.req)
+    places_ref[0:1, :] = starts
+    places_ref[1:2, :] = ends
+    places_ref[2:3, :] = variates
+    places_ref[3:4, :] = home_of.astype(F32)
     other, turn = split_by(iota((z.slots, 1), 0), z.slot)
-    home_of, local = split_by(order, z.req)
-
-    def choose(home, pool):
-        low = (pool * z.pool).astype(F32)
-        first = jnp.sum(jnp.where(ends <= low, F32(1), F32(0)), axis=1, keepdims=True)
-        first = first.astype(I32) + turn * z.groups
-        return (
-            (home_of == home)
-            & (starts < low + F32(z.pool))
-            & (place >= first)
-            & (place < first + z.groups)
-        )
-
-    mine = choose(me, other)
+    mine = choose(z, starts, ends, home_of, turn, me, other)
     row = jnp.sum(jnp.where(mine, local.astype(F32) + 1.0, F32(0)), axis=1, keepdims=True) - 1.0
     row = row.astype(I32)
-    theirs = choose(other, jnp.full((1, 1), me, I32))
-    low = (me * z.pool).astype(F32)
-    begin = jnp.sum(jnp.where(theirs, starts - low, F32(0)), axis=1, keepdims=True)
-    finish = jnp.sum(jnp.where(theirs, ends - low, F32(0)), axis=1, keepdims=True)
-    kind = jnp.sum(jnp.where(theirs, variates, F32(0)), axis=1, keepdims=True)
-    lane = iota((z.slots, LANES), 1)
-    facts = jnp.where(lane == 0, begin, jnp.where(lane == 1, finish, kind))
-    facts_ref[8:, 0:LANES] = facts
     home_ref[...] = jnp.broadcast_to(row, home_ref.shape)
-    blocks = live_ref.shape[1]
-    spread = one_hot(
-        split_by(iota((blocks, z.pool), 1), z.block)[0] == iota((blocks, z.pool), 0)
-    )
-    live = jnp.broadcast_to(live_ref[...].astype(F32).astype(BF16), (16, blocks))
-    kinds = jnp.where(dot(live, spread)[:1] > 0, key_variate_ref[...], -1)
-    facts_ref[0:1, :] = kinds.astype(F32)
-    facts_ref[1:3, 0 : z.heads] = bias_ref[...]
-
-    for copy in copies[6:]:
+
+    for copy in copies[3:]:
         copy.wait()
     normed = normalize(tokens_ref[...].astype(F32), gain_ref[...]).astype(BF16)
     rows_ref[:, z.width :] = normed
     query = dot(normed, w_query_ref[...]).astype(BF16)
     rows_ref[:, : z.width] = query
     deal(z, dot(one_hot(row == iota((z.slots, z.req), 1)), query), ask_ref)
+
+
+def slot_facts(z, places_ref, live, key_variate, bias, facts_ref):
+    me = lax.axis_index("blk")
+    starts, ends, variates = places_ref[0:1, :], places_ref[1:2, :], places_ref[2:3, :]
+    home_of = places_ref[3:4, :].astype(I32)
+    other, turn = split_by(iota((z.slots, 1), 0), z.slot)
+    theirs = choose(z, starts, ends, home_of, turn, other, jnp.full((1, 1), me, I32))
+    low = (me * z.pool).astype(F32)
+    begin = jnp.sum(jnp.where(theirs, starts - low, F32(0)), axis=1, keepdims=True)
+    finish = jnp.sum(jnp.where(theirs, ends - low, F32(0)), axis=1, keepdims=True)
+    kind = jnp.sum(jnp.where(theirs, variates, F32(0)), axis=1, keepdims=True)
+    lane = iota((z.slots, LANES), 1)
+    facts_ref[8:, 0:LANES] = jnp.where(lane == 0, begin, jnp.where(lane == 1, finish, kind))
+    blocks = live.shape[1]
+    spread = one_hot(
+        split_by(iota((blocks, z.pool), 1), z.block)[0] == iota((blocks, z.pool), 0)
+    )
+    live = jnp.broadcast_to(live.astype(F32).astype(BF16), (16, blocks))
+    kinds = jnp.where(dot(live, spread)[:1] > 0, key_variate, -1)
+    facts_ref[0:1, :] = kinds.astype(F32)
+    facts_ref[1:3, 0 : z.heads] = bias
 
 
 def pieces(z, columns):
@@ -191,12 +196,17 @@
     )
 
 
-def first_load_kernel(z, count, facts_ref, rows_ref, *refs):
-    far, w_key_hbm, w_value_hbm = refs[:count], refs[count], refs[count + 1]
-    near, own_ref, w_key_ref, w_value_ref, sems = refs[count + 2 : 2 * count + 2], *refs[2 * count + 2 :]
-    copies = fetch([(w_key_hbm, w_key_ref), (w_value_hbm, w_value_ref), *zip(far, near)], sems)
+def first_load_kernel(z, count, places_ref, rows_ref, *refs):
+    far, small = refs[:count], refs[count : count + 5]
+    near, (facts_ref, own_ref) = refs[count + 5 : 2 * count + 5], refs[2 * count + 5 : 2 * count + 7]
+    held, sems = refs[2 * count + 7 : -1], refs[-1]
+    copies = fetch([*zip(small, held), *zip(far, near)], sems)
+    live_ref, key_variate_ref, bias_ref, w_key_ref, w_value_ref = held
+    for copy in copies[:3]:
+        copy.wait()
+    slot_facts(z, places_ref, live_ref[...], key_variate_ref[...], bias_ref[...], facts_ref)
     normed = rows_ref[:, z.width :]
-    copies[0].wait()
+    copies[3].wait()
     key_new = dot(normed, w_key_ref[...]).astype(BF16)
     product = rows_ref[:, : z.width].astype(F32) * key_new.astype(F32)
     columns = []
@@ -205,21 +215,25 @@
         part = product[:, c * LANES : (c + 1) * LANES]
         lane_head = split_by(iota(part.shape, 1), z.dim)[0]
         raw = jnp.sum(jnp.where(lane_head == inner, part, F32(0)), axis=1, keepdims=True)
-        columns.append(raw * F32(z.dim**-0.5) + facts_ref[1:2, h : h + 1])
+        columns.append(raw * F32(z.dim**-0.5) + bias_ref[0:1, h : h + 1])
     own_ref[:, z.width :] = pieces(z, columns).astype(BF16)
-    copies[1].wait()
+    copies[4].wait()
     own_ref[:, : z.width] = dot(normed, w_value_ref[...]).astype(BF16)
-    for copy in copies[2:]:
+    for copy in copies[5:]:
         copy.wait()
 
 
-def second_load_kernel(count, after_ref, *refs):
+def core_columns(ref, shift, cores):
+    width = ref.shape[-1] // cores
+    core = lax.rem(lax.axis_index("head") + shift, cores)
+    return ref.at[:, pl.ds(pl.multiple_of(core * width, width), width)]
+
+
+def second_load_kernel(z, count, after_ref, *refs):
     del after_ref
-    down_hbm, down_ref, sems = refs[count], refs[-2], refs[-1]
-    rows = down_ref.shape[0]
     pairs = list(zip(refs[:count], refs[count + 1 : 2 * count + 1]))
-    pairs.append((down_hbm.at[down_hbm.shape[0] - rows :, :], down_ref))
-    for copy in fetch(pairs, sems):
+    pairs.append((core_columns(refs[count], 0, z.cores), refs[-2]))
+    for copy in fetch(pairs, refs[-1]):
         copy.wait()
 
 
@@ -292,22 +306,26 @@
     return attended.astype(BF16)
 
 
-def tail_kernel(z, steps, *refs):
+def tail_kernel(z, *refs):
     n = z.cores
     back_ref, home_ref, tokens_ref, gain_ref = refs[:4]
-    owns, outs = refs[4 : 4 + n], refs[4 + n : 4 + 2 * n]
-    kept_ref, gate_hbm, up_hbm, down_hbm, here_ref, *away_refs = refs[4 + 2 * n : 8 + 3 * n]
-    gate_ref, up_ref, down_ref, total_ref, sems = refs[8 + 3 * n :]
-    kept, streamed = kept_ref.shape[0], down_ref.shape[0]
+    owns, out_ref, refs = refs[4 : 4 + n], refs[4 + n], refs[5 + n :]
+    out_hbms, (gate_hbm, up_hbm, down_hbm), refs = refs[: n - 1], refs[n - 1 : n + 2], refs[n + 2 :]
+    hidden_ref, here_ref, away_refs, refs = refs[0], refs[1], refs[2 : n + 1], refs[n + 1 :]
+    out_refs, (gate_ref, up_ref), refs = refs[: n - 1], refs[n - 1 : n + 1], refs[n + 1 :]
+    down_refs, mixed_ref, sems = refs[: n - 1], refs[n - 1], refs[n]
 
     def cut(rows, count):
         return [slice(i * (rows // count), (i + 1) * (rows // count)) for i in range(count)]
 
-    deep, unit = cut(gate_ref.shape[0], steps), cut(streamed, DOWN_STEPS)
-    pairs = [(gate_hbm.at[at, :], gate_ref.at[at, :]) for at in deep]
+    deep, unit = cut(gate_ref.shape[0], STEPS), cut(down_hbm.shape[0], DOWN_STEPS)
+    pairs = list(zip(out_hbms, out_refs))
+    pairs += [(gate_hbm.at[at, :], gate_ref.at[at, :]) for at in deep]
     pairs += [(up_hbm.at[at, :], up_ref.at[at, :]) for at in deep]
-    pairs += [(down_hbm.at[at, :], down_ref.at[at, :]) for at in unit]
-    copies = fetch(pairs, sems)
+    for i in range(1, n):
+        columns = core_columns(down_hbm, i, n)
+        pairs += [(columns.at[at, :], down_refs[i - 1].at[at, :]) for at in unit]
+    copies = iter(fetch(pairs, sems))
     me = lax.axis_index("head")
     owner = jnp.concatenate([home_ref[:, 0:1], iota((z.req, 1), 0)], axis=0)
     attended = []
@@ -315,32 +333,34 @@
         core = lax.rem(me + i, n)
         stacked = collect(z, back_ref, n, core).astype(BF16)
         attended.append(merged(z, stacked, owner, owns[i][:, : z.width], owns[i][:, z.width :]))
-    mixed = sum(dot(attended[i], outs[i][...]) for i in range(n))
+    mixed = dot(attended[0], out_ref[...])
+    for i in range(1, n):
+        next(copies).wait()
+        mixed = mixed + dot(attended[i], out_refs[i - 1][...])
     mixed = (tokens_ref[...].astype(F32) + mixed).astype(BF16).astype(F32)
+    mixed_ref[...] = mixed
+    here_ref[...] = core_columns(mixed_ref, 0, n)[...]
     hidden_in = normalize(mixed, gain_ref[...]).astype(BF16)
     gate = upper = 0
-    for i, at in enumerate(deep):
-        copies[i].wait()
+    for at in deep:
+        next(copies).wait()
         gate = gate + dot(hidden_in[:, at], gate_ref[at, :])
     gate = jax.nn.silu(gate)
-    for i, at in enumerate(deep):
-        copies[steps + i].wait()
+    for at in deep:
+        next(copies).wait()
         upper = upper + dot(hidden_in[:, at], up_ref[at, :])
     hidden = (gate * upper).astype(BF16)
-    total = dot(hidden[:, streamed:], kept_ref[...])
-    for i, at in enumerate(unit):
-        copies[2 * steps + i].wait()
-        total = total + dot(hidden[:, at], down_ref[at, :])
-    width = mixed.shape[1] // n
-
-    def block(i):
-        return pl.ds(pl.multiple_of(lax.rem(me + i, n) * width, width), width)
-
-    total_ref[0] = total
-    total_ref[1] = mixed
-    here_ref[...] = total_ref[0, :, block(0)] + total_ref[1, :, block(0)]
-    for i in range(1, n):
-        away_refs[i - 1][...] = total_ref[0, :, block(i)].astype(BF16)
+    hidden_ref[...] = hidden
+    for away_ref, down_ref in zip(away_refs, down_refs):
+        total = 0
+        for at in unit:
+            next(copies).wait()
+            total = total + dot(hidden[:, at], down_ref[at, :])
+        away_ref[...] = total.astype(BF16)
+
+
+def finish_kernel(hidden_ref, mixed_ref, down_ref, here_ref):
+    here_ref[...] = mixed_ref[...] + dot(hidden_ref[...], down_ref[...])
 
 
 VMEM = pl.BlockSpec(memory_space=pltpu.VMEM)
@@ -407,32 +427,31 @@
     d_model = tokens.shape[1]
     width_local = d_model // head_count
     row = lambda x: x.reshape(1, -1)
-    small = (row(lengths), row(order), row(query_variate), row(live_blocks), row(key_variate))
-    operands = small + (bias, tokens, row(norm_gain), w_query)
-    ask, rows, facts, home = call(
+    operands = (row(lengths), row(order), row(query_variate), tokens, row(norm_gain), w_query)
+    ask, rows, places, home = call(
         functools.partial(ask_kernel, z),
         [
             jax.ShapeDtypeStruct((groups, z.slot, z.width), BF16),
             pltpu.VMEM((z.req, z.width + d_model), BF16),
-            pltpu.VMEM((8 + z.slots, z.pool), F32),
+            pltpu.VMEM((8, z.total), F32),
             pltpu.VMEM((z.slots, LANES), I32),
         ],
         in_hbm(*operands),
         [HBM] * len(operands),
-        scratch=[pltpu.VMEM((2, z.heads), F32)]
-        + [pltpu.VMEM(x.shape, x.dtype) for x in small + operands[6:]]
+        scratch=[pltpu.VMEM(x.shape, x.dtype) for x in operands]
         + [pltpu.SemaphoreType.DMA((len(operands),))],
         name="ask",
     )
     asked = lax.all_to_all(ask, "blk", 0, 0)
-    early = (keys, values)
-    keys_near, values_near, own = call(
+    early, small = (keys, values), (row(live_blocks), row(key_variate), bias, w_key, w_value)
+    keys_near, values_near, facts, own = call(
         functools.partial(first_load_kernel, z, len(early)),
-        [pltpu.VMEM(x.shape, x.dtype) for x in early] + [pltpu.VMEM((z.req, z.width + LANES), BF16)],
-        (facts, rows) + in_hbm(*early, w_key, w_value),
-        [VMEM] * 2 + [HBM] * (len(early) + 2),
-        scratch=[pltpu.VMEM(x.shape, x.dtype) for x in (w_key, w_value)]
-        + [pltpu.SemaphoreType.DMA((len(early) + 2,))],
+        [pltpu.VMEM(x.shape, x.dtype) for x in early]
+        + [pltpu.VMEM((8 + z.slots, z.pool), F32), pltpu.VMEM((z.req, z.width + LANES), BF16)],
+        (places, rows) + in_hbm(*early, *small),
+        [VMEM] * 2 + [HBM] * (len(early) + len(small)),
+        scratch=[pltpu.VMEM(x.shape, x.dtype) for x in small]
+        + [pltpu.SemaphoreType.DMA((len(early) + len(small),))],
         name="first_load",
     )
     w_out_after, _ = lax.optimization_barrier((w_out, own))
@@ -446,32 +465,43 @@
         name="attend",
     )
     returned = lax.all_to_all(back, ("blk", "head"), 0, 0)
-    kept = w_down.shape[0] // 4
-    late = (tokens, row(ffn_gain), *outs)
-    tokens_near, gain_near, *outs_near, down_near = call(
-        functools.partial(second_load_kernel, len(late)),
-        [pltpu.VMEM(x.shape, x.dtype) for x in late] + [pltpu.VMEM((kept, d_model), BF16)],
+    late = (tokens, row(ffn_gain), w_out)
+    units = w_down.shape[0]
+    tokens_near, gain_near, out_near, down_near = call(
+        functools.partial(second_load_kernel, z, len(late)),
+        [pltpu.VMEM(x.shape, x.dtype) for x in late] + [pltpu.VMEM((units, width_local), BF16)],
         (done,) + in_hbm(*late, w_down),
         [VMEM] + [HBM] * (len(late) + 1),
         scratch=[pltpu.SemaphoreType.DMA((len(late) + 1,))],
         name="second_load",
     )
-    given = (returned, home, tokens_near, gain_near, *owns, *outs_near, down_near)
-    feed = (w_gate, w_up, w_down)
-    here, *away = call(
-        functools.partial(tail_kernel, z, STEPS),
-        [pltpu.VMEM((z.req, width_local), F32)]
+    given = (returned, home, tokens_near, gain_near, *owns, out_near)
+    streamed = (*outs[1:], w_gate, w_up)
+    hidden, here, *away = call(
+        functools.partial(tail_kernel, z),
+        [pltpu.VMEM((z.req, units), BF16), pltpu.VMEM((z.req, width_local), F32)]
         + [pltpu.VMEM((z.req, width_local), BF16)] * (head_count - 1),
-        given + in_hbm(*feed),
-        [VMEM] * len(given) + [HBM] * 3,
-        scratch=[pltpu.VMEM(x.shape, x.dtype) for x in feed[:2]]
-        + [pltpu.VMEM((w_down.shape[0] - kept, d_model), BF16)]
-        + [pltpu.VMEM((2, z.req, d_model), F32), pltpu.SemaphoreType.DMA((2 * STEPS + DOWN_STEPS,))],
+        given + in_hbm(*streamed, w_down),
+        [VMEM] * len(given) + [HBM] * (len(streamed) + 1),
+        scratch=[pltpu.VMEM(x.shape, x.dtype) for x in streamed]
+        + [pltpu.VMEM((units, width_local), BF16)] * (head_count - 1)
+        + [
+            pltpu.VMEM((z.req, d_model), F32),
+            pltpu.SemaphoreType.DMA((head_count - 1 + 2 * STEPS + DOWN_STEPS * (head_count - 1),)),
+        ],
         name="tail",
         limit=24,
     )
-    for i, x in enumerate(away, 1):
-        here = here + from_core(x, head_count - i).astype(F32)
+    arrived = [from_core(x, head_count - i) for i, x in enumerate(away, 1)]
+    (here,) = call(
+        finish_kernel,
+        [pltpu.VMEM((z.req, width_local), F32)],
+        (hidden, here, down_near),
+        [VMEM] * 3,
+        name="finish",
+    )
+    for x in arrived:
+        here = here + x.astype(F32)
     return here.astype(BF16)
 
 

time: 39.8 us -> 39.1 us (0.982)
  waiting for transfers between devices: 12.2 us -> 11.6 us
    ppermute x3, waiting for transfers between devices: 0.87 us -> 0.41 us  [from_core(): return lax.ppermute(x, 'head', [((i + shift) % n, i) for i in range(n)])]
    pallas_call x5 -> x6, Pallas kernels: 14.7 us -> 14.5 us  [call(): pl.pallas_call(kernel, out_shape=out, in_specs=specs, out_specs=[VMEM] *...]
  transfers between devices with their start and end apart: 5 -> 5, of which waited for: 3 -> 3; matrix products, arithmetic and copies ran while one was open for 0% -> 0% of each run, Pallas kernels for 16% -> 18%
where the time goes in v5:
time: 39.1 us; the launch traced here: 38.8 us
  Pallas kernels  14.5 us (37%)
  starting transfers between devices  11.9 us (30%)
  waiting for transfers between devices  11.6 us (30%)
  other arithmetic  0.62 us (2%)
    pallas_call x6, Pallas kernels, call(): pl.pallas_call(kernel, out_shape=out, in_specs=specs, out_specs=[VMEM] *...  14.5 us
    all_to_all x1, starting transfers between devices, body(): asked = lax.all_to_all(ask, 'blk', 0, 0)  8.33 us
    all_to_all x1, waiting for transfers between devices, body(): returned = lax.all_to_all(back, ('blk', 'head'), 0, 0)  6.55 us
    all_to_all x1, waiting for transfers between devices, body(): asked = lax.all_to_all(ask, 'blk', 0, 0)  4.66 us
    all_to_all x1, starting transfers between devices, body(): returned = lax.all_to_all(back, ('blk', 'head'), 0, 0)  2.58 us
    ppermute x3, starting transfers between devices, from_core(): return lax.ppermute(x, 'head', [((i + shift) % n, i) for i in range(n)])  1.03 us
  transfers between devices with their start and end apart: 5, of which 3 were waited for; matrix products, arithmetic and copies ran while one was open for 0% of the time, Pallas kernels for 18%

profile of v5, /device:TPU:0, one launch (start us, length us, event | category | flops | bytes accessed | tf_op | source)
XLA Modules:
  0.0 38.8 jit_solution(1872904004426896774)
XLA Ops:
  0.0 2.5 %ask.1 = (bf16[16,4,512]{2,1,0:T(4,128)(2,1)}, bf16[32,1536]{1,0:T(8,128)(2,1)S(1)}, f32[8,512]{1,0:T(8,128)S(1)}, s32[64,128]{1,0:T(8,128)S(1)}) custom-call(s32[1,512]{1,0:T(1,128)} %bitcast.10, s32[1,512]{1,0:T(1,128)} %bitcast.11, s32[1,512]{1,0:T(1,128)} %bitcast.12, bf16[32,1024]{1,0:T(8,128)(2,1)} %refs_0_.3, f32[1,1024]{1,0:T(1,128)} %bitcast.7, ...), custom_call_target="tpu_custom_call" | custom-call | flops 10000000000 | bytes 10000000 | tf_op jit(solution)/shard_map/ask/pallas_call | solution.py:375
  2.5 8.3 %all-to-all-start = ((bf16[16,4,512]{2,1,0:T(4,128)(2,1)}), bf16[16,4,512]{2,1,0:T(4,128)(2,1)S(1)}, u32[]{:S(2)}, u32[]{:S(2)}) async-start(bf16[16,4,512]{2,1,0:T(4,128)(2,1)} %get-tuple-element.23), calls=%async_computation | async-start | bytes 131072 | tf_op jit(solution)/shard_map/all_to_all | solution.py:445
  10.8 2.3 %first_load.1 = (bf16[1024,512]{1,0:T(8,128)(2,1)S(1)}, bf16[1024,512]{1,0:T(8,128)(2,1)S(1)}, f32[72,1024]{1,0:T(8,128)S(1)}, bf16[32,640]{1,0:T(8,128)(2,1)S(1)}) custom-call(f32[8,512]{1,0:T(8,128)S(1)} %get-tuple-element.24.places_ref, bf16[32,1536]{1,0:T(8,128)(2,1)S(1)} %get-tuple-element.25.rows_ref, bf16[1024,512]{1,0:T(8,128)(2,1)} %refs_0_.2, ...), custom_call_target="tpu_custom_call" | custom-call | flops 10000000000 | bytes 10000000 | tf_op jit(solution)/shard_map/first_load/pallas_call | solution.py:375
  13.1 0.1 collective-permute-start
  13.2 0.5 %collective-permute-start.1 = (bf16[512,1024]{1,0:T(8,128)(2,1)}, bf16[512,1024]{1,0:T(8,128)(2,1)}, u32[]{:S(2)}, u32[]{:S(2)}) collective-permute-start(bf16[512,1024]{1,0:T(8,128)(2,1)} %refs_2_.1), channel_id=1, source_target_pairs={{1,0},{0,1},{3,2},{2,3},{5,4},{4,5},{7,6},{6,7},{9,8},{8,9},{11,10... | collective-permute-start | bytes 3145736 | tf_op jit(solution)/shard_map/ppermute | solution.py:389
  13.7 4.7 %all-to-all-done.ask_ref = bf16[16,4,512]{2,1,0:T(4,128)(2,1)S(1)} async-done(((bf16[16,4,512]{2,1,0:T(4,128)(2,1)}), bf16[16,4,512]{2,1,0:T(4,128)(2,1)S(1)}, u32[]{:S(2)}, u32[]{:S(2)}) %all-to-all-start) | async-done | bytes 65568 | tf_op jit(solution)/shard_map/all_to_all | solution.py:445
  18.4 2.2 %attend.1 = (bf16[32,4,640]{2,1,0:T(4,128)(2,1)}, f32[8,128]{1,0:T(8,128)S(1)}) custom-call(bf16[16,4,512]{2,1,0:T(4,128)(2,1)S(1)} %all-to-all-done.ask_ref, bf16[1024,512]{1,0:T(8,128)(2,1)S(1)} %get-tuple-element.26.keys_ref, bf16[1024,512]{1,0:T(8,128)(2,1)S(1)} %get-tuple-element.27.values_ref, f32[72,1024]{1,0:T(8,128)S(1)} %get-tuple-element.28.facts_ref), custom_call_target="tpu_custom_call" | custom-call | flops 10000000000 | bytes 10000000 | tf_op jit(solution)/shard_map/attend/pallas_call | solution.py:375
  20.6 2.6 %all-to-all-start.1 = ((bf16[32,4,640]{2,1,0:T(4,128)(2,1)}), bf16[32,4,640]{2,1,0:T(4,128)(2,1)S(1)}, u32[]{:S(2)}, u32[]{:S(2)}) async-start(bf16[32,4,640]{2,1,0:T(4,128)(2,1)} %get-tuple-element.29), calls=%async_computation.1 | async-start | bytes 327680 | tf_op jit(solution)/shard_map/all_to_all | solution.py:467
  23.1 2.0 %second_load.1 = (bf16[32,1024]{1,0:T(8,128)(2,1)S(1)}, f32[1,1024]{1,0:T(1,128)S(1)}, bf16[512,1024]{1,0:T(8,128)(2,1)S(1)}, bf16[2048,512]{1,0:T(8,128)(2,1)S(1)}) custom-call(f32[8,128]{1,0:T(8,128)S(1)} %get-tuple-element.31.after_ref, bf16[32,1024]{1,0:T(8,128)(2,1)} %refs_0_.3, f32[1,1024]{1,0:T(1,128)} %bitcast.9, bf16[512,1024]{1,0:T(8,128)(2,1)} %refs_2_.1, ...), custom_call_target="tpu_custom_call" | custom-call | flops 10000000000 | bytes 10000000 | tf_op jit(solution)/shard_map/second_load/pallas_call | solution.py:375
  25.2 0.0 collective-permute-done.refs_5_
  25.2 6.6 %all-to-all-done.1.refs_0_ = bf16[32,4,640]{2,1,0:T(4,128)(2,1)S(1)} async-done(((bf16[32,4,640]{2,1,0:T(4,128)(2,1)}), bf16[32,4,640]{2,1,0:T(4,128)(2,1)S(1)}, u32[]{:S(2)}, u32[]{:S(2)}) %all-to-all-start.1) | async-done | bytes 163872 | tf_op jit(solution)/shard_map/all_to_all | solution.py:467
  31.7 0.0 collective-permute-done.1.refs_7_
  31.7 5.1 %tail.1 = (bf16[32,2048]{1,0:T(8,128)(2,1)S(1)}, f32[32,512]{1,0:T(8,128)S(1)}, bf16[32,512]{1,0:T(8,128)(2,1)S(1)}) custom-call(bf16[32,4,640]{2,1,0:T(4,128)(2,1)S(1)} %all-to-all-done.1.refs_0_, s32[64,128]{1,0:T(8,128)S(1)} %get-tuple-element.30.refs_1_, bf16[32,1024]{1,0:T(8,128)(2,1)S(1)} %get-tuple-element.32.refs_2_, ...), custom_call_target="tpu_custom_call" | custom-call | flops 10000000000 | bytes 10000000 | tf_op jit(solution)/shard_map/tail/pallas_call | solution.py:375
  36.8 0.5 %collective-permute-start.2 = (bf16[32,512]{1,0:T(8,128)(2,1)S(1)}, bf16[32,512]{1,0:T(8,128)(2,1)S(1)}, u32[]{:S(2)}, u32[]{:S(2)}) collective-permute-start(bf16[32,512]{1,0:T(8,128)(2,1)S(1)} %get-tuple-element.40), channel_id=1, source_target_pairs={{1,0},{0,1},{3,2},{2,3},{5,4},{4,5},{7,6},{6,7},{9,8},{8,9},{11,10... | collective-permute-start | bytes 98312 | tf_op jit(solution)/shard_map/ppermute | solution.py:389
  37.3 0.5 %finish.1 = f32[32,512]{1,0:T(8,128)S(1)} custom-call(bf16[32,2048]{1,0:T(8,128)(2,1)S(1)} %get-tuple-element.37.hidden_ref, f32[32,512]{1,0:T(8,128)S(1)} %get-tuple-element.38.mixed_ref, bf16[2048,512]{1,0:T(8,128)(2,1)S(1)} %get-tuple-element.39.down_ref), custom_call_target="tpu_custom_call" | custom-call | flops 10000000000 | bytes 10000000 | tf_op jit(solution)/shard_map/finish/pallas_call | solution.py:375
  37.7 0.4 %collective-permute-done.2 = bf16[32,512]{1,0:T(8,128)(2,1)S(1)} collective-permute-done((bf16[32,512]{1,0:T(8,128)(2,1)S(1)}, bf16[32,512]{1,0:T(8,128)(2,1)S(1)}, u32[]{:S(2)}, u32[]{:S(2)}) %collective-permute-start.2) | collective-permute-done | bytes 32800 | tf_op jit(solution)/shard_map/ppermute | solution.py:389
  38.2 0.6 %add_convert_fusion = bf16[32,512]{1,0:T(8,128)(2,1)} fusion(f32[32,512]{1,0:T(8,128)S(1)} %finish.1, bf16[32,512]{1,0:T(8,128)(2,1)S(1)} %collective-permute-done.2), kind=kLoop, calls=%fused_computation | loop fusion | flops 49152 | bytes 131072 | tf_op jit(solution)/shard_map/convert_element_type | solution.py:505
Async XLA Ops:
  2.5 15.9 %all-to-all-start = ((bf16[16,4,512]{2,1,0:T(4,128)(2,1)}), bf16[16,4,512]{2,1,0:T(4,128)(2,1)S(1)}, u32[]{:S(2)}, u32[]{:S(2)}) async-start(bf16[16,4,512]{2,1,0:T(4,128)(2,1)} %get-tuple-element.23), calls=%async_computation | async-start | bytes 131072 | tf_op jit(solution)/shard_map/all_to_all | solution.py:445
  13.1 12.0 %collective-permute-start = (bf16[32,640]{1,0:T(8,128)(2,1)S(1)}, bf16[32,640]{1,0:T(8,128)(2,1)S(1)}, u32[]{:S(2)}, u32[]{:S(2)}) collective-permute-start(bf16[32,640]{1,0:T(8,128)(2,1)S(1)} %get-tuple-element.34.refs_4_), channel_id=1, source_target_pairs={{1,0},{0,1},{3,2},{2,3},{5,4},{4,5},{7,6},{6,7},{9,8},{8,9},{11,10... | collective-permute-start | bytes 122888 | tf_op jit(solution)/shard_map/ppermute | solution.py:389
  13.2 18.5 %collective-permute-start.1 = (bf16[512,1024]{1,0:T(8,128)(2,1)}, bf16[512,1024]{1,0:T(8,128)(2,1)}, u32[]{:S(2)}, u32[]{:S(2)}) collective-permute-start(bf16[512,1024]{1,0:T(8,128)(2,1)} %refs_2_.1), channel_id=1, source_target_pairs={{1,0},{0,1},{3,2},{2,3},{5,4},{4,5},{7,6},{6,7},{9,8},{8,9},{11,10... | collective-permute-start | bytes 3145736 | tf_op jit(solution)/shard_map/ppermute | solution.py:389
  20.6 11.2 %all-to-all-start.1 = ((bf16[32,4,640]{2,1,0:T(4,128)(2,1)}), bf16[32,4,640]{2,1,0:T(4,128)(2,1)S(1)}, u32[]{:S(2)}, u32[]{:S(2)}) async-start(bf16[32,4,640]{2,1,0:T(4,128)(2,1)} %get-tuple-element.29), calls=%async_computation.1 | async-start | bytes 327680 | tf_op jit(solution)/shard_map/all_to_all | solution.py:467
  36.8 1.3 %collective-permute-start.2 = (bf16[32,512]{1,0:T(8,128)(2,1)S(1)}, bf16[32,512]{1,0:T(8,128)(2,1)S(1)}, u32[]{:S(2)}, u32[]{:S(2)}) collective-permute-start(bf16[32,512]{1,0:T(8,128)(2,1)S(1)} %get-tuple-element.40), channel_id=1, source_target_pairs={{1,0},{0,1},{3,2},{2,3},{5,4},{4,5},{7,6},{6,7},{9,8},{8,9},{11,10... | collective-permute-start | bytes 98312 | tf_op jit(solution)/shard_map/ppermute | solution.py:389

commit v6 on v5

--- a/solution.py
+++ b/solution.py
@@ -123,6 +123,7 @@
                places_ref, home_ref, lengths_ref, order_ref, variate_ref, tokens_ref, gain_ref, w_query_ref,
                sems):
     me = lax.axis_index("blk")
+    half = w_query_hbm.shape[0] // 2
     copies = fetch(
         [
             (lengths_hbm, lengths_ref),
@@ -130,7 +131,8 @@
             (variate_hbm, variate_ref),
             (tokens_hbm, tokens_ref),
             (gain_hbm, gain_ref),
-            (w_query_hbm, w_query_ref),
+            (w_query_hbm.at[:half, :], w_query_ref.at[:half, :]),
+            (w_query_hbm.at[half:, :], w_query_ref.at[half:, :]),
         ],
         sems,
     )
@@ -168,16 +170,18 @@
     begin = jnp.sum(jnp.where(theirs, starts - low, F32(0)), axis=1, keepdims=True)
     finish = jnp.sum(jnp.where(theirs, ends - low, F32(0)), axis=1, keepdims=True)
     kind = jnp.sum(jnp.where(theirs, variates, F32(0)), axis=1, keepdims=True)
-    lane = iota((z.slots, LANES), 1)
-    facts_ref[8:, 0:LANES] = jnp.where(lane == 0, begin, jnp.where(lane == 1, finish, kind))
     blocks = live.shape[1]
     spread = one_hot(
         split_by(iota((blocks, z.pool), 1), z.block)[0] == iota((blocks, z.pool), 0)
     )
     live = jnp.broadcast_to(live.astype(F32).astype(BF16), (16, blocks))
     kinds = jnp.where(dot(live, spread)[:1] > 0, key_variate, -1)
-    facts_ref[0:1, :] = kinds.astype(F32)
-    facts_ref[1:3, 0 : z.heads] = bias
+    kinds = kinds.astype(F32)
+    token = iota((z.slots, z.pool), 1).astype(F32)
+    used = (token >= begin) & (token < finish) & (kinds >= 0)
+    facts_ref[: z.slots, :] = jnp.where(kinds == kind, F32(1), F32(0))
+    facts_ref[z.slots : 2 * z.slots, :] = jnp.where(used, F32(0), F32(FLOOR))
+    facts_ref[2 * z.slots : 2 * z.slots + 2, 0 : z.heads] = bias
 
 
 def pieces(z, columns):
@@ -240,11 +244,8 @@
 def attend_kernel(z, ask_ref, keys_ref, values_ref, facts_ref, back_ref, done_ref):
     done_ref[...] = jnp.zeros(done_ref.shape, F32)
     stacked = collect(z, ask_ref)
-    begin, finish, kind = facts_ref[8:, 0:1], facts_ref[8:, 1:2], facts_ref[8:, 2:3]
-    token = iota((z.slots, z.pool), 1).astype(F32)
-    kinds = facts_ref[0:1, :]
-    used = (token >= begin) & (token < finish) & (kinds >= 0)
-    same = kinds == kind
+    same, unused = facts_ref[: z.slots, :], facts_ref[z.slots : 2 * z.slots, :]
+    bias = facts_ref[2 * z.slots : 2 * z.slots + 2, 0 : z.heads]
     lane = split_by(iota((z.slots, z.wide), 1), z.dim)[0]
     many = z.wide // z.dim
     columns, parts = [], []
@@ -262,14 +263,13 @@
         for i in range(many):
             h = c * many + i
             one = score[i * z.slots : (i + 1) * z.slots]
-            one = one + jnp.where(same, facts_ref[1:2, h : h + 1], facts_ref[2:3, h : h + 1])
-            one = jnp.where(used, one, F32(FLOOR))
+            one = one + (same * (bias[0:1, h : h + 1] - bias[1:2, h : h + 1]) + unused)
             top = jnp.maximum(jnp.max(one, axis=1, keepdims=True), F32(FLOOR * 0.1))
             weight = jnp.exp(one - top)
             total = jnp.sum(weight, axis=1, keepdims=True)
             some = total > 0
             safe = jnp.where(some, total, F32(1))
-            columns.append(jnp.where(some, top + jnp.log(safe), F32(FLOOR)))
+            columns.append(jnp.where(some, top + bias[1:2, h : h + 1] + jnp.log(safe), F32(FLOOR)))
             scale.append(1.0 / safe)
             weights.append(weight.astype(BF16))
         summed = dot(jnp.concatenate(weights, axis=0), values_ref[:, chunk])
@@ -439,7 +439,7 @@
         in_hbm(*operands),
         [HBM] * len(operands),
         scratch=[pltpu.VMEM(x.shape, x.dtype) for x in operands]
-        + [pltpu.SemaphoreType.DMA((len(operands),))],
+        + [pltpu.SemaphoreType.DMA((len(operands) + 1,))],
         name="ask",
     )
     asked = lax.all_to_all(ask, "blk", 0, 0)
@@ -447,7 +447,7 @@
     keys_near, values_near, facts, own = call(
         functools.partial(first_load_kernel, z, len(early)),
         [pltpu.VMEM(x.shape, x.dtype) for x in early]
-        + [pltpu.VMEM((8 + z.slots, z.pool), F32), pltpu.VMEM((z.req, z.width + LANES), BF16)],
+        + [pltpu.VMEM((8 + 2 * z.slots, z.pool), F32), pltpu.VMEM((z.req, z.width + LANES), BF16)],
         (places, rows) + in_hbm(*early, *small),
         [VMEM] * 2 + [HBM] * (len(early) + len(small)),
         scratch=[pltpu.VMEM(x.shape, x.dtype) for x in small]

time: 39.1 us -> 38.9 us (level)
  transfers between devices with their start and end apart: 5 -> 5, of which waited for: 3 -> 3; matrix products, arithmetic and copies ran while one was open for 0% -> 0% of each run, Pallas kernels for 18% -> 17%
where the time goes in v6:
time: 38.9 us; the launch traced here: 38.6 us
  Pallas kernels  14.3 us (37%)
  starting transfers between devices  11.9 us (31%)
  waiting for transfers between devices  11.6 us (30%)
  other arithmetic  0.62 us (2%)
    pallas_call x6, Pallas kernels, call(): pl.pallas_call(kernel, out_shape=out, in_specs=specs, out_specs=[VMEM] *...  14.3 us
    all_to_all x1, starting transfers between devices, body(): asked = lax.all_to_all(ask, 'blk', 0, 0)  8.33 us
    all_to_all x1, waiting for transfers between devices, body(): returned = lax.all_to_all(back, ('blk', 'head'), 0, 0)  6.55 us
    all_to_all x1, waiting for transfers between devices, body(): asked = lax.all_to_all(ask, 'blk', 0, 0)  4.66 us
    all_to_all x1, starting transfers between devices, body(): returned = lax.all_to_all(back, ('blk', 'head'), 0, 0)  2.58 us
    ppermute x3, starting transfers between devices, from_core(): return lax.ppermute(x, 'head', [((i + shift) % n, i) for i in range(n)])  1.02 us
  transfers between devices with their start and end apart: 5, of which 3 were waited for; matrix products, arithmetic and copies ran while one was open for 0% of the time, Pallas kernels for 17%

profile of v6, /device:TPU:0, one launch (start us, length us, event | category | flops | bytes accessed | tf_op | source)
XLA Modules:
  0.0 38.6 jit_solution(7300843115485301134)
XLA Ops:
  0.0 2.5 %ask.1 = (bf16[16,4,512]{2,1,0:T(4,128)(2,1)}, bf16[32,1536]{1,0:T(8,128)(2,1)S(1)}, f32[8,512]{1,0:T(8,128)S(1)}, s32[64,128]{1,0:T(8,128)S(1)}) custom-call(s32[1,512]{1,0:T(1,128)} %bitcast.10, s32[1,512]{1,0:T(1,128)} %bitcast.11, s32[1,512]{1,0:T(1,128)} %bitcast.12, bf16[32,1024]{1,0:T(8,128)(2,1)} %refs_0_.3, f32[1,1024]{1,0:T(1,128)} %bitcast.7, ...), custom_call_target="tpu_custom_call" | custom-call | flops 10000000000 | bytes 10000000 | tf_op jit(solution)/shard_map/ask/pallas_call | solution.py:375
  2.5 8.3 %all-to-all-start = ((bf16[16,4,512]{2,1,0:T(4,128)(2,1)}), bf16[16,4,512]{2,1,0:T(4,128)(2,1)S(1)}, u32[]{:S(2)}, u32[]{:S(2)}) async-start(bf16[16,4,512]{2,1,0:T(4,128)(2,1)} %get-tuple-element.23), calls=%async_computation | async-start | bytes 131072 | tf_op jit(solution)/shard_map/all_to_all | solution.py:445
  10.8 2.3 %first_load.1 = (bf16[1024,512]{1,0:T(8,128)(2,1)S(1)}, bf16[1024,512]{1,0:T(8,128)(2,1)S(1)}, f32[136,1024]{1,0:T(8,128)S(1)}, bf16[32,640]{1,0:T(8,128)(2,1)S(1)}) custom-call(f32[8,512]{1,0:T(8,128)S(1)} %get-tuple-element.24.places_ref, bf16[32,1536]{1,0:T(8,128)(2,1)S(1)} %get-tuple-element.25.rows_ref, bf16[1024,512]{1,0:T(8,128)(2,1)} %refs_0_.2, ...), custom_call_target="tpu_custom_call" | custom-call | flops 10000000000 | bytes 10000000 | tf_op jit(solution)/shard_map/first_load/pallas_call | solution.py:375
  13.1 0.1 collective-permute-start
  13.2 0.5 %collective-permute-start.1 = (bf16[512,1024]{1,0:T(8,128)(2,1)}, bf16[512,1024]{1,0:T(8,128)(2,1)}, u32[]{:S(2)}, u32[]{:S(2)}) collective-permute-start(bf16[512,1024]{1,0:T(8,128)(2,1)} %refs_2_.1), channel_id=1, source_target_pairs={{1,0},{0,1},{3,2},{2,3},{5,4},{4,5},{7,6},{6,7},{9,8},{8,9},{11,10... | collective-permute-start | bytes 3145736 | tf_op jit(solution)/shard_map/ppermute | solution.py:389
  13.7 4.7 %all-to-all-done.ask_ref = bf16[16,4,512]{2,1,0:T(4,128)(2,1)S(1)} async-done(((bf16[16,4,512]{2,1,0:T(4,128)(2,1)}), bf16[16,4,512]{2,1,0:T(4,128)(2,1)S(1)}, u32[]{:S(2)}, u32[]{:S(2)}) %all-to-all-start) | async-done | bytes 65568 | tf_op jit(solution)/shard_map/all_to_all | solution.py:445
  18.4 2.0 %attend.1 = (bf16[32,4,640]{2,1,0:T(4,128)(2,1)}, f32[8,128]{1,0:T(8,128)S(1)}) custom-call(bf16[16,4,512]{2,1,0:T(4,128)(2,1)S(1)} %all-to-all-done.ask_ref, bf16[1024,512]{1,0:T(8,128)(2,1)S(1)} %get-tuple-element.26.keys_ref, bf16[1024,512]{1,0:T(8,128)(2,1)S(1)} %get-tuple-element.27.values_ref, f32[136,1024]{1,0:T(8,128)S(1)} %get-tuple-element.28.facts_ref), custom_call_target="tpu_custom_call" | custom-call | flops 10000000000 | bytes 10000000 | tf_op jit(solution)/shard_map/attend/pallas_call | solution.py:375
  20.4 2.6 %all-to-all-start.1 = ((bf16[32,4,640]{2,1,0:T(4,128)(2,1)}), bf16[32,4,640]{2,1,0:T(4,128)(2,1)S(1)}, u32[]{:S(2)}, u32[]{:S(2)}) async-start(bf16[32,4,640]{2,1,0:T(4,128)(2,1)} %get-tuple-element.29), calls=%async_computation.1 | async-start | bytes 327680 | tf_op jit(solution)/shard_map/all_to_all | solution.py:467
  23.0 2.0 %second_load.1 = (bf16[32,1024]{1,0:T(8,128)(2,1)S(1)}, f32[1,1024]{1,0:T(1,128)S(1)}, bf16[512,1024]{1,0:T(8,128)(2,1)S(1)}, bf16[2048,512]{1,0:T(8,128)(2,1)S(1)}) custom-call(f32[8,128]{1,0:T(8,128)S(1)} %get-tuple-element.31.after_ref, bf16[32,1024]{1,0:T(8,128)(2,1)} %refs_0_.3, f32[1,1024]{1,0:T(1,128)} %bitcast.9, bf16[512,1024]{1,0:T(8,128)(2,1)} %refs_2_.1, ...), custom_call_target="tpu_custom_call" | custom-call | flops 10000000000 | bytes 10000000 | tf_op jit(solution)/shard_map/second_load/pallas_call | solution.py:375
  25.0 0.0 collective-permute-done.refs_5_
  25.0 6.6 %all-to-all-done.1.refs_0_ = bf16[32,4,640]{2,1,0:T(4,128)(2,1)S(1)} async-done(((bf16[32,4,640]{2,1,0:T(4,128)(2,1)}), bf16[32,4,640]{2,1,0:T(4,128)(2,1)S(1)}, u32[]{:S(2)}, u32[]{:S(2)}) %all-to-all-start.1) | async-done | bytes 163872 | tf_op jit(solution)/shard_map/all_to_all | solution.py:467
  31.5 0.0 collective-permute-done.1.refs_7_
  31.5 5.1 %tail.1 = (bf16[32,2048]{1,0:T(8,128)(2,1)S(1)}, f32[32,512]{1,0:T(8,128)S(1)}, bf16[32,512]{1,0:T(8,128)(2,1)S(1)}) custom-call(bf16[32,4,640]{2,1,0:T(4,128)(2,1)S(1)} %all-to-all-done.1.refs_0_, s32[64,128]{1,0:T(8,128)S(1)} %get-tuple-element.30.refs_1_, bf16[32,1024]{1,0:T(8,128)(2,1)S(1)} %get-tuple-element.32.refs_2_, ...), custom_call_target="tpu_custom_call" | custom-call | flops 10000000000 | bytes 10000000 | tf_op jit(solution)/shard_map/tail/pallas_call | solution.py:375
  36.6 0.4 %collective-permute-start.2 = (bf16[32,512]{1,0:T(8,128)(2,1)S(1)}, bf16[32,512]{1,0:T(8,128)(2,1)S(1)}, u32[]{:S(2)}, u32[]{:S(2)}) collective-permute-start(bf16[32,512]{1,0:T(8,128)(2,1)S(1)} %get-tuple-element.40), channel_id=1, source_target_pairs={{1,0},{0,1},{3,2},{2,3},{5,4},{4,5},{7,6},{6,7},{9,8},{8,9},{11,10... | collective-permute-start | bytes 98312 | tf_op jit(solution)/shard_map/ppermute | solution.py:389
  37.1 0.5 %finish.1 = f32[32,512]{1,0:T(8,128)S(1)} custom-call(bf16[32,2048]{1,0:T(8,128)(2,1)S(1)} %get-tuple-element.37.hidden_ref, f32[32,512]{1,0:T(8,128)S(1)} %get-tuple-element.38.mixed_ref, bf16[2048,512]{1,0:T(8,128)(2,1)S(1)} %get-tuple-element.39.down_ref), custom_call_target="tpu_custom_call" | custom-call | flops 10000000000 | bytes 10000000 | tf_op jit(solution)/shard_map/finish/pallas_call | solution.py:375
  37.5 0.4 %collective-permute-done.2 = bf16[32,512]{1,0:T(8,128)(2,1)S(1)} collective-permute-done((bf16[32,512]{1,0:T(8,128)(2,1)S(1)}, bf16[32,512]{1,0:T(8,128)(2,1)S(1)}, u32[]{:S(2)}, u32[]{:S(2)}) %collective-permute-start.2) | collective-permute-done | bytes 32800 | tf_op jit(solution)/shard_map/ppermute | solution.py:389
  38.0 0.6 %add_convert_fusion = bf16[32,512]{1,0:T(8,128)(2,1)} fusion(f32[32,512]{1,0:T(8,128)S(1)} %finish.1, bf16[32,512]{1,0:T(8,128)(2,1)S(1)} %collective-permute-done.2), kind=kLoop, calls=%fused_computation | loop fusion | flops 49152 | bytes 131072 | tf_op jit(solution)/shard_map/convert_element_type | solution.py:505
Async XLA Ops:
  2.5 15.9 %all-to-all-start = ((bf16[16,4,512]{2,1,0:T(4,128)(2,1)}), bf16[16,4,512]{2,1,0:T(4,128)(2,1)S(1)}, u32[]{:S(2)}, u32[]{:S(2)}) async-start(bf16[16,4,512]{2,1,0:T(4,128)(2,1)} %get-tuple-element.23), calls=%async_computation | async-start | bytes 131072 | tf_op jit(solution)/shard_map/all_to_all | solution.py:445
  13.1 11.8 %collective-permute-start = (bf16[32,640]{1,0:T(8,128)(2,1)S(1)}, bf16[32,640]{1,0:T(8,128)(2,1)S(1)}, u32[]{:S(2)}, u32[]{:S(2)}) collective-permute-start(bf16[32,640]{1,0:T(8,128)(2,1)S(1)} %get-tuple-element.34.refs_4_), channel_id=1, source_target_pairs={{1,0},{0,1},{3,2},{2,3},{5,4},{4,5},{7,6},{6,7},{9,8},{8,9},{11,10... | collective-permute-start | bytes 122888 | tf_op jit(solution)/shard_map/ppermute | solution.py:389
  13.2 18.3 %collective-permute-start.1 = (bf16[512,1024]{1,0:T(8,128)(2,1)}, bf16[512,1024]{1,0:T(8,128)(2,1)}, u32[]{:S(2)}, u32[]{:S(2)}) collective-permute-start(bf16[512,1024]{1,0:T(8,128)(2,1)} %refs_2_.1), channel_id=1, source_target_pairs={{1,0},{0,1},{3,2},{2,3},{5,4},{4,5},{7,6},{6,7},{9,8},{8,9},{11,10... | collective-permute-start | bytes 3145736 | tf_op jit(solution)/shard_map/ppermute | solution.py:389
  20.4 11.2 %all-to-all-start.1 = ((bf16[32,4,640]{2,1,0:T(4,128)(2,1)}), bf16[32,4,640]{2,1,0:T(4,128)(2,1)S(1)}, u32[]{:S(2)}, u32[]{:S(2)}) async-start(bf16[32,4,640]{2,1,0:T(4,128)(2,1)} %get-tuple-element.29), calls=%async_computation.1 | async-start | bytes 327680 | tf_op jit(solution)/shard_map/all_to_all | solution.py:467
  36.6 1.3 %collective-permute-start.2 = (bf16[32,512]{1,0:T(8,128)(2,1)S(1)}, bf16[32,512]{1,0:T(8,128)(2,1)S(1)}, u32[]{:S(2)}, u32[]{:S(2)}) collective-permute-start(bf16[32,512]{1,0:T(8,128)(2,1)S(1)} %get-tuple-element.40), channel_id=1, source_target_pairs={{1,0},{0,1},{3,2},{2,3},{5,4},{4,5},{7,6},{6,7},{9,8},{8,9},{11,10... | collective-permute-start | bytes 98312 | tf_op jit(solution)/shard_map/ppermute | solution.py:389

commit v7 on v6

--- a/solution.py
+++ b/solution.py
@@ -74,14 +74,14 @@
     return jnp.concatenate([ref[g * cores + core].astype(F32) for g in range(z.groups)], axis=0)
 
 
-def place_rows(lengths, order, variate, step=512):
+def place_rows(lengths, order, step=512):
     total = order.shape[1]
     step = min(step, total)
     sub = iota((16, total), 0)
     table = jnp.where(
         sub == 0,
         lax.shift_right_logical(lengths, 6),
-        jnp.where(sub == 1, lengths & 63, jnp.where(sub == 2, variate, 0)),
+        jnp.where(sub == 1, lengths & 63, 0),
     )
     table = table.astype(F32).astype(BF16)
     request = iota((total, step), 0)
@@ -96,7 +96,7 @@
     summed = jnp.concatenate(sums, axis=1) if len(sums) > 1 else sums[0]
     ends = summed[0:1] * 64.0 + summed[1:2]
     starts = ends - (ordered[0:1] * 64.0 + ordered[1:2])
-    return starts, ends, ordered[2:3]
+    return starts, ends
 
 
 def fetch(pairs, sems):
@@ -119,8 +119,8 @@
     )
 
 
-def ask_kernel(z, lengths_hbm, order_hbm, variate_hbm, tokens_hbm, gain_hbm, w_query_hbm, ask_ref, rows_ref,
-               places_ref, home_ref, lengths_ref, order_ref, variate_ref, tokens_ref, gain_ref, w_query_ref,
+def ask_kernel(z, lengths_hbm, order_hbm, tokens_hbm, gain_hbm, w_query_hbm, ask_ref, rows_ref,
+               places_ref, home_ref, lengths_ref, order_ref, tokens_ref, gain_ref, w_query_ref,
                sems):
     me = lax.axis_index("blk")
     half = w_query_hbm.shape[0] // 2
@@ -128,7 +128,6 @@
         [
             (lengths_hbm, lengths_ref),
             (order_hbm, order_ref),
-            (variate_hbm, variate_ref),
             (tokens_hbm, tokens_ref),
             (gain_hbm, gain_ref),
             (w_query_hbm.at[:half, :], w_query_ref.at[:half, :]),
@@ -136,22 +135,21 @@
         ],
         sems,
     )
-    for copy in copies[:3]:
+    for copy in copies[:2]:
         copy.wait()
     order = order_ref[...]
-    starts, ends, variates = place_rows(lengths_ref[...], order, variate_ref[...])
+    starts, ends = place_rows(lengths_ref[...], order)
     home_of, local = split_by(order, z.req)
     places_ref[0:1, :] = starts
     places_ref[1:2, :] = ends
-    places_ref[2:3, :] = variates
-    places_ref[3:4, :] = home_of.astype(F32)
+    places_ref[2:3, :] = order.astype(F32)
     other, turn = split_by(iota((z.slots, 1), 0), z.slot)
     mine = choose(z, starts, ends, home_of, turn, me, other)
     row = jnp.sum(jnp.where(mine, local.astype(F32) + 1.0, F32(0)), axis=1, keepdims=True) - 1.0
     row = row.astype(I32)
     home_ref[...] = jnp.broadcast_to(row, home_ref.shape)
 
-    for copy in copies[3:]:
+    for copy in copies[2:]:
         copy.wait()
     normed = normalize(tokens_ref[...].astype(F32), gain_ref[...]).astype(BF16)
     rows_ref[:, z.width :] = normed
@@ -160,16 +158,18 @@
     deal(z, dot(one_hot(row == iota((z.slots, z.req), 1)), query), ask_ref)
 
 
-def slot_facts(z, places_ref, live, key_variate, bias, facts_ref):
+def slot_facts(z, places_ref, variate, live, key_variate, bias, facts_ref):
     me = lax.axis_index("blk")
-    starts, ends, variates = places_ref[0:1, :], places_ref[1:2, :], places_ref[2:3, :]
-    home_of = places_ref[3:4, :].astype(I32)
+    starts, ends, order = places_ref[0:1, :], places_ref[1:2, :], places_ref[2:3, :]
+    home_of, _ = split_by(order.astype(I32), z.req)
     other, turn = split_by(iota((z.slots, 1), 0), z.slot)
     theirs = choose(z, starts, ends, home_of, turn, other, jnp.full((1, 1), me, I32))
     low = (me * z.pool).astype(F32)
     begin = jnp.sum(jnp.where(theirs, starts - low, F32(0)), axis=1, keepdims=True)
     finish = jnp.sum(jnp.where(theirs, ends - low, F32(0)), axis=1, keepdims=True)
-    kind = jnp.sum(jnp.where(theirs, variates, F32(0)), axis=1, keepdims=True)
+    request = jnp.sum(jnp.where(theirs, order, F32(0)), axis=1, keepdims=True).astype(I32)
+    its = request == iota((z.slots, z.total), 1)
+    kind = jnp.sum(jnp.where(its, variate.astype(F32), F32(0)), axis=1, keepdims=True)
     blocks = live.shape[1]
     spread = one_hot(
         split_by(iota((blocks, z.pool), 1), z.block)[0] == iota((blocks, z.pool), 0)
@@ -201,16 +201,16 @@
 
 
 def first_load_kernel(z, count, places_ref, rows_ref, *refs):
-    far, small = refs[:count], refs[count : count + 5]
-    near, (facts_ref, own_ref) = refs[count + 5 : 2 * count + 5], refs[2 * count + 5 : 2 * count + 7]
-    held, sems = refs[2 * count + 7 : -1], refs[-1]
+    far, small = refs[:count], refs[count : count + 6]
+    near, (facts_ref, own_ref) = refs[count + 6 : 2 * count + 6], refs[2 * count + 6 : 2 * count + 8]
+    held, sems = refs[2 * count + 8 : -1], refs[-1]
     copies = fetch([*zip(small, held), *zip(far, near)], sems)
-    live_ref, key_variate_ref, bias_ref, w_key_ref, w_value_ref = held
-    for copy in copies[:3]:
+    variate_ref, live_ref, key_variate_ref, bias_ref, w_key_ref, w_value_ref = held
+    for copy in copies[:4]:
         copy.wait()
-    slot_facts(z, places_ref, live_ref[...], key_variate_ref[...], bias_ref[...], facts_ref)
+    slot_facts(z, places_ref, variate_ref[...], live_ref[...], key_variate_ref[...], bias_ref[...], facts_ref)
     normed = rows_ref[:, z.width :]
-    copies[3].wait()
+    copies[4].wait()
     key_new = dot(normed, w_key_ref[...]).astype(BF16)
     product = rows_ref[:, : z.width].astype(F32) * key_new.astype(F32)
     columns = []
@@ -221,9 +221,9 @@
         raw = jnp.sum(jnp.where(lane_head == inner, part, F32(0)), axis=1, keepdims=True)
         columns.append(raw * F32(z.dim**-0.5) + bias_ref[0:1, h : h + 1])
     own_ref[:, z.width :] = pieces(z, columns).astype(BF16)
-    copies[4].wait()
+    copies[5].wait()
     own_ref[:, : z.width] = dot(normed, w_value_ref[...]).astype(BF16)
-    for copy in copies[5:]:
+    for copy in copies[6:]:
         copy.wait()
 
 
@@ -427,7 +427,7 @@
     d_model = tokens.shape[1]
     width_local = d_model // head_count
     row = lambda x: x.reshape(1, -1)
-    operands = (row(lengths), row(order), row(query_variate), tokens, row(norm_gain), w_query)
+    operands = (row(lengths), row(order), tokens, row(norm_gain), w_query)
     ask, rows, places, home = call(
         functools.partial(ask_kernel, z),
         [
@@ -443,7 +443,7 @@
         name="ask",
     )
     asked = lax.all_to_all(ask, "blk", 0, 0)
-    early, small = (keys, values), (row(live_blocks), row(key_variate), bias, w_key, w_value)
+    early, small = (keys, values), (row(query_variate), row(live_blocks), row(key_variate), bias, w_key, w_value)
     keys_near, values_near, facts, own = call(
         functools.partial(first_load_kernel, z, len(early)),
         [pltpu.VMEM(x.shape, x.dtype) for x in early]

time: 38.9 us -> 38.9 us (level)
  transfers between devices with their start and end apart: 5 -> 5, of which waited for: 3 -> 3; matrix products, arithmetic and copies ran while one was open for 0% -> 0% of each run, Pallas kernels for 17% -> 18%
where the time goes in v7:
time: 38.9 us; the launch traced here: 38.6 us
  Pallas kernels  14.3 us (37%)
  starting transfers between devices  11.9 us (31%)
  waiting for transfers between devices  11.6 us (30%)
  other arithmetic  0.62 us (2%)
    pallas_call x6, Pallas kernels, call(): pl.pallas_call(kernel, out_shape=out, in_specs=specs, out_specs=[VMEM] *...  14.3 us
    all_to_all x1, starting transfers between devices, body(): asked = lax.all_to_all(ask, 'blk', 0, 0)  8.33 us
    all_to_all x1, waiting for transfers between devices, body(): returned = lax.all_to_all(back, ('blk', 'head'), 0, 0)  6.55 us
    all_to_all x1, waiting for transfers between devices, body(): asked = lax.all_to_all(ask, 'blk', 0, 0)  4.64 us
    all_to_all x1, starting transfers between devices, body(): returned = lax.all_to_all(back, ('blk', 'head'), 0, 0)  2.58 us
    ppermute x3, starting transfers between devices, from_core(): return lax.ppermute(x, 'head', [((i + shift) % n, i) for i in range(n)])  1.01 us
  transfers between devices with their start and end apart: 5, of which 3 were waited for; matrix products, arithmetic and copies ran while one was open for 0% of the time, Pallas kernels for 18%

profile of v7, /device:TPU:0, one launch (start us, length us, event | category | flops | bytes accessed | tf_op | source)
XLA Modules:
  0.0 38.6 jit_solution(9584225947789935710)
XLA Ops:
  0.0 2.5 %ask.1 = (bf16[16,4,512]{2,1,0:T(4,128)(2,1)}, bf16[32,1536]{1,0:T(8,128)(2,1)S(1)}, f32[8,512]{1,0:T(8,128)S(1)}, s32[64,128]{1,0:T(8,128)S(1)}) custom-call(s32[1,512]{1,0:T(1,128)} %bitcast.10, s32[1,512]{1,0:T(1,128)} %bitcast.11, bf16[32,1024]{1,0:T(8,128)(2,1)} %refs_0_.3, f32[1,1024]{1,0:T(1,128)} %bitcast.7, bf16[1024,512]{1,0:T(8,128)(2,1)} %w_query_hbm.1), custom_call_target="tpu_custom_call" | custom-call | flops 10000000000 | bytes 10000000 | tf_op jit(solution)/shard_map/ask/pallas_call | solution.py:375
  2.5 8.3 %all-to-all-start = ((bf16[16,4,512]{2,1,0:T(4,128)(2,1)}), bf16[16,4,512]{2,1,0:T(4,128)(2,1)S(1)}, u32[]{:S(2)}, u32[]{:S(2)}) async-start(bf16[16,4,512]{2,1,0:T(4,128)(2,1)} %get-tuple-element.23), calls=%async_computation | async-start | bytes 131072 | tf_op jit(solution)/shard_map/all_to_all | solution.py:445
  10.8 2.3 %first_load.1 = (bf16[1024,512]{1,0:T(8,128)(2,1)S(1)}, bf16[1024,512]{1,0:T(8,128)(2,1)S(1)}, f32[136,1024]{1,0:T(8,128)S(1)}, bf16[32,640]{1,0:T(8,128)(2,1)S(1)}) custom-call(f32[8,512]{1,0:T(8,128)S(1)} %get-tuple-element.24.places_ref, bf16[32,1536]{1,0:T(8,128)(2,1)S(1)} %get-tuple-element.25.rows_ref, bf16[1024,512]{1,0:T(8,128)(2,1)} %refs_0_.2, ...), custom_call_target="tpu_custom_call" | custom-call | flops 10000000000 | bytes 10000000 | tf_op jit(solution)/shard_map/first_load/pallas_call | solution.py:375
  13.1 0.1 collective-permute-start
  13.2 0.5 %collective-permute-start.1 = (bf16[512,1024]{1,0:T(8,128)(2,1)}, bf16[512,1024]{1,0:T(8,128)(2,1)}, u32[]{:S(2)}, u32[]{:S(2)}) collective-permute-start(bf16[512,1024]{1,0:T(8,128)(2,1)} %refs_2_.1), channel_id=1, source_target_pairs={{1,0},{0,1},{3,2},{2,3},{5,4},{4,5},{7,6},{6,7},{9,8},{8,9},{11,10... | collective-permute-start | bytes 3145736 | tf_op jit(solution)/shard_map/ppermute | solution.py:389
  13.7 4.6 %all-to-all-done.ask_ref = bf16[16,4,512]{2,1,0:T(4,128)(2,1)S(1)} async-done(((bf16[16,4,512]{2,1,0:T(4,128)(2,1)}), bf16[16,4,512]{2,1,0:T(4,128)(2,1)S(1)}, u32[]{:S(2)}, u32[]{:S(2)}) %all-to-all-start) | async-done | bytes 65568 | tf_op jit(solution)/shard_map/all_to_all | solution.py:445
  18.3 2.0 %attend.1 = (bf16[32,4,640]{2,1,0:T(4,128)(2,1)}, f32[8,128]{1,0:T(8,128)S(1)}) custom-call(bf16[16,4,512]{2,1,0:T(4,128)(2,1)S(1)} %all-to-all-done.ask_ref, bf16[1024,512]{1,0:T(8,128)(2,1)S(1)} %get-tuple-element.26.keys_ref, bf16[1024,512]{1,0:T(8,128)(2,1)S(1)} %get-tuple-element.27.values_ref, f32[136,1024]{1,0:T(8,128)S(1)} %get-tuple-element.28.facts_ref), custom_call_target="tpu_custom_call" | custom-call | flops 10000000000 | bytes 10000000 | tf_op jit(solution)/shard_map/attend/pallas_call | solution.py:375
  20.3 2.6 %all-to-all-start.1 = ((bf16[32,4,640]{2,1,0:T(4,128)(2,1)}), bf16[32,4,640]{2,1,0:T(4,128)(2,1)S(1)}, u32[]{:S(2)}, u32[]{:S(2)}) async-start(bf16[32,4,640]{2,1,0:T(4,128)(2,1)} %get-tuple-element.29), calls=%async_computation.1 | async-start | bytes 327680 | tf_op jit(solution)/shard_map/all_to_all | solution.py:467
  22.9 2.0 %second_load.1 = (bf16[32,1024]{1,0:T(8,128)(2,1)S(1)}, f32[1,1024]{1,0:T(1,128)S(1)}, bf16[512,1024]{1,0:T(8,128)(2,1)S(1)}, bf16[2048,512]{1,0:T(8,128)(2,1)S(1)}) custom-call(f32[8,128]{1,0:T(8,128)S(1)} %get-tuple-element.31.after_ref, bf16[32,1024]{1,0:T(8,128)(2,1)} %refs_0_.3, f32[1,1024]{1,0:T(1,128)} %bitcast.9, bf16[512,1024]{1,0:T(8,128)(2,1)} %refs_2_.1, ...), custom_call_target="tpu_custom_call" | custom-call | flops 10000000000 | bytes 10000000 | tf_op jit(solution)/shard_map/second_load/pallas_call | solution.py:375
  24.9 0.0 collective-permute-done.refs_5_
  24.9 6.6 %all-to-all-done.1.refs_0_ = bf16[32,4,640]{2,1,0:T(4,128)(2,1)S(1)} async-done(((bf16[32,4,640]{2,1,0:T(4,128)(2,1)}), bf16[32,4,640]{2,1,0:T(4,128)(2,1)S(1)}, u32[]{:S(2)}, u32[]{:S(2)}) %all-to-all-start.1) | async-done | bytes 163872 | tf_op jit(solution)/shard_map/all_to_all | solution.py:467
  31.5 0.0 collective-permute-done.1.refs_7_
  31.5 5.1 %tail.1 = (bf16[32,2048]{1,0:T(8,128)(2,1)S(1)}, f32[32,512]{1,0:T(8,128)S(1)}, bf16[32,512]{1,0:T(8,128)(2,1)S(1)}) custom-call(bf16[32,4,640]{2,1,0:T(4,128)(2,1)S(1)} %all-to-all-done.1.refs_0_, s32[64,128]{1,0:T(8,128)S(1)} %get-tuple-element.30.refs_1_, bf16[32,1024]{1,0:T(8,128)(2,1)S(1)} %get-tuple-element.32.refs_2_, ...), custom_call_target="tpu_custom_call" | custom-call | flops 10000000000 | bytes 10000000 | tf_op jit(solution)/shard_map/tail/pallas_call | solution.py:375
  36.6 0.4 %collective-permute-start.2 = (bf16[32,512]{1,0:T(8,128)(2,1)S(1)}, bf16[32,512]{1,0:T(8,128)(2,1)S(1)}, u32[]{:S(2)}, u32[]{:S(2)}) collective-permute-start(bf16[32,512]{1,0:T(8,128)(2,1)S(1)} %get-tuple-element.40), channel_id=1, source_target_pairs={{1,0},{0,1},{3,2},{2,3},{5,4},{4,5},{7,6},{6,7},{9,8},{8,9},{11,10... | collective-permute-start | bytes 98312 | tf_op jit(solution)/shard_map/ppermute | solution.py:389
  37.1 0.5 %finish.1 = f32[32,512]{1,0:T(8,128)S(1)} custom-call(bf16[32,2048]{1,0:T(8,128)(2,1)S(1)} %get-tuple-element.37.hidden_ref, f32[32,512]{1,0:T(8,128)S(1)} %get-tuple-element.38.mixed_ref, bf16[2048,512]{1,0:T(8,128)(2,1)S(1)} %get-tuple-element.39.down_ref), custom_call_target="tpu_custom_call" | custom-call | flops 10000000000 | bytes 10000000 | tf_op jit(solution)/shard_map/finish/pallas_call | solution.py:375
  37.5 0.4 %collective-permute-done.2 = bf16[32,512]{1,0:T(8,128)(2,1)S(1)} collective-permute-done((bf16[32,512]{1,0:T(8,128)(2,1)S(1)}, bf16[32,512]{1,0:T(8,128)(2,1)S(1)}, u32[]{:S(2)}, u32[]{:S(2)}) %collective-permute-start.2) | collective-permute-done | bytes 32800 | tf_op jit(solution)/shard_map/ppermute | solution.py:389
  37.9 0.6 %add_convert_fusion = bf16[32,512]{1,0:T(8,128)(2,1)} fusion(f32[32,512]{1,0:T(8,128)S(1)} %finish.1, bf16[32,512]{1,0:T(8,128)(2,1)S(1)} %collective-permute-done.2), kind=kLoop, calls=%fused_computation | loop fusion | flops 49152 | bytes 131072 | tf_op jit(solution)/shard_map/convert_element_type | solution.py:505
Async XLA Ops:
  2.5 15.9 %all-to-all-start = ((bf16[16,4,512]{2,1,0:T(4,128)(2,1)}), bf16[16,4,512]{2,1,0:T(4,128)(2,1)S(1)}, u32[]{:S(2)}, u32[]{:S(2)}) async-start(bf16[16,4,512]{2,1,0:T(4,128)(2,1)} %get-tuple-element.23), calls=%async_computation | async-start | bytes 131072 | tf_op jit(solution)/shard_map/all_to_all | solution.py:445
  13.1 11.8 %collective-permute-start = (bf16[32,640]{1,0:T(8,128)(2,1)S(1)}, bf16[32,640]{1,0:T(8,128)(2,1)S(1)}, u32[]{:S(2)}, u32[]{:S(2)}) collective-permute-start(bf16[32,640]{1,0:T(8,128)(2,1)S(1)} %get-tuple-element.34.refs_4_), channel_id=1, source_target_pairs={{1,0},{0,1},{3,2},{2,3},{5,4},{4,5},{7,6},{6,7},{9,8},{8,9},{11,10... | collective-permute-start | bytes 122888 | tf_op jit(solution)/shard_map/ppermute | solution.py:389
  13.2 18.3 %collective-permute-start.1 = (bf16[512,1024]{1,0:T(8,128)(2,1)}, bf16[512,1024]{1,0:T(8,128)(2,1)}, u32[]{:S(2)}, u32[]{:S(2)}) collective-permute-start(bf16[512,1024]{1,0:T(8,128)(2,1)} %refs_2_.1), channel_id=1, source_target_pairs={{1,0},{0,1},{3,2},{2,3},{5,4},{4,5},{7,6},{6,7},{9,8},{8,9},{11,10... | collective-permute-start | bytes 3145736 | tf_op jit(solution)/shard_map/ppermute | solution.py:389
  20.3 11.2 %all-to-all-start.1 = ((bf16[32,4,640]{2,1,0:T(4,128)(2,1)}), bf16[32,4,640]{2,1,0:T(4,128)(2,1)S(1)}, u32[]{:S(2)}, u32[]{:S(2)}) async-start(bf16[32,4,640]{2,1,0:T(4,128)(2,1)} %get-tuple-element.29), calls=%async_computation.1 | async-start | bytes 327680 | tf_op jit(solution)/shard_map/all_to_all | solution.py:467
  36.6 1.3 %collective-permute-start.2 = (bf16[32,512]{1,0:T(8,128)(2,1)S(1)}, bf16[32,512]{1,0:T(8,128)(2,1)S(1)}, u32[]{:S(2)}, u32[]{:S(2)}) collective-permute-start(bf16[32,512]{1,0:T(8,128)(2,1)S(1)} %get-tuple-element.40), channel_id=1, source_target_pairs={{1,0},{0,1},{3,2},{2,3},{5,4},{4,5},{7,6},{6,7},{9,8},{8,9},{11,10... | collective-permute-start | bytes 98312 | tf_op jit(solution)/shard_map/ppermute | solution.py:389

commit v8 on v6

--- a/solution.py
+++ b/solution.py
@@ -294,7 +294,7 @@
     level = jnp.where(match, level, F32(FLOOR))
     top = jnp.max(level, axis=0, keepdims=True)
     weight = jnp.where(match, jnp.exp(level - top), F32(0))
-    weight = weight / jnp.sum(weight, axis=0, keepdims=True)
+    weight = weight * (1.0 / jnp.sum(weight, axis=0, keepdims=True))
     high = weight.astype(BF16)
     held = jnp.concatenate([stacked[:, : z.width], value], axis=0)
     dims = (((0,), (0,)), ((), ()))

time: 38.9 us -> 38.9 us (level)
  no operation moved by 1% of the time
where the time goes in v8:
time: 38.9 us; the launch traced here: 38.6 us
  Pallas kernels  14.3 us (37%)
  starting transfers between devices  11.9 us (31%)
  waiting for transfers between devices  11.6 us (30%)
  other arithmetic  0.62 us (2%)
    pallas_call x6, Pallas kernels, call(): pl.pallas_call(kernel, out_shape=out, in_specs=specs, out_specs=[VMEM] *...  14.3 us
    all_to_all x1, starting transfers between devices, body(): asked = lax.all_to_all(ask, 'blk', 0, 0)  8.33 us
    all_to_all x1, waiting for transfers between devices, body(): returned = lax.all_to_all(back, ('blk', 'head'), 0, 0)  6.55 us
    all_to_all x1, waiting for transfers between devices, body(): asked = lax.all_to_all(ask, 'blk', 0, 0)  4.66 us
    all_to_all x1, starting transfers between devices, body(): returned = lax.all_to_all(back, ('blk', 'head'), 0, 0)  2.58 us
    ppermute x3, starting transfers between devices, from_core(): return lax.ppermute(x, 'head', [((i + shift) % n, i) for i in range(n)])  1.02 us
  transfers between devices with their start and end apart: 5, of which 3 were waited for; matrix products, arithmetic and copies ran while one was open for 0% of the time, Pallas kernels for 17%

profile of v8, /device:TPU:0, one launch (start us, length us, event | category | flops | bytes accessed | tf_op | source)
XLA Modules:
  0.0 38.6 jit_solution(7300843115485301134)
XLA Ops:
  0.0 2.5 %ask.1 = (bf16[16,4,512]{2,1,0:T(4,128)(2,1)}, bf16[32,1536]{1,0:T(8,128)(2,1)S(1)}, f32[8,512]{1,0:T(8,128)S(1)}, s32[64,128]{1,0:T(8,128)S(1)}) custom-call(s32[1,512]{1,0:T(1,128)} %bitcast.10, s32[1,512]{1,0:T(1,128)} %bitcast.11, s32[1,512]{1,0:T(1,128)} %bitcast.12, bf16[32,1024]{1,0:T(8,128)(2,1)} %refs_0_.3, f32[1,1024]{1,0:T(1,128)} %bitcast.7, ...), custom_call_target="tpu_custom_call" | custom-call | flops 10000000000 | bytes 10000000 | tf_op jit(solution)/shard_map/ask/pallas_call | solution.py:375
  2.5 8.3 %all-to-all-start = ((bf16[16,4,512]{2,1,0:T(4,128)(2,1)}), bf16[16,4,512]{2,1,0:T(4,128)(2,1)S(1)}, u32[]{:S(2)}, u32[]{:S(2)}) async-start(bf16[16,4,512]{2,1,0:T(4,128)(2,1)} %get-tuple-element.23), calls=%async_computation | async-start | bytes 131072 | tf_op jit(solution)/shard_map/all_to_all | solution.py:445
  10.8 2.3 %first_load.1 = (bf16[1024,512]{1,0:T(8,128)(2,1)S(1)}, bf16[1024,512]{1,0:T(8,128)(2,1)S(1)}, f32[136,1024]{1,0:T(8,128)S(1)}, bf16[32,640]{1,0:T(8,128)(2,1)S(1)}) custom-call(f32[8,512]{1,0:T(8,128)S(1)} %get-tuple-element.24.places_ref, bf16[32,1536]{1,0:T(8,128)(2,1)S(1)} %get-tuple-element.25.rows_ref, bf16[1024,512]{1,0:T(8,128)(2,1)} %refs_0_.2, ...), custom_call_target="tpu_custom_call" | custom-call | flops 10000000000 | bytes 10000000 | tf_op jit(solution)/shard_map/first_load/pallas_call | solution.py:375
  13.1 0.1 collective-permute-start
  13.2 0.5 %collective-permute-start.1 = (bf16[512,1024]{1,0:T(8,128)(2,1)}, bf16[512,1024]{1,0:T(8,128)(2,1)}, u32[]{:S(2)}, u32[]{:S(2)}) collective-permute-start(bf16[512,1024]{1,0:T(8,128)(2,1)} %refs_2_.1), channel_id=1, source_target_pairs={{1,0},{0,1},{3,2},{2,3},{5,4},{4,5},{7,6},{6,7},{9,8},{8,9},{11,10... | collective-permute-start | bytes 3145736 | tf_op jit(solution)/shard_map/ppermute | solution.py:389
  13.7 4.7 %all-to-all-done.ask_ref = bf16[16,4,512]{2,1,0:T(4,128)(2,1)S(1)} async-done(((bf16[16,4,512]{2,1,0:T(4,128)(2,1)}), bf16[16,4,512]{2,1,0:T(4,128)(2,1)S(1)}, u32[]{:S(2)}, u32[]{:S(2)}) %all-to-all-start) | async-done | bytes 65568 | tf_op jit(solution)/shard_map/all_to_all | solution.py:445
  18.4 2.0 %attend.1 = (bf16[32,4,640]{2,1,0:T(4,128)(2,1)}, f32[8,128]{1,0:T(8,128)S(1)}) custom-call(bf16[16,4,512]{2,1,0:T(4,128)(2,1)S(1)} %all-to-all-done.ask_ref, bf16[1024,512]{1,0:T(8,128)(2,1)S(1)} %get-tuple-element.26.keys_ref, bf16[1024,512]{1,0:T(8,128)(2,1)S(1)} %get-tuple-element.27.values_ref, f32[136,1024]{1,0:T(8,128)S(1)} %get-tuple-element.28.facts_ref), custom_call_target="tpu_custom_call" | custom-call | flops 10000000000 | bytes 10000000 | tf_op jit(solution)/shard_map/attend/pallas_call | solution.py:375
  20.4 2.6 %all-to-all-start.1 = ((bf16[32,4,640]{2,1,0:T(4,128)(2,1)}), bf16[32,4,640]{2,1,0:T(4,128)(2,1)S(1)}, u32[]{:S(2)}, u32[]{:S(2)}) async-start(bf16[32,4,640]{2,1,0:T(4,128)(2,1)} %get-tuple-element.29), calls=%async_computation.1 | async-start | bytes 327680 | tf_op jit(solution)/shard_map/all_to_all | solution.py:467
  23.0 2.0 %second_load.1 = (bf16[32,1024]{1,0:T(8,128)(2,1)S(1)}, f32[1,1024]{1,0:T(1,128)S(1)}, bf16[512,1024]{1,0:T(8,128)(2,1)S(1)}, bf16[2048,512]{1,0:T(8,128)(2,1)S(1)}) custom-call(f32[8,128]{1,0:T(8,128)S(1)} %get-tuple-element.31.after_ref, bf16[32,1024]{1,0:T(8,128)(2,1)} %refs_0_.3, f32[1,1024]{1,0:T(1,128)} %bitcast.9, bf16[512,1024]{1,0:T(8,128)(2,1)} %refs_2_.1, ...), custom_call_target="tpu_custom_call" | custom-call | flops 10000000000 | bytes 10000000 | tf_op jit(solution)/shard_map/second_load/pallas_call | solution.py:375
  25.0 0.0 collective-permute-done.refs_5_
  25.0 6.6 %all-to-all-done.1.refs_0_ = bf16[32,4,640]{2,1,0:T(4,128)(2,1)S(1)} async-done(((bf16[32,4,640]{2,1,0:T(4,128)(2,1)}), bf16[32,4,640]{2,1,0:T(4,128)(2,1)S(1)}, u32[]{:S(2)}, u32[]{:S(2)}) %all-to-all-start.1) | async-done | bytes 163872 | tf_op jit(solution)/shard_map/all_to_all | solution.py:467
  31.5 0.0 collective-permute-done.1.refs_7_
  31.5 5.1 %tail.1 = (bf16[32,2048]{1,0:T(8,128)(2,1)S(1)}, f32[32,512]{1,0:T(8,128)S(1)}, bf16[32,512]{1,0:T(8,128)(2,1)S(1)}) custom-call(bf16[32,4,640]{2,1,0:T(4,128)(2,1)S(1)} %all-to-all-done.1.refs_0_, s32[64,128]{1,0:T(8,128)S(1)} %get-tuple-element.30.refs_1_, bf16[32,1024]{1,0:T(8,128)(2,1)S(1)} %get-tuple-element.32.refs_2_, ...), custom_call_target="tpu_custom_call" | custom-call | flops 10000000000 | bytes 10000000 | tf_op jit(solution)/shard_map/tail/pallas_call | solution.py:375
  36.6 0.4 %collective-permute-start.2 = (bf16[32,512]{1,0:T(8,128)(2,1)S(1)}, bf16[32,512]{1,0:T(8,128)(2,1)S(1)}, u32[]{:S(2)}, u32[]{:S(2)}) collective-permute-start(bf16[32,512]{1,0:T(8,128)(2,1)S(1)} %get-tuple-element.40), channel_id=1, source_target_pairs={{1,0},{0,1},{3,2},{2,3},{5,4},{4,5},{7,6},{6,7},{9,8},{8,9},{11,10... | collective-permute-start | bytes 98312 | tf_op jit(solution)/shard_map/ppermute | solution.py:389
  37.1 0.5 %finish.1 = f32[32,512]{1,0:T(8,128)S(1)} custom-call(bf16[32,2048]{1,0:T(8,128)(2,1)S(1)} %get-tuple-element.37.hidden_ref, f32[32,512]{1,0:T(8,128)S(1)} %get-tuple-element.38.mixed_ref, bf16[2048,512]{1,0:T(8,128)(2,1)S(1)} %get-tuple-element.39.down_ref), custom_call_target="tpu_custom_call" | custom-call | flops 10000000000 | bytes 10000000 | tf_op jit(solution)/shard_map/finish/pallas_call | solution.py:375
  37.5 0.4 %collective-permute-done.2 = bf16[32,512]{1,0:T(8,128)(2,1)S(1)} collective-permute-done((bf16[32,512]{1,0:T(8,128)(2,1)S(1)}, bf16[32,512]{1,0:T(8,128)(2,1)S(1)}, u32[]{:S(2)}, u32[]{:S(2)}) %collective-permute-start.2) | collective-permute-done | bytes 32800 | tf_op jit(solution)/shard_map/ppermute | solution.py:389
  38.0 0.6 %add_convert_fusion = bf16[32,512]{1,0:T(8,128)(2,1)} fusion(f32[32,512]{1,0:T(8,128)S(1)} %finish.1, bf16[32,512]{1,0:T(8,128)(2,1)S(1)} %collective-permute-done.2), kind=kLoop, calls=%fused_computation | loop fusion | flops 49152 | bytes 131072 | tf_op jit(solution)/shard_map/convert_element_type | solution.py:505
Async XLA Ops:
  2.5 15.9 %all-to-all-start = ((bf16[16,4,512]{2,1,0:T(4,128)(2,1)}), bf16[16,4,512]{2,1,0:T(4,128)(2,1)S(1)}, u32[]{:S(2)}, u32[]{:S(2)}) async-start(bf16[16,4,512]{2,1,0:T(4,128)(2,1)} %get-tuple-element.23), calls=%async_computation | async-start | bytes 131072 | tf_op jit(solution)/shard_map/all_to_all | solution.py:445
  13.1 11.8 %collective-permute-start = (bf16[32,640]{1,0:T(8,128)(2,1)S(1)}, bf16[32,640]{1,0:T(8,128)(2,1)S(1)}, u32[]{:S(2)}, u32[]{:S(2)}) collective-permute-start(bf16[32,640]{1,0:T(8,128)(2,1)S(1)} %get-tuple-element.34.refs_4_), channel_id=1, source_target_pairs={{1,0},{0,1},{3,2},{2,3},{5,4},{4,5},{7,6},{6,7},{9,8},{8,9},{11,10... | collective-permute-start | bytes 122888 | tf_op jit(solution)/shard_map/ppermute | solution.py:389
  13.2 18.3 %collective-permute-start.1 = (bf16[512,1024]{1,0:T(8,128)(2,1)}, bf16[512,1024]{1,0:T(8,128)(2,1)}, u32[]{:S(2)}, u32[]{:S(2)}) collective-permute-start(bf16[512,1024]{1,0:T(8,128)(2,1)} %refs_2_.1), channel_id=1, source_target_pairs={{1,0},{0,1},{3,2},{2,3},{5,4},{4,5},{7,6},{6,7},{9,8},{8,9},{11,10... | collective-permute-start | bytes 3145736 | tf_op jit(solution)/shard_map/ppermute | solution.py:389
  20.4 11.2 %all-to-all-start.1 = ((bf16[32,4,640]{2,1,0:T(4,128)(2,1)}), bf16[32,4,640]{2,1,0:T(4,128)(2,1)S(1)}, u32[]{:S(2)}, u32[]{:S(2)}) async-start(bf16[32,4,640]{2,1,0:T(4,128)(2,1)} %get-tuple-element.29), calls=%async_computation.1 | async-start | bytes 327680 | tf_op jit(solution)/shard_map/all_to_all | solution.py:467
  36.6 1.3 %collective-permute-start.2 = (bf16[32,512]{1,0:T(8,128)(2,1)S(1)}, bf16[32,512]{1,0:T(8,128)(2,1)S(1)}, u32[]{:S(2)}, u32[]{:S(2)}) collective-permute-start(bf16[32,512]{1,0:T(8,128)(2,1)S(1)} %get-tuple-element.40), channel_id=1, source_target_pairs={{1,0},{0,1},{3,2},{2,3},{5,4},{4,5},{7,6},{6,7},{9,8},{8,9},{11,10... | collective-permute-start | bytes 98312 | tf_op jit(solution)/shard_map/ppermute | solution.py:389
